TPU v7x, 256 devices: a whole 4x4x8 slice. The times are simulated.
256 devices in a mesh: dp: 16 (over z, core), proto: 16 (over y, x).
Axes of the slice: x: 4, y: 4, z: 8, core: 2. Of those that a mesh axis runs over, the one named last changes fastest.
Arguments:
- teacher_emb: bfloat16 [8192, 256], P('dp'), may hold values from -0.8 to 0.8
- student_emb: bfloat16 [8192, 256], P('dp'), may hold values from -0.9 to 0.9
- prototypes: bfloat16 [65536, 256], P('proto'), may hold values from -0.36 to 0.36
Outputs:
- grad_student: float32 [8192, 256], P('dp')
- grad_protos: float32 [16, 4096, 256], P('proto', 'dp')
- mean_loss: float32 [], replicated
All inputs are finite; a program needn't handle non-finite values.
Results may differ from a plain program's by a relative error of at most 0.006.
Values may be sent and summed in bfloat16 or wider, within the bound.
No kernel may reach another device: no remote copies, remote signals or barrier semaphores. Data moves between devices by JAX's collectives and lax.ppermute only.
A program may use at most 64 MiB of HBM per device.

v0:
```python
import jax
import jax.numpy as jnp
from jax import lax
from jax.sharding import PartitionSpec as P

ITERS = 3


def unit_rows(matrix):
    values = matrix.astype(jnp.float32)
    row_norms = jnp.sqrt(jnp.sum(values * values, axis=-1, keepdims=True) + 1e-06)
    return (values / row_norms, row_norms)


def column_step(targets):
    col_sums = lax.psum(jnp.sum(targets, axis=0), "dp")
    return targets / col_sums[None, :]


def per_device(teacher_emb, student_emb, prototypes):
    t_unit, t_norms = unit_rows(teacher_emb)
    s_unit, s_norms = unit_rows(student_emb)
    w_unit, w_norms = unit_rows(prototypes)
    t_half = t_unit.astype(jnp.bfloat16)
    s_half = s_unit.astype(jnp.bfloat16)
    w_half = w_unit.astype(jnp.bfloat16)
    contract_last = (((1,), (1,)), ((), ()))
    targets = jnp.exp(
        lax.dot_general(t_half, w_half, contract_last, preferred_element_type=jnp.float32) / 0.07
    )
    logits = (
        lax.dot_general(s_half, w_half, contract_last, preferred_element_type=jnp.float32) / 0.1
    )
    student_exp = jnp.exp(logits)
    student_local = jnp.sum(student_exp, axis=1)
    targets = column_step(targets)
    row_totals = lax.psum(jnp.sum(targets, axis=1), "proto")
    totals = lax.psum(student_local, "proto")
    targets = targets / row_totals[:, None]
    for sweep_index in range(ITERS - 1):
        targets = column_step(targets)
        row_totals = lax.psum(jnp.sum(targets, axis=1), "proto")
        targets = targets / row_totals[:, None]
    lse_rows = jnp.log(totals)
    probs = student_exp / totals[:, None]
    loss_local = jnp.sum(targets * (logits - lse_rows[:, None]))
    grad_scores = ((probs - targets) / 0.1).astype(jnp.bfloat16)
    grad_local = jnp.dot(grad_scores, w_half, preferred_element_type=jnp.float32)
    grad_s, loss_rows = lax.psum((grad_local, loss_local), "proto")
    loss_sum = lax.psum(loss_rows, "dp")
    crop_count = student_emb.shape[0] * lax.axis_size("dp")
    mean_loss = -loss_sum / crop_count
    grad_student = (grad_s - s_unit * jnp.sum(s_unit * grad_s, axis=-1, keepdims=True)) / s_norms
    owned_rows = prototypes.shape[0] // lax.axis_size("dp")
    contract_first = (((0,), (0,)), ((), ()))
    proto_part = lax.psum_scatter(
        lax.dot_general(grad_scores, s_half, contract_first, preferred_element_type=jnp.float32),
        "dp",
        scatter_dimension=0,
        tiled=True,
    )
    first_owned = lax.axis_index("dp") * owned_rows
    w_mine = lax.dynamic_slice_in_dim(w_unit, first_owned, owned_rows, 0)
    n_mine = lax.dynamic_slice_in_dim(w_norms, first_owned, owned_rows, 0)
    grad_protos = (
        proto_part - w_mine * jnp.sum(w_mine * proto_part, axis=-1, keepdims=True)
    ) / n_mine
    return (grad_student, grad_protos[None], mean_loss)


def solution(mesh):
    in_specs = (P("dp", None), P("dp", None), P("proto", None))
    out_specs = (P("dp", None), P("proto", "dp", None), P())
    return jax.shard_map(
        per_device, mesh=mesh, in_specs=in_specs, out_specs=out_specs, check_vma=False
    )
```

profile of v0, /device:TPU:1, one launch (start us, length us, event | category | flops | bytes accessed | tf_op | source)
XLA Modules:
  0.0 418.3 jit_solution(10437933296797755693)
XLA Ops:
  8.0 0.0 all-reduce.3.cloned.1.call-start
  8.0 2.2 fusion.11
  10.3 1.1 fusion.13
  11.4 6.9 %fusion.25 = (f32[4096]{0:T(1024)S(1)}, f32[512,4096]{1,0:T(8,128)}) fusion(f32[4096]{0:T(1024)S(1)} %add_sqrt_fusion, bf16[4096,256]{1,0:T(8,128)(2,1)} %param.5, bf16[512,256]{1,0:T(8,128)(2,1)} %param.3, f32[512]{0:T(512)S(1)} %add_sqrt_fusion.1), kind=kOutput, calls=%fused_computation.44 | convolution fusion | flops 1081470976 | bytes 10782720 | tf_op jit(solution)/shard_map/dot_general | solution.py:29
  18.3 48.9 %psum.71 = f32[4096]{0:T(1024)S(1)} all-reduce(f32[4096]{0:T(1024)S(1)} %get-tuple-element.9), channel_id=1, replica_groups=mesh['dp'=16,'proto'=16] {'dp'}, use_global_device_ids=true, to_apply=%region_6.0 | all-reduce | flops 4096 | bytes 32768 | tf_op jit(solution)/shard_map/psum | solution.py:16
  67.2 4.0 divide_reduce_fusion
  71.2 33.5 %psum.72 = f32[512]{0:T(512)S(1)} all-reduce(f32[512]{0:T(512)S(1)} %divide_reduce_fusion), channel_id=1, replica_groups=mesh['dp'=16,'proto'=16] {'proto'}, use_global_device_ids=true, to_apply=%region_8.0 | all-reduce | flops 512 | bytes 4096 | tf_op jit(solution)/shard_map/psum | solution.py:37
  104.7 4.7 %fusion.7 = f32[4096]{0:T(1024)S(1)} fusion(f32[512,4096]{1,0:T(8,128)} %get-tuple-element.10, f32[512]{0:T(512)S(1)} %psum.72, f32[4096]{0:T(1024)S(1)} %psum.71), kind=kLoop, calls=%fused_computation.13 | loop fusion | flops 6287360 | bytes 8423424 | tf_op jit(solution)/shard_map/reduce_sum | solution.py:16
  109.5 52.8 %psum.73 = f32[4096]{0:T(1024)S(1)} all-reduce(f32[4096]{0:T(1024)S(1)} %fusion.7), channel_id=1, replica_groups=mesh['dp'=16,'proto'=16] {'dp'}, use_global_device_ids=true, to_apply=%region_10.0 | all-reduce | flops 4096 | bytes 32768 | tf_op jit(solution)/shard_map/psum | solution.py:16
  162.3 4.3 %fusion.8 = f32[512]{0:T(512)S(1)} fusion(f32[512,4096]{1,0:T(8,128)} %get-tuple-element.10, f32[4096]{0:T(1024)S(1)} %psum.73, f32[512]{0:T(512)S(1)} %psum.72, f32[4096]{0:T(1024)S(1)} %psum.71), kind=kLoop, calls=%fused_computation.14 | loop fusion | flops 8388096 | bytes 8425472 | tf_op jit(solution)/shard_map/reduce_sum | solution.py:42
  166.6 28.5 %psum.74 = f32[512]{0:T(512)S(1)} all-reduce(f32[512]{0:T(512)S(1)} %fusion.8), channel_id=1, replica_groups=mesh['dp'=16,'proto'=16] {'proto'}, use_global_device_ids=true, to_apply=%region_12.0 | all-reduce | flops 512 | bytes 4096 | tf_op jit(solution)/shard_map/psum | solution.py:42
  195.1 0.0 copy-start.2
  195.1 0.0 copy-start
  195.1 4.6 %fusion.9 = f32[4096]{0:T(1024)S(1)} fusion(f32[512,4096]{1,0:T(8,128)} %get-tuple-element.10, f32[512]{0:T(512)S(1)} %psum.74, f32[4096]{0:T(1024)S(1)} %psum.73, f32[512]{0:T(512)S(1)} %psum.72, f32[4096]{0:T(1024)S(1)} %psum.71), kind=kLoop, calls=%fused_computation.15 | loop fusion | flops 10481664 | bytes 8441856 | tf_op jit(solution)/shard_map/reduce_sum | solution.py:16
  199.7 52.7 %psum.75 = f32[4096]{0:T(1024)S(1)} all-reduce(f32[4096]{0:T(1024)S(1)} %fusion.9), channel_id=1, replica_groups=mesh['dp'=16,'proto'=16] {'dp'}, use_global_device_ids=true, to_apply=%region_14.0 | all-reduce | flops 4096 | bytes 32768 | tf_op jit(solution)/shard_map/psum | solution.py:16
  252.3 4.6 %fusion.10 = f32[512]{0:T(512)S(1)} fusion(f32[512,4096]{1,0:T(8,128)} %get-tuple-element.10, f32[4096]{0:T(1024)S(1)} %psum.75, f32[512]{0:T(512)S(1)} %psum.74, f32[4096]{0:T(1024)S(1)} %psum.73, f32[512]{0:T(512)S(1)} %psum.72, f32[4096]{0:T(1024)S(1)} %psum.71), kind=kLoop, calls=%fused_computation.16 | loop fusion | flops 12582400 | bytes 8443904 | tf_op jit(solution)/shard_map/reduce_sum | solution.py:42
  257.0 0.0 copy-done.2
  257.0 0.1 fusion.12
  257.1 0.0 copy-done
  257.1 4.4 %exponential_reduce_fusion = (f32[512]{0:T(512)S(1)}, f32[512,4096]{1,0:T(8,128)}) fusion(f32[4096]{0:T(1024)S(1)} %add_sqrt_fusion, bf16[4096,256]{1,0:T(8,128)(2,1)S(1)} %copy-done, f32[512]{0:T(512)S(1)} %add_sqrt_fusion.2, bf16[512,256]{1,0:T(8,128)(2,1)S(1)} %copy-done.2), kind=kOutput, calls=%fused_computation.17 | convolution fusion | flops 1081474560 | bytes 10768384 | tf_op jit(solution)/shard_map/dot_general | solution.py:32
  261.5 30.6 %all-reduce = (f32[512]{0:T(512)S(1)}, f32[512]{0:T(512)S(1)}) all-reduce(f32[512]{0:T(512)S(1)} %get-tuple-element.7, f32[512]{0:T(512)S(1)} %fusion.10), channel_id=1, replica_groups=mesh['dp'=16,'proto'=16] {'proto'}, use_global_device_ids=true, to_apply=%region_3.0 | all-reduce | flops 1024 | bytes 8192 | tf_op jit(solution)/shard_map/psum | solution.py:38
  292.1 10.1 %multiply_reduce_fusion = (f32[]{:T(128)}, bf16[512,4096]{1,0:T(8,128)(2,1)S(1)}) fusion(f32[512,4096]{1,0:T(8,128)} %get-tuple-element.8, f32[512]{0:T(512)S(1)} %log.3, f32[512,4096]{1,0:T(8,128)} %get-tuple-element.10, f32[512]{0:T(512)S(1)} %get-tuple-element.4, f32[4096]{0:T(1024)S(1)} %psum.75, f32[512]{0:T(512)S(1)} %psum.74, f32[4096]{0:T(1024)S(1)} %psum.73, ...), kind=kLoop, calls=%fused_computation.9 | loop fusion | flops 29360128 | bytes 21030916 | tf_op jit(solution)/shard_map/reduce_sum | solution.py:46
  302.2 0.0 copy-start.1
  302.2 2.0 copy-done.1
  304.1 2.2 fusion.21
  306.4 0.0 all-reduce.3.cloned.1.call-update
  306.4 0.0 reduce-scatter.2.cloned.1.call-start
  306.4 5.5 %fusion.17 = f32[4096,256]{1,0:T(8,128)} fusion(bf16[512,4096]{1,0:T(8,128)(2,1)} %copy-done.1, bf16[512,256]{1,0:T(8,128)(2,1)S(1)} %copy-done.2, f32[512]{0:T(512)S(1)} %add_sqrt_fusion.2), kind=kOutput, calls=%fused_computation.33 | convolution fusion | flops 1074135040 | bytes 8652800 | tf_op jit(solution)/shard_map/dot_general | solution.py:57
  311.9 0.0 reduce-scatter.2.cloned.1.call-update
  312.0 29.3 %psum.78 = f32[]{:T(128)} all-reduce(f32[]{:T(128)} %get-tuple-element.5), channel_id=1, replica_groups=mesh['dp'=16,'proto'=16] {'proto'}, use_global_device_ids=true, to_apply=%region_22.0 | all-reduce | flops 1 | bytes 8 | tf_op jit(solution)/shard_map/psum | solution.py:49
  341.3 41.4 %psum.79 = f32[]{:T(128)} all-reduce(f32[]{:T(128)} %psum.78), channel_id=1, replica_groups=mesh['dp'=16,'proto'=16] {'dp'}, use_global_device_ids=true, to_apply=%region_23.0 | all-reduce | flops 1 | bytes 8 | tf_op jit(solution)/shard_map/psum | solution.py:50
  382.7 0.1 dynamic-slice.3
  383.4 2.3 convert_divide_fusion
  385.8 17.6 %all-reduce.3.cloned.1.call-done = f32[512,256]{1,0:T(8,128)} async-done(((f32[512,256]{1,0:T(8,128)}), f32[512,256]{1,0:T(8,128)}) %all-reduce.3.cloned.1.call-update) | async-done | bytes 524304 | tf_op jit(solution)/shard_map/psum | solution.py:49
  403.4 1.3 multiply_reduce_fusion.1
  404.6 2.0 subtract_divide_fusion
  406.7 0.0 reduce-scatter.2.cloned.1.call-done
  406.7 1.1 multiply_reduce_fusion.2
  407.8 1.9 divide_bitcast_fusion
  (4 shorter events, 0.0 us)
Async XLA Ops:
  8.0 395.4 %all-reduce.3.cloned.1.call-start = ((), (), s32[]{:S(2)}) async-start(), calls=%async_computation.1 | async-start | bytes 1048576 | tf_op jit(solution)/shard_map/psum | solution.py:49
  195.1 61.9 %copy-start.2 = (bf16[512,256]{1,0:T(8,128)(2,1)S(1)}, bf16[512,256]{1,0:T(8,128)(2,1)}, u32[]{:S(2)}) copy-start(bf16[512,256]{1,0:T(8,128)(2,1)} %param.4) | copy-start | bytes 786436
  195.1 62.0 %copy-start = (bf16[4096,256]{1,0:T(8,128)(2,1)S(1)}, bf16[4096,256]{1,0:T(8,128)(2,1)}, u32[]{:S(2)}) copy-start(bf16[4096,256]{1,0:T(8,128)(2,1)} %param.5) | copy-start | bytes 6291460
  302.2 2.0 copy-start.1
  306.4 100.3 %reduce-scatter.2.cloned.1.call-start = ((), (), s32[]{:S(2)}) async-start(), calls=%async_computation.2 | async-start | bytes 4456448 | tf_op jit(solution)/shard_map/reduce_scatter | solution.py:56
Sparse Core Ops, SparseCore 0:
  306.5 96.8 all-reduce.2
Sparse Core Ops, SparseCore 1:
  312.0 63.0 reduce-scatter.1
where the time goes:
time: 419 us; the launch traced here: 418 us
  blocking collectives  318 us (76%)
  other arithmetic  44.5 us (11%)
  matrix products  19 us (5%)
  waiting for transfers between devices  17.6 us (4%)
  between operations  17.3 us (4%)
    psum x3, blocking collectives, column_step(): col_sums = lax.psum(jnp.sum(targets, axis=0), 'dp')  154 us
    psum x2, blocking collectives, per_device(): row_totals = lax.psum(jnp.sum(targets, axis=1), 'proto')  62 us
    psum x1, blocking collectives, per_device(): loss_sum = lax.psum(loss_rows, 'dp')  41.4 us
    psum x1, blocking collectives, per_device(): totals = lax.psum(student_local, 'proto')  30.6 us
    psum x1, blocking collectives, per_device(): grad_s, loss_rows = lax.psum((grad_local, loss_local), 'proto')  29.3 us
    psum x1, waiting for transfers between devices, per_device(): grad_s, loss_rows = lax.psum((grad_local, loss_local), 'proto')  17.6 us
    reduce_sum x3, other arithmetic, per_device(): row_totals = lax.psum(jnp.sum(targets, axis=1), 'proto')  12.9 us
    reduce_sum x1, other arithmetic, per_device(): loss_local = jnp.sum(targets * (logits - lse_rows[:, None]))  10.1 us
  transfers between devices with their start and end apart: 2, of which 1 were waited for; matrix products, arithmetic and copies ran while one was open for 3% of the time, Pallas kernels for 0%

commit v1 on v0

v1 whole, which is shorter than its diff:
```python
import jax
import jax.numpy as jnp
import numpy as np
from jax import lax
from jax.sharding import Mesh, PartitionSpec as P

ITERS = 3
CROPS = ("z", "core")
PROTOS = ("y", "x")


def unit_rows(matrix):
    values = matrix.astype(jnp.float32)
    row_norms = jnp.sqrt(jnp.sum(values * values, axis=-1, keepdims=True) + 1e-06)
    return (values / row_norms, row_norms)


def spread(part, axes, count):
    return lax.all_to_all(jnp.broadcast_to(part[None], (count,) + part.shape), axes, 0, 0)


def per_device(teacher_emb, student_emb, prototypes):
    crops = teacher_emb.shape[0]
    protos = prototypes.shape[0]
    n_dp = lax.axis_size("z") * lax.axis_size("core")
    n_proto = lax.axis_size("y") * lax.axis_size("x")

    def sum_dp(vec):
        return jnp.sum(spread(vec.reshape(-1, 128), CROPS, n_dp), axis=0).reshape(-1)

    def sum_proto(vec):
        return jnp.sum(spread(vec.reshape(-1, 128), PROTOS, n_proto), axis=0).reshape(-1)

    t_unit, t_norms = unit_rows(teacher_emb)
    s_unit, s_norms = unit_rows(student_emb)
    w_unit, w_norms = unit_rows(prototypes)
    t_half = t_unit.astype(jnp.bfloat16)
    s_half = s_unit.astype(jnp.bfloat16)
    w_half = w_unit.astype(jnp.bfloat16)
    contract_last = (((1,), (1,)), ((), ()))
    expo = jnp.exp(
        lax.dot_general(t_half, w_half, contract_last, preferred_element_type=jnp.float32) / 0.07
    )
    logits = (
        lax.dot_general(s_half, w_half, contract_last, preferred_element_type=jnp.float32) / 0.1
    )
    student_exp = jnp.exp(logits)
    col = 1.0 / sum_dp(jnp.sum(expo, axis=0))
    sums = sum_proto(
        jnp.concatenate([jnp.sum(expo * col[None, :], axis=1), jnp.sum(student_exp, axis=1)])
    )
    row, totals = 1.0 / sums[:crops], sums[crops:]
    col = 1.0 / sum_dp(jnp.sum(expo * row[:, None], axis=0))
    row = 1.0 / sum_proto(jnp.sum(expo * col[None, :], axis=1))
    col = 1.0 / sum_dp(jnp.sum(expo * row[:, None], axis=0))
    weighted = expo * col[None, :]
    sums = sum_proto(
        jnp.concatenate([jnp.sum(weighted, axis=1), jnp.sum(weighted * logits, axis=1)])
    )
    row = 1.0 / sums[:crops]
    loss_block = jnp.sum(row * sums[crops:] - jnp.log(totals))
    grad_scores = ((student_exp / totals[:, None] - weighted * row[:, None]) / 0.1).astype(
        jnp.bfloat16
    )
    contract_first = (((0,), (0,)), ((), ()))
    grad_w = lax.dot_general(
        grad_scores, s_half, contract_first, preferred_element_type=jnp.float32
    )
    owned = protos // n_dp
    grad_w = grad_w.astype(jnp.bfloat16).reshape(n_dp // 2, 2, owned, -1)
    core = lax.axis_index("core")
    keep = jnp.where(core == 0, grad_w[:, 0], grad_w[:, 1])
    give = jnp.where(core == 0, grad_w[:, 1], grad_w[:, 0])
    got = lax.ppermute(give, "core", [(0, 1), (1, 0)])
    half = (keep.astype(jnp.float32) + got.astype(jnp.float32)).astype(jnp.bfloat16)
    parts = lax.all_to_all(half, "z", 0, 0)
    proto_part = jnp.sum(parts.astype(jnp.float32), axis=0)

    grad_local = jnp.dot(grad_scores, w_half, preferred_element_type=jnp.float32)
    piece = lax.all_to_all(
        grad_local.astype(jnp.bfloat16).reshape(n_proto, crops // n_proto, -1), PROTOS, 0, 0
    )
    piece = jnp.sum(piece.astype(jnp.float32), axis=0)
    grad_s = spread(piece.astype(jnp.bfloat16), PROTOS, n_proto).reshape(crops, -1)
    grad_s = grad_s.astype(jnp.float32)
    loss_sum = jnp.sum(spread(jnp.broadcast_to(loss_block, (8, 128)), CROPS, n_dp)[:, 0, 0])
    mean_loss = -loss_sum / (crops * n_dp)
    grad_student = (grad_s - s_unit * jnp.sum(s_unit * grad_s, axis=-1, keepdims=True)) / s_norms
    first_owned = (lax.axis_index("z") * 2 + core) * owned
    w_mine = lax.dynamic_slice_in_dim(w_unit, first_owned, owned, 0)
    n_mine = lax.dynamic_slice_in_dim(w_norms, first_owned, owned, 0)
    grad_protos = (
        proto_part - w_mine * jnp.sum(w_mine * proto_part, axis=-1, keepdims=True)
    ) / n_mine
    return (grad_student, grad_protos[None], mean_loss)


def solution(mesh):
    fine = Mesh(np.asarray(mesh.devices).reshape(8, 2, 4, 4), ("z", "core", "y", "x"))
    in_specs = (P(CROPS, None), P(CROPS, None), P(PROTOS, None))
    out_specs = (P(CROPS, None), P(PROTOS, CROPS, None), P())
    return jax.shard_map(
        per_device, mesh=fine, in_specs=in_specs, out_specs=out_specs, check_vma=False
    )
```

time: 419 us -> 209 us (0.50)
  blocking collectives: 318 us -> 65.3 us
  waiting for transfers between devices: 17.6 us -> 47.3 us
  starting transfers between devices: 0.08 us -> 25.6 us
  between operations: 17.3 us -> 2.65 us
  matrix products: 19 us -> 14.2 us
  other arithmetic: 44.5 us -> 48.9 us
    psum x8 -> x0, blocking collectives: 318 us -> none  [the longest x3 154 us: column_step(): col_sums = lax.psum(jnp.sum(targets, axis=0), 'dp')]
    all_to_all x0 -> x5, blocking collectives: none -> 65.3 us  [the longest x4 54 us: spread(): lax.all_to_all(jnp.broadcast_to(part[None], (count,) + part.shape), axes,...]
    all_to_all x0 -> x5, waiting for transfers between devices: none -> 47.3 us  [the longest x4 27.1 us: spread(): lax.all_to_all(jnp.broadcast_to(part[None], (count,) + part.shape), axes,...]
    all_to_all x0 -> x5, starting transfers between devices: none -> 25.2 us  [the longest x4 21.7 us: spread(): lax.all_to_all(jnp.broadcast_to(part[None], (count,) + part.shape), axes,...]
    psum x1 -> x0, waiting for transfers between devices: 17.6 us -> none  [per_device(): grad_s, loss_rows = lax.psum((grad_local, loss_local), 'proto')]
    convert_element_type x0 -> x2, other arithmetic: none -> 10.5 us  [the longest x1 7.23 us: per_device(): ((student_exp / totals[:, None] - weighted * row[:, None]) / 0.1).astype(...]
    reduce_sum x6 -> x15, other arithmetic: 32.4 us -> 25.4 us  [the longest x2 9.1 us: per_device(): col = 1.0 / sum_dp(jnp.sum(expo * row[:, None], axis=0))]
  transfers between devices with their start and end apart: 2 -> 6, of which waited for: 1 -> 5; matrix products, arithmetic and copies ran while one was open for 3% -> 8% of each run, Pallas kernels for 0% -> 0%
where the time goes in v1:
time: 209 us; the launch traced here: 208 us
  blocking collectives  65.3 us (31%)
  other arithmetic  48.9 us (23%)
  waiting for transfers between devices  47.3 us (23%)
  starting transfers between devices  25.6 us (12%)
  matrix products  14.2 us (7%)
  local copies, waits for them, and re-layouts  4.23 us (2%)
  between operations  2.65 us (1%)
    all_to_all x4, blocking collectives, spread(): lax.all_to_all(jnp.broadcast_to(part[None], (count,) + part.shape), axes,...  54 us
    all_to_all x4, waiting for transfers between devices, spread(): lax.all_to_all(jnp.broadcast_to(part[None], (count,) + part.shape), axes,...  27.1 us
    all_to_all x4, starting transfers between devices, spread(): lax.all_to_all(jnp.broadcast_to(part[None], (count,) + part.shape), axes,...  21.7 us
    all_to_all x1, waiting for transfers between devices, per_device(): parts = lax.all_to_all(half, 'z', 0, 0)  20.2 us
    all_to_all x1, blocking collectives, per_device(): lax.all_to_all(grad_local.astype(jnp.bfloat16).reshape(n_proto, crops //...  11.3 us
    reduce_sum x2, other arithmetic, per_device(): col = 1.0 / sum_dp(jnp.sum(expo * row[:, None], axis=0))  9.1 us
    convert_element_type x1, other arithmetic, per_device(): ((student_exp / totals[:, None] - weighted * row[:, None]) / 0.1).astype(...  7.23 us
    dot_general x1, matrix products, per_device(): lax.dot_general(t_half, w_half, contract_last, preferred_element_type=jnp...  7.1 us
  transfers between devices with their start and end apart: 6, of which 5 were waited for; matrix products, arithmetic and copies ran while one was open for 8% of the time, Pallas kernels for 0%

profile of v1, /device:TPU:1, one launch (start us, length us, event | category | flops | bytes accessed | tf_op | source)
XLA Modules:
  0.0 208.2 jit_solution(18313599093973379732)
XLA Ops:
  0.6 2.2 %fusion = f32[4096]{0:T(1024)S(1)} fusion(bf16[4096,256]{1,0:T(8,128)(2,1)} %param.5), kind=kLoop, calls=%fused_computation.12 | loop fusion | flops 3141632 | bytes 2113536 | tf_op jit(solution)/shard_map/reduce_sum | solution.py:14
  2.9 1.1 fusion.5
  4.0 0.0 copy-start.2
  4.0 0.0 copy-start
  4.0 7.1 %fusion.18 = (f32[4096]{0:T(1024)S(1)}, f32[512,4096]{1,0:T(8,128)}) fusion(f32[4096]{0:T(1024)S(1)} %add_sqrt_fusion, bf16[4096,256]{1,0:T(8,128)(2,1)} %param.5, bf16[512,256]{1,0:T(8,128)(2,1)} %param.3, f32[512]{0:T(512)S(1)} %add_sqrt_fusion.1), kind=kOutput, calls=%fused_computation.56 | convolution fusion | flops 1081470976 | bytes 10782720 | tf_op jit(solution)/shard_map/dot_general | solution.py:42
  11.1 0.7 broadcast_in_dim.25
  11.8 10.0 %all-to-all-start = ((f32[16,32,128]{2,1,0:T(8,128)}), f32[16,32,128]{2,1,0:T(8,128)S(1)}, u32[]{:S(2)}, u32[]{:S(2)}) async-start(f32[16,32,128]{2,1,0:T(8,128)} %broadcast_in_dim.25), calls=%async_computation | async-start | bytes 524288 | tf_op jit(solution)/shard_map/all_to_all | solution.py:19
  21.8 0.1 fusion.4
  22.0 4.3 %exponential_reduce_fusion = (f32[512]{0:T(512)S(1)}, f32[512,4096]{1,0:T(8,128)}) fusion(f32[4096]{0:T(1024)S(1)} %add_sqrt_fusion, bf16[4096,256]{1,0:T(8,128)(2,1)S(1)} %copy-done, f32[512]{0:T(512)S(1)} %add_sqrt_fusion.2, bf16[512,256]{1,0:T(8,128)(2,1)S(1)} %copy-done.2), kind=kOutput, calls=%fused_computation.7 | convolution fusion | flops 1081474560 | bytes 10768384 | tf_op jit(solution)/shard_map/dot_general | solution.py:45
  26.3 7.3 %all-to-all-done = f32[16,32,128]{2,1,0:T(8,128)S(1)} async-done(((f32[16,32,128]{2,1,0:T(8,128)}), f32[16,32,128]{2,1,0:T(8,128)S(1)}, u32[]{:S(2)}, u32[]{:S(2)}) %all-to-all-start) | async-done | bytes 262176 | tf_op jit(solution)/shard_map/all_to_all | solution.py:19
  33.6 4.0 %multiply_reduce_fusion.4 = f32[512]{0:T(512)S(1)} fusion(f32[512,4096]{1,0:T(8,128)} %get-tuple-element.11, f32[4096]{0:T(1024)S(1)} %divide_bitcast_fusion.3), kind=kLoop, calls=%fused_computation.5 | loop fusion | flops 4193792 | bytes 8407040 | tf_op jit(solution)/shard_map/reduce_sum | solution.py:50
  37.6 13.4 %all_to_all.50 = f32[16,8,128]{2,1,0:T(8,128)S(1)} all-to-all(f32[16,8,128]{2,1,0:T(8,128)S(1)} %broadcast_in_dim.26), channel_id=1, replica_groups=mesh['z'=8,'core'=2,'y'=4,'x'=4] {'y','x'}, dimensions={0} | all-to-all | bytes 131072 | tf_op jit(solution)/shard_map/all_to_all | solution.py:19
  51.0 4.6 %multiply_reduce_fusion.3 = f32[4096]{0:T(1024)S(1)} fusion(f32[512,4096]{1,0:T(8,128)} %get-tuple-element.11, f32[512]{0:T(512)S(1)} %divide_bitcast_fusion.5), kind=kLoop, calls=%fused_computation.4 | loop fusion | flops 4190208 | bytes 8407040 | tf_op jit(solution)/shard_map/reduce_sum | solution.py:53
  55.6 15.5 %all_to_all.51 = f32[16,32,128]{2,1,0:T(8,128)S(1)} all-to-all(f32[16,32,128]{2,1,0:T(8,128)S(1)} %broadcast_in_dim.28), channel_id=1, replica_groups=mesh['z'=8,'core'=2,'y'=4,'x'=4] {'z','core'}, dimensions={0} | all-to-all | bytes 524288 | tf_op jit(solution)/shard_map/all_to_all | solution.py:19
  71.2 4.0 %multiply_reduce_fusion.2 = f32[512]{0:T(512)S(1)} fusion(f32[512,4096]{1,0:T(8,128)} %get-tuple-element.11, f32[4096]{0:T(1024)S(1)} %divide_bitcast_fusion.2), kind=kLoop, calls=%fused_computation.3 | loop fusion | flops 4193792 | bytes 8407040 | tf_op jit(solution)/shard_map/reduce_sum | solution.py:54
  75.2 9.5 %all_to_all.52 = f32[16,4,128]{2,1,0:T(4,128)S(1)} all-to-all(f32[16,4,128]{2,1,0:T(4,128)S(1)} %broadcast_in_dim.30), channel_id=1, replica_groups=mesh['z'=8,'core'=2,'y'=4,'x'=4] {'y','x'}, dimensions={0} | all-to-all | bytes 65536 | tf_op jit(solution)/shard_map/all_to_all | solution.py:19
  84.7 4.6 %multiply_reduce_fusion.1 = f32[4096]{0:T(1024)S(1)} fusion(f32[512,4096]{1,0:T(8,128)} %get-tuple-element.11, f32[512]{0:T(512)S(1)} %divide_bitcast_fusion.4), kind=kLoop, calls=%fused_computation.2 | loop fusion | flops 4190208 | bytes 8407040 | tf_op jit(solution)/shard_map/reduce_sum | solution.py:55
  89.3 15.7 %all_to_all.53 = f32[16,32,128]{2,1,0:T(8,128)S(1)} all-to-all(f32[16,32,128]{2,1,0:T(8,128)S(1)} %broadcast_in_dim.32), channel_id=1, replica_groups=mesh['z'=8,'core'=2,'y'=4,'x'=4] {'z','core'}, dimensions={0} | all-to-all | bytes 524288 | tf_op jit(solution)/shard_map/all_to_all | solution.py:19
  105.0 6.7 %multiply_reduce_fusion.5 = (f32[512]{0:T(512)S(1)}, f32[512]{0:T(512)S(1)}) fusion(f32[512,4096]{1,0:T(8,128)} %get-tuple-element.11, f32[4096]{0:T(1024)S(1)} %divide_bitcast_fusion.1, f32[512,4096]{1,0:T(8,128)} %get-tuple-element.9), kind=kLoop, calls=%fused_computation.8 | loop fusion | flops 10484736 | bytes 16797696 | tf_op jit(solution)/shard_map/reduce_sum | solution.py:58
  111.7 0.6 broadcast_in_dim.33
  112.4 3.7 %all-to-all-start.5 = ((f32[16,8,128]{2,1,0:T(8,128)}), f32[16,8,128]{2,1,0:T(8,128)S(1)}, u32[]{:S(2)}, u32[]{:S(2)}) async-start(f32[16,8,128]{2,1,0:T(8,128)} %broadcast_in_dim.33), calls=%async_computation.5 | async-start | bytes 131072 | tf_op jit(solution)/shard_map/all_to_all | solution.py:19
  116.1 6.9 %all-to-all-done.5 = f32[16,8,128]{2,1,0:T(8,128)S(1)} async-done(((f32[16,8,128]{2,1,0:T(8,128)}), f32[16,8,128]{2,1,0:T(8,128)S(1)}, u32[]{:S(2)}, u32[]{:S(2)}) %all-to-all-start.5) | async-done | bytes 65568 | tf_op jit(solution)/shard_map/all_to_all | solution.py:19
  123.0 0.6 subtract_reduce_fusion
  123.6 7.2 %multiply_convert_fusion = bf16[512,4096]{1,0:T(8,128)(2,1)S(1)} fusion(f32[512,4096]{1,0:T(8,128)} %get-tuple-element.11, f32[512,4096]{1,0:T(8,128)} %get-tuple-element.9, f32[512]{0:T(512)S(1)} %get-tuple-element.7, f32[4096]{0:T(1024)S(1)} %divide_bitcast_fusion.1, f32[512]{0:T(512)S(1)} %get-tuple-element.6), kind=kLoop, calls=%fused_computation | loop fusion | flops 14680064 | bytes 20992000 | tf_op jit(solution)/shard_map/convert_element_type | solution.py:62
  130.8 1.4 convolution_convert_fusion
  132.2 1.2 fusion.2
  133.4 0.4 collective-permute-start
  133.8 1.4 convolution_convert_fusion.1
  135.3 11.3 %all_to_all.54 = bf16[16,32,256]{2,1,0:T(8,128)(2,1)S(1)} all-to-all(bf16[16,32,256]{2,1,0:T(8,128)(2,1)S(1)} %bitcast.55), channel_id=1, replica_groups=mesh['z'=8,'core'=2,'y'=4,'x'=4] {'y','x'}, dimensions={0} | all-to-all | bytes 524288 | tf_op jit(solution)/shard_map/all_to_all | solution.py:80
  146.6 1.3 broadcast_in_dim_broadcast_in_dim_broadcast_in_dim.3
  147.9 4.5 %all-to-all-start.9 = ((f32[16,8,128]{2,1,0:T(8,128)}), f32[16,8,128]{2,1,0:T(8,128)S(1)}, u32[]{:S(2)}, u32[]{:S(2)}) async-start(f32[16,8,128]{2,1,0:T(8,128)} %broadcast_in_dim_broadcast_in_dim_broadcast_in_dim.3), calls=%async_computation.9 | async-start | bytes 131072 | tf_op jit(solution)/shard_map/all_to_all | solution.py:19
  152.4 7.8 %all-to-all-done.9 = f32[16,8,128]{2,1,0:T(8,128)S(1)} async-done(((f32[16,8,128]{2,1,0:T(8,128)}), f32[16,8,128]{2,1,0:T(8,128)S(1)}, u32[]{:S(2)}, u32[]{:S(2)}) %all-to-all-start.9) | async-done | bytes 65568 | tf_op jit(solution)/shard_map/all_to_all | solution.py:19
  160.2 0.7 broadcast_in_dim.34
  160.9 3.5 %all-to-all-start.7 = ((bf16[16,32,256]{2,1,0:T(8,128)(2,1)}), bf16[16,32,256]{2,1,0:T(8,128)(2,1)S(1)}, u32[]{:S(2)}, u32[]{:S(2)}) async-start(bf16[16,32,256]{2,1,0:T(8,128)(2,1)} %broadcast_in_dim.34), calls=%async_computation.7 | async-start | bytes 524288 | tf_op jit(solution)/shard_map/all_to_all | solution.py:19
  164.4 0.0 collective-permute-done
  164.4 3.2 %fusion.1 = bf16[8,256,256]{2,1,0:T(8,128)(2,1)} fusion(bf16[8,256,256]{2,1,0:T(8,128)(2,1)} %collective-permute-done, pred[]{:T(512)S(6)} %eq.4, bf16[8,2,256,256]{3,2,1,0:T(8,128)(2,1)} %bitcast.54), kind=kLoop, calls=%fused_computation.14 | loop fusion | flops 2621440 | bytes 4194305 | tf_op jit(solution)/shard_map/convert_element_type | solution.py:75
  167.7 5.2 %all-to-all-done.7 = bf16[16,32,256]{2,1,0:T(8,128)(2,1)S(1)} async-done(((bf16[16,32,256]{2,1,0:T(8,128)(2,1)}), bf16[16,32,256]{2,1,0:T(8,128)(2,1)S(1)}, u32[]{:S(2)}, u32[]{:S(2)}) %all-to-all-start.7) | async-done | bytes 262176 | tf_op jit(solution)/shard_map/all_to_all | solution.py:19
  172.9 0.7 copy-done.3
  173.6 3.6 %all-to-all-start.8 = ((bf16[8,256,256]{2,1,0:T(8,128)(2,1)}), bf16[8,256,256]{2,1,0:T(8,128)(2,1)S(1)}, u32[]{:S(2)}, u32[]{:S(2)}) async-start(bf16[8,256,256]{2,1,0:T(8,128)(2,1)} %fusion.1), calls=%async_computation.8 | async-start | bytes 2097152 | tf_op jit(solution)/shard_map/all_to_all | solution.py:76
  177.2 0.1 dynamic-slice.3
  177.2 2.3 %convert_divide_fusion = f32[4096,256]{1,0:T(8,128)} fusion(bf16[4096,256]{1,0:T(8,128)(2,1)S(1)} %copy-done, f32[4096]{0:T(1024)S(1)} %add_sqrt_fusion), kind=kLoop, calls=%fused_computation.9 | loop fusion | flops 2097152 | bytes 6307840 | tf_op jit(solution)/shard_map/div | solution.py:15
  179.5 0.6 slice_reduce_fusion
  180.8 1.2 fusion.7
  182.0 2.0 fusion.8
  183.9 20.2 %all-to-all-done.8 = bf16[8,256,256]{2,1,0:T(8,128)(2,1)S(1)} async-done(((bf16[8,256,256]{2,1,0:T(8,128)(2,1)}), bf16[8,256,256]{2,1,0:T(8,128)(2,1)S(1)}, u32[]{:S(2)}, u32[]{:S(2)}) %all-to-all-start.8) | async-done | bytes 1048608 | tf_op jit(solution)/shard_map/all_to_all | solution.py:76
  204.1 0.1 convert_reduce_fusion
  204.2 1.1 multiply_reduce_fusion.6
  205.3 1.8 divide_bitcast_fusion
  (26 shorter events, 0.3 us)
Async XLA Ops:
  4.0 17.8 %copy-start.2 = (bf16[512,256]{1,0:T(8,128)(2,1)S(1)}, bf16[512,256]{1,0:T(8,128)(2,1)}, u32[]{:S(2)}) copy-start(bf16[512,256]{1,0:T(8,128)(2,1)} %param.4) | copy-start | bytes 786436
  4.0 18.0 %copy-start = (bf16[4096,256]{1,0:T(8,128)(2,1)S(1)}, bf16[4096,256]{1,0:T(8,128)(2,1)}, u32[]{:S(2)}) copy-start(bf16[4096,256]{1,0:T(8,128)(2,1)} %param.5) | copy-start | bytes 6291460
  11.8 21.7 %all-to-all-start = ((f32[16,32,128]{2,1,0:T(8,128)}), f32[16,32,128]{2,1,0:T(8,128)S(1)}, u32[]{:S(2)}, u32[]{:S(2)}) async-start(f32[16,32,128]{2,1,0:T(8,128)} %broadcast_in_dim.25), calls=%async_computation | async-start | bytes 524288 | tf_op jit(solution)/shard_map/all_to_all | solution.py:19
  112.4 10.6 %all-to-all-start.5 = ((f32[16,8,128]{2,1,0:T(8,128)}), f32[16,8,128]{2,1,0:T(8,128)S(1)}, u32[]{:S(2)}, u32[]{:S(2)}) async-start(f32[16,8,128]{2,1,0:T(8,128)} %broadcast_in_dim.33), calls=%async_computation.5 | async-start | bytes 131072 | tf_op jit(solution)/shard_map/all_to_all | solution.py:19
  132.2 3.1 %copy-start.1 = (bf16[4096,256]{1,0:T(8,128)(2,1)}, bf16[4096,256]{1,0:T(8,128)(2,1)S(1)}, u32[]{:S(2)}) copy-start(bf16[4096,256]{1,0:T(8,128)(2,1)S(1)} %convolution_convert_fusion) | copy-start | bytes 6291460
  133.4 31.0 %collective-permute-start = (bf16[8,256,256]{2,1,0:T(8,128)(2,1)}, bf16[8,256,256]{2,1,0:T(8,128)(2,1)}, u32[]{:S(2)}, u32[]{:S(2)}) collective-permute-start(bf16[8,256,256]{2,1,0:T(8,128)(2,1)} %fusion.2), channel_id=1, source_target_pairs={{0,16},{16,0},{1,17},{17,1},{2,18},{18,2},{3,19},{19,3},{4,20},{20... | collective-permute-start | bytes 3145736 | tf_op jit(solution)/shard_map/ppermute | solution.py:74
  147.9 12.3 %all-to-all-start.9 = ((f32[16,8,128]{2,1,0:T(8,128)}), f32[16,8,128]{2,1,0:T(8,128)S(1)}, u32[]{:S(2)}, u32[]{:S(2)}) async-start(f32[16,8,128]{2,1,0:T(8,128)} %broadcast_in_dim_broadcast_in_dim_broadcast_in_dim.3), calls=%async_computation.9 | async-start | bytes 131072 | tf_op jit(solution)/shard_map/all_to_all | solution.py:19
  160.9 12.0 %all-to-all-start.7 = ((bf16[16,32,256]{2,1,0:T(8,128)(2,1)}), bf16[16,32,256]{2,1,0:T(8,128)(2,1)S(1)}, u32[]{:S(2)}, u32[]{:S(2)}) async-start(bf16[16,32,256]{2,1,0:T(8,128)(2,1)} %broadcast_in_dim.34), calls=%async_computation.7 | async-start | bytes 524288 | tf_op jit(solution)/shard_map/all_to_all | solution.py:19
  172.9 0.7 copy-start.3
  173.6 30.5 %all-to-all-start.8 = ((bf16[8,256,256]{2,1,0:T(8,128)(2,1)}), bf16[8,256,256]{2,1,0:T(8,128)(2,1)S(1)}, u32[]{:S(2)}, u32[]{:S(2)}) async-start(bf16[8,256,256]{2,1,0:T(8,128)(2,1)} %fusion.1), calls=%async_computation.8 | async-start | bytes 2097152 | tf_op jit(solution)/shard_map/all_to_all | solution.py:76

commit v2 on v1

v2 whole, which is shorter than its diff:
```python
import functools

import jax
import jax.numpy as jnp
import numpy as np
from jax import lax
from jax.experimental import pallas as pl
from jax.experimental.pallas import tpu as pltpu
from jax.sharding import Mesh, PartitionSpec as P

CROPS = ("z", "core")
PROTOS = ("y", "x")
LOG2E = 1.4426950408889634
T_SCALE = LOG2E / 0.07
S_SCALE = LOG2E / 0.1
F32 = jnp.float32
BF16 = jnp.bfloat16
VMEM = pl.BlockSpec(memory_space=pltpu.VMEM)
SMEM = pl.BlockSpec(memory_space=pltpu.SMEM)
HBM = pl.BlockSpec(memory_space=pltpu.HBM)
LAST = (((1,), (1,)), ((), ()))
CHUNK = 512


def inverse_norms(values):
    return lax.rsqrt(jnp.sum(values * values, axis=-1, keepdims=True) + 1e-06)


def half_unit(block):
    values = block.astype(F32)
    return (values * inverse_norms(values)).astype(BF16)


def column(row):
    return jnp.broadcast_to(row, (128, 128)).T


def lay_down(block):
    return jnp.sum(block.T, axis=0, keepdims=True)


def twice(block):
    return jnp.concatenate([block, block], axis=1)


def call(kernel, out, operands, specs=None, outs=None, scratch=(), flops=0, limit=12):
    touched = sum(x.size * x.dtype.itemsize for x in operands)
    return pl.pallas_call(
        kernel,
        out_shape=out,
        in_specs=specs or [VMEM] * len(operands),
        out_specs=outs or jax.tree.map(lambda _: VMEM, out),
        scratch_shapes=list(scratch),
        cost_estimate=pl.CostEstimate(flops=flops, bytes_accessed=touched, transcendentals=0),
        compiler_params=pltpu.CompilerParams(vmem_limit_bytes=limit << 20),
    )(*operands)


def copies(pairs, sems):
    out = [pltpu.make_async_copy(a, b, sems.at[k]) for k, (a, b) in enumerate(pairs)]
    return out


def begin(pairs, sems):
    started = copies(pairs, sems)
    for c in started:
        c.start()
    return started


def lanes(k, size=CHUNK):
    return pl.ds(k * size, size)


def dp_place():
    return lax.axis_index("z") * lax.axis_size("core") + lax.axis_index("core")


def proto_place():
    return lax.axis_index("y") * lax.axis_size("x") + lax.axis_index("x")


def halves_kernel(t_hbm, s_hbm, th_ref, sh_ref, t_buf, s_buf, sems):
    one, two = begin([(t_hbm, t_buf), (s_hbm, s_buf)], sems)
    one.wait()
    th_ref[...] = half_unit(t_buf[...])
    two.wait()
    sh_ref[...] = half_unit(s_buf[...])


def teacher_kernel(n, th_ref, w_ref, e_ref, wh_ref, own_ref, msg_ref, sums):
    for j in range(w_ref.shape[0] // CHUNK):
        w_half = half_unit(w_ref[lanes(j), :])
        wh_ref[lanes(j), :] = w_half
        scores = lax.dot_general(th_ref[...], w_half, LAST, preferred_element_type=F32)
        expo = jnp.exp2(scores * T_SCALE)
        e_ref[:, lanes(j)] = expo.astype(BF16)
        part = jnp.sum(expo, axis=0, keepdims=True)
        for b in range(CHUNK // 128):
            at = j * (CHUNK // 128) + b
            sums[at : at + 1, :] = part[:, b * 128 : (b + 1) * 128]
    total = sums[...].astype(msg_ref.dtype)
    for k in range(n):
        msg_ref[k] = total
    owned = own_ref.shape[0]
    own_ref[...] = w_ref[pl.ds(pl.multiple_of(dp_place() * owned, owned), owned), :]


def student_kernel(sh_ref, wh_ref, tot_ref, p_ref, acc):
    for j in range(wh_ref.shape[0] // CHUNK):
        w_half = wh_ref[lanes(j), :]
        scores = lax.dot_general(sh_ref[...], w_half, LAST, preferred_element_type=F32)
        expo = jnp.exp2(scores * S_SCALE)
        part = sum(expo[:, b * 128 : (b + 1) * 128] for b in range(CHUNK // 128))
        prod = jnp.dot(expo.astype(BF16), w_half, preferred_element_type=F32)
        if j == 0:
            acc[...] = part
            p_ref[...] = prod
        else:
            acc[...] += part
            p_ref[...] += prod
    for i in range(4):
        tot_ref[i : i + 1, :] = lay_down(acc[lanes(i, 128), :])


def first_row_kernel(n, parts_ref, e_ref, tot_ref, p_ref, msg_ref, c_ref):
    size = CHUNK // n
    tails = [jnp.concatenate([row, tot_ref[i : i + 1, :]], axis=1)
             for i, row in enumerate(row_sums(parts_ref, e_ref, c_ref))]
    tail = jnp.concatenate(tails + [jnp.zeros((4, 256), F32)], axis=0)
    for k in range(n):
        msg_ref[k, 0:size, :] = p_ref[lanes(k, size), :]
        msg_ref[k, size : size + 8, :] = tail


def row_sums(parts_ref, e_ref, c_ref):
    c_ref[...] = 1.0 / jnp.sum(parts_ref[:, 0:32, :].astype(F32), axis=0)
    out = []
    for i in range(4):
        acc = jnp.zeros((128, 128), F32)
        for b in range(32):
            acc += e_ref[lanes(i, 128), b * 128 : (b + 1) * 128].astype(F32) * c_ref[b : b + 1, :]
        out.append(lay_down(acc))
    return out


def row_kernel(n, parts_ref, e_ref, msg_ref, c_ref):
    whole = jnp.concatenate(row_sums(parts_ref, e_ref, c_ref), axis=0)
    for k in range(n):
        msg_ref[k] = whole


def column_sums(scale, e_ref, row_col, out):
    for i in range(4):
        row_col[lanes(i, 128), :] = column(scale[i : i + 1])
    for b in range(32):
        acc = jnp.zeros((8, 128), F32)
        for i in range(4):
            rows = lanes(i, 128)
            prod = e_ref[rows, b * 128 : (b + 1) * 128].astype(F32) * row_col[rows, :]
            acc += jnp.sum(prod.reshape(16, 8, 128), axis=0)
        out[b : b + 1, :] = jnp.sum(acc, axis=0, keepdims=True)


def first_column_kernel(n, parts_ref, e_ref, msg_ref, tot_ref, p_ref, row_col, out):
    size = p_ref.shape[0]
    total = jnp.sum(parts_ref[...], axis=0)
    p_ref[...] = total[0:size]
    tot = total[size : size + 4, 128:256]
    tot_ref[...] = tot
    column_sums(1.0 / total[size : size + 4, 0:128], e_ref, row_col, out)
    whole = out[...].astype(BF16)
    high = tot.astype(BF16)
    low = (tot - high.astype(F32)).astype(BF16)
    tail = jnp.concatenate([high.astype(F32), low.astype(F32), jnp.zeros((8, 128), F32)], 0)
    tail = tail.astype(BF16)
    for k in range(n):
        msg_ref[k, 0:32, :] = whole
        msg_ref[k, 32:48, :] = tail


def column_kernel(n, parts_ref, e_ref, msg_ref, row_col, out):
    column_sums(1.0 / jnp.sum(parts_ref[...], axis=0), e_ref, row_col, out)
    whole = out[...]
    for k in range(n):
        msg_ref[k] = whole


def last_kernel(n, parts_ref, e_ref, wh_ref, sh_ref, msg_ref, c_ref, prod, acc):
    c_ref[...] = 1.0 / jnp.sum(parts_ref[...], axis=0)
    size = CHUNK // n
    for j in range(e_ref.shape[1] // CHUNK):
        pieces = []
        for b in range(CHUNK // 128):
            at = j * (CHUNK // 128) + b
            piece = e_ref[:, at * 128 : (at + 1) * 128].astype(F32) * c_ref[at : at + 1, :]
            pieces.append(piece)
        part = sum(pieces)
        scaled = jnp.concatenate([p.astype(BF16) for p in pieces], axis=1)
        term = jnp.dot(scaled, wh_ref[lanes(j), :], preferred_element_type=F32)
        if j == 0:
            acc[...] = part
            prod[...] = term
        else:
            acc[...] += part
            prod[...] += term
    tails = []
    for i in range(4):
        rows = lanes(i, 128)
        dots = prod[rows, :] * sh_ref[rows, :].astype(F32)
        dots = (dots[:, 0:128] + dots[:, 128:256]) * 10.0
        tails.append(jnp.concatenate([lay_down(acc[rows, :]), lay_down(dots)], axis=1))
    tail = jnp.concatenate(tails + [jnp.zeros((4, 256), F32)], axis=0)
    for k in range(n):
        msg_ref[k, 0:size, :] = prod[lanes(k, size), :]
        msg_ref[k, size : size + 8, :] = tail


def pick_rows(rows_ref, col_ref, me, size):
    per = 128 // size
    col_ref[...] = column(rows_ref[pl.ds(me // per, 1), :])
    return twice(col_ref[pl.ds(pl.multiple_of((me % per) * size, 8), size), :])


def crops_kernel(
    n_dp, n, parts_ref, tot_ref, p_ref, s_ref, rmsg_ref, gmsg_ref, rows_ref, col_ref
):
    size = CHUNK // n
    total = jnp.sum(parts_ref[...], axis=0)
    scale = 1.0 / total[size : size + 4, 0:128]
    tot = tot_ref[...]
    loss = jnp.sum(scale * total[size : size + 4, 128:256] - jnp.log(tot))
    whole = jnp.concatenate([scale, jnp.full((4, 128), loss, F32)], axis=0)
    for k in range(n_dp):
        rmsg_ref[k] = whole
    me = proto_place()
    rows_ref[...] = jnp.concatenate([scale, 1.0 / tot], axis=0)
    r_col = pick_rows(rows_ref.at[0:4], col_ref, me, size)
    tot_col = pick_rows(rows_ref.at[4:8], col_ref, me, size)
    grad = (p_ref[...] * tot_col - r_col * total[0:size]) * 10.0
    values = s_ref[pl.ds(pl.multiple_of(me * size, 16), size), :].astype(F32)
    inverse = inverse_norms(values)
    s_unit = values * inverse
    grad = (grad - s_unit * jnp.sum(s_unit * grad, axis=-1, keepdims=True)) * inverse
    grad = grad.astype(BF16)
    for k in range(n):
        gmsg_ref[k] = grad


def own_teacher_kernel(w_ref, t_ref, e_ref, done_ref):
    w_half = half_unit(w_ref[...])
    for d in range(t_ref.shape[0]):
        scores = lax.dot_general(w_half, t_ref[d], LAST, preferred_element_type=F32)
        e_ref[:, lanes(d)] = jnp.exp2(scores * T_SCALE).astype(BF16)
    done_ref[...] = jnp.zeros((8, 128), F32)


def own_student_kernel(w_ref, s_hbm, parts_ref, g_ref, s_buf, sems):
    blocks = s_buf.shape[0]
    fetched = begin([(s_hbm.at[d], s_buf.at[d]) for d in range(blocks)], sems)
    w_half = half_unit(w_ref[...])
    total = jnp.zeros((256, 256), F32)
    for d in range(blocks):
        fetched[d].wait()
        scores = lax.dot_general(w_half, s_buf[d], LAST, preferred_element_type=F32)
        tail = parts_ref[d, 32:48, :].astype(F32)
        inv = 1.0 / (tail[0:4] + tail[4:8])
        row = jnp.concatenate([inv[i : i + 1] for i in range(4)], axis=1)
        probs = (jnp.exp2(scores * S_SCALE) * row).astype(BF16)
        total += jnp.dot(probs, s_buf[d], preferred_element_type=F32)
    g_ref[...] = total


def protos_kernel(
    count, parts_ref, e_ref, s_ref, g_ref, c_ref, w_ref, piece_ref, out_ref, loss_ref, crop_ref
):
    size = piece_ref.shape[1]
    for k in range(piece_ref.shape[0]):
        crop_ref[lanes(k, size), :] = piece_ref[k].astype(F32)
    total = jnp.zeros((256, 256), F32)
    loss = jnp.zeros((1, 128), F32)
    for d in range(s_ref.shape[0]):
        row = jnp.concatenate([parts_ref[d, i : i + 1, :] for i in range(4)], axis=1)
        loss += parts_ref[d, 4:5, :]
        scaled = (e_ref[:, lanes(d)].astype(F32) * row).astype(BF16)
        total += jnp.dot(scaled, s_ref[d], preferred_element_type=F32)
    values = w_ref[...].astype(F32)
    inverse = inverse_norms(values)
    w_unit = values * inverse
    first = dp_place() * 2
    cols = [column(c_ref[pl.ds(first + k, 1), :]) for k in range(2)]
    cols = twice(jnp.concatenate(cols, axis=0))
    grad = (g_ref[...] - total * cols) * 10.0
    out_ref[...] = (grad - w_unit * jnp.sum(w_unit * grad, axis=-1, keepdims=True)) * inverse
    loss_ref[0, 0] = loss[0, 0] * (-1.0 / count)


def shape(dims, dtype=F32):
    return jax.ShapeDtypeStruct(dims, dtype)


def per_device(teacher_emb, student_emb, prototypes):
    n_dp = lax.axis_size("z") * lax.axis_size("core")
    n = lax.axis_size("y") * lax.axis_size("x")
    crops, width = teacher_emb.shape
    protos = prototypes.shape[0]
    owned = protos // n_dp
    size = crops // n
    to_dp = lambda msg: lax.all_to_all(msg, CROPS, 0, 0)
    to_proto = lambda msg: lax.all_to_all(msg, PROTOS, 0, 0)
    tie = lax.optimization_barrier
    vm = lambda dims, dtype=F32: pltpu.VMEM(dims, dtype)
    sems = lambda count: pltpu.SemaphoreType.DMA((count,))
    block_flops = 2 * crops * protos * width

    t_half, s_half = call(
        halves_kernel,
        (shape((crops, width), BF16), shape((crops, width), BF16)),
        (teacher_emb, student_emb),
        specs=[HBM, HBM],
        scratch=[vm((crops, width), BF16), vm((crops, width), BF16), sems(2)],
        limit=57,
    )
    t_all = lax.all_gather(t_half, CROPS)
    s_all = lax.all_gather(s_half, CROPS)

    expo, w_half, w_own, msg = call(
        functools.partial(teacher_kernel, n_dp),
        (
            shape((crops, protos), BF16), shape((protos, width), BF16),
            shape((owned, width), BF16), shape((n_dp, 32, 128), BF16),
        ),
        (t_half, prototypes),
        scratch=[vm((32, 128))],
        flops=block_flops,
    )
    tot_part, p_part = call(
        student_kernel,
        (shape((4, 128)), shape((crops, width))),
        (s_half, w_half),
        scratch=[vm((crops, 128))],
        flops=2 * block_flops,
    )
    msg, p_part = tie((msg, p_part))
    parts = to_dp(msg)
    msg = call(
        functools.partial(first_row_kernel, n),
        shape((n, size + 8, width)),
        (parts, expo, tot_part, p_part),
        scratch=[vm((32, 128))],
    )
    parts = to_proto(msg)
    column_scratch = [vm((crops, 128)), vm((32, 128))]
    msg, totals, p_sum = call(
        functools.partial(first_column_kernel, n_dp),
        (shape((n_dp, 48, 128), BF16), shape((4, 128)), shape((size, width))),
        (parts, expo),
        scratch=column_scratch,
    )
    tot_parts = to_dp(msg)
    msg = call(
        functools.partial(row_kernel, n),
        shape((n, 4, 128)),
        (tot_parts, expo),
        scratch=[vm((32, 128))],
    )
    msg, t_all = tie((msg, t_all))
    parts = to_proto(msg)
    parts, t_all = tie((parts, t_all))
    e_own, done = call(
        own_teacher_kernel,
        (shape((owned, n_dp * crops), BF16), shape((8, 128))),
        (w_own, t_all),
        flops=block_flops,
    )
    msg = call(
        functools.partial(column_kernel, n_dp),
        shape((n_dp, 32, 128)),
        (parts, expo),
        scratch=column_scratch,
    )
    msg, done = tie((msg, done))
    parts = to_dp(msg)
    msg, col = call(
        functools.partial(last_kernel, n),
        (shape((n, size + 8, width)), shape((32, 128))),
        (parts, expo, w_half, s_half),
        scratch=[vm((crops, width)), vm((crops, 128))],
        flops=block_flops,
    )
    parts = to_proto(msg)
    rmsg, gmsg = call(
        functools.partial(crops_kernel, n_dp, n),
        (shape((n_dp, 8, 128)), shape((n, size, width), BF16)),
        (parts, totals, p_sum, student_emb),
        scratch=[vm((8, 128)), vm((128, 128))],
    )
    s_all, rmsg = tie((s_all, rmsg))
    g_student = call(
        own_student_kernel,
        shape((owned, width)),
        (w_own, s_all, tot_parts),
        specs=[VMEM, HBM, VMEM],
        scratch=[vm((n_dp, crops, width), BF16), sems(n_dp)],
        flops=2 * block_flops,
        limit=57,
    )
    pieces = to_proto(gmsg)
    rmsg, g_student, pieces = tie((rmsg, g_student, pieces))
    parts = to_dp(rmsg)
    grad_protos, loss, grad_student = call(
        functools.partial(protos_kernel, float(crops * n_dp)),
        (shape((owned, width)), shape((1, 1)), shape((crops, width))),
        (parts, e_own, s_all, g_student, col, w_own, pieces),
        outs=(VMEM, SMEM, VMEM),
        flops=block_flops,
    )
    return grad_student, grad_protos[None], loss[0, 0]


def solution(mesh):
    fine = Mesh(np.asarray(mesh.devices).reshape(8, 2, 4, 4), ("z", "core", "y", "x"))
    in_specs = (P(CROPS, None), P(CROPS, None), P(PROTOS, None))
    out_specs = (P(CROPS, None), P(PROTOS, CROPS, None), P())
    return jax.shard_map(
        per_device, mesh=fine, in_specs=in_specs, out_specs=out_specs, check_vma=False
    )
```

time: 209 us -> 162 us (0.78)
  other arithmetic: 48.9 us -> 0 us
  waiting for transfers between devices: 47.3 us -> 2.55 us
  blocking collectives: 65.3 us -> 96.5 us
  Pallas kernels: 0 us -> 25.3 us
  starting transfers between devices: 25.6 us -> 9.17 us
  matrix products: 14.2 us -> 0 us
  between operations: 2.65 us -> 14.2 us
  local copies, waits for them, and re-layouts: 4.23 us -> 14.1 us
    all_to_all x5 -> x2, waiting for transfers between devices: 47.3 us -> 1.8 us  [the longest x1 1.8 us: per_device(): to_dp = lambda msg: lax.all_to_all(msg, CROPS, 0, 0)]
    all_to_all x5 -> x6, blocking collectives: 65.3 us -> 96.5 us  [the longest x3 51 us: per_device(): to_dp = lambda msg: lax.all_to_all(msg, CROPS, 0, 0)]
    reduce_sum x20 -> x0, other arithmetic: 31.1 us -> none  [the longest x2 9.1 us: per_device(): col = 1.0 / sum_dp(jnp.sum(expo * row[:, None], axis=0))]
    pallas_call x0 -> x12, Pallas kernels: none -> 25.3 us  [call(): pl.pallas_call(kernel, out_shape=out, in_specs=specs or [VMEM] * len(oper...]
    all_to_all x5 -> x2, starting transfers between devices: 25.2 us -> 9.09 us  [the longest x1 5.26 us: per_device(): to_dp = lambda msg: lax.all_to_all(msg, CROPS, 0, 0)]
    dot_general x4 -> x0, matrix products: 14.2 us -> none  [the longest x1 7.1 us: per_device(): lax.dot_general(t_half, w_half, contract_last, preferred_element_type=jnp...]
    unnamed x8 -> x30, local copies, waits for them, and re-layouts: 0.72 us -> 14.1 us
    convert_element_type x2 -> x0, other arithmetic: 10.5 us -> none  [the longest x1 7.23 us: per_device(): ((student_exp / totals[:, None] - weighted * row[:, None]) / 0.1).astype(...]
  transfers between devices with their start and end apart: 6 -> 4, of which waited for: 5 -> 1; matrix products, arithmetic and copies ran while one was open for 8% -> 0% of each run, Pallas kernels for 0% -> 13%
where the time goes in v2:
time: 162 us
  blocking collectives  96.5 us (60%)
  Pallas kernels  25.3 us (16%)
  between operations  14.2 us (9%)
  local copies, waits for them, and re-layouts  14.1 us (9%)
  starting transfers between devices  9.17 us (6%)
  waiting for transfers between devices  2.55 us (2%)
    all_to_all x3, blocking collectives, per_device(): to_dp = lambda msg: lax.all_to_all(msg, CROPS, 0, 0)  51 us
    all_to_all x3, blocking collectives, per_device(): to_proto = lambda msg: lax.all_to_all(msg, PROTOS, 0, 0)  45.5 us
    pallas_call x12, Pallas kernels, call(): pl.pallas_call(kernel, out_shape=out, in_specs=specs or [VMEM] * len(oper...  25.3 us
    unnamed x30, local copies, waits for them, and re-layouts  14.1 us
    all_to_all x1, starting transfers between devices, per_device(): to_dp = lambda msg: lax.all_to_all(msg, CROPS, 0, 0)  5.26 us
    all_to_all x1, starting transfers between devices, per_device(): to_proto = lambda msg: lax.all_to_all(msg, PROTOS, 0, 0)  3.83 us
  transfers between devices with their start and end apart: 4, of which 1 were waited for; matrix products, arithmetic and copies ran while one was open for 0% of the time, Pallas kernels for 13%

profile of v2, /device:TPU:1, one launch (start us, length us, event | category | flops | bytes accessed | tf_op | source)
XLA Modules:
  0.0 161.7 jit_solution(7219133784983774743)
XLA Ops:
  7.2 0.0 all-gather.7.cloned.1.call-start
  7.2 2.0 %shard_map.58 = (bf16[512,256]{1,0:T(8,128)(2,1)}, bf16[512,256]{1,0:T(8,128)(2,1)}) custom-call(bf16[512,256]{1,0:T(8,128)(2,1)} %t_hbm.1, bf16[512,256]{1,0:T(8,128)(2,1)} %s_ref.1), custom_call_target="tpu_custom_call" | custom-call | bytes 524288 | tf_op jit(solution)/shard_map/pallas_call | solution.py:48
  9.2 0.0 copy-start.8
  9.2 0.0 all-gather.7.cloned.1.call-update
  9.2 0.0 all-gather.5.cloned.1.call-start
  9.3 0.7 all-gather.5.cloned.1.call-update
  10.0 0.0 copy-start.13
  10.0 0.9 copy-done.13
  10.9 0.0 copy-start.14
  10.9 1.6 copy-done.14
  12.5 2.1 %shard_map.59 = (bf16[512,4096]{1,0:T(8,128)(2,1)S(1)}, bf16[4096,256]{1,0:T(8,128)(2,1)S(1)}, bf16[256,256]{1,0:T(8,128)(2,1)S(1)}, bf16[16,32,128]{2,1,0:T(8,128)(2,1)S(1)}) custom-call(bf16[512,256]{1,0:T(8,128)(2,1)S(1)} %copy-done.13, bf16[4096,256]{1,0:T(8,128)(2,1)S(1)} %copy-done.14), custom_call_target="tpu_custom_call" | custom-call | flops 1073741824 | bytes 2359296 | tf_op jit(solution)/shard_map/pallas_call | solution.py:48
  14.6 0.0 copy-start.10
  14.6 0.6 copy-done.10
  15.3 0.0 copy-done.8
  15.3 2.5 %shard_map.60 = (f32[4,128]{1,0:T(4,128)S(1)}, f32[512,256]{1,0:T(8,128)S(1)}) custom-call(bf16[512,256]{1,0:T(8,128)(2,1)S(1)} %copy-done.8, bf16[4096,256]{1,0:T(8,128)(2,1)S(1)} %get-tuple-element.36.wh_ref), custom_call_target="tpu_custom_call" | custom-call | flops 2147483648 | bytes 2359296 | tf_op jit(solution)/shard_map/pallas_call | solution.py:48
  17.8 20.4 %all_to_all.40.parts_ref = bf16[16,32,128]{2,1,0:T(8,128)(2,1)S(1)} all-to-all(bf16[16,32,128]{2,1,0:T(8,128)(2,1)S(1)} %get-tuple-element.38), channel_id=1, replica_groups=mesh['z'=8,'core'=2,'y'=4,'x'=4] {'z','core'}, dimensions={0} | all-to-all | bytes 262144 | tf_op jit(solution)/shard_map/all_to_all | solution.py:309
  38.2 0.9 shard_map.61
  39.1 19.4 %all_to_all.41.parts_ref = f32[16,40,256]{2,1,0:T(8,128)S(1)} all-to-all(f32[16,40,256]{2,1,0:T(8,128)S(1)} %shard_map.61), channel_id=1, replica_groups=mesh['z'=8,'core'=2,'y'=4,'x'=4] {'y','x'}, dimensions={0} | all-to-all | bytes 1310720 | tf_op jit(solution)/shard_map/all_to_all | solution.py:310
  58.5 1.1 shard_map.62
  59.6 13.8 %all_to_all.42.parts_ref = bf16[16,48,128]{2,1,0:T(8,128)(2,1)S(1)} all-to-all(bf16[16,48,128]{2,1,0:T(8,128)(2,1)S(1)} %get-tuple-element.42), channel_id=1, replica_groups=mesh['z'=8,'core'=2,'y'=4,'x'=4] {'z','core'}, dimensions={0} | all-to-all | bytes 393216 | tf_op jit(solution)/shard_map/all_to_all | solution.py:309
  73.4 0.0 copy-done
  73.4 0.9 shard_map.63
  74.4 0.0 all-gather.7.cloned.1.call-done
  74.4 9.2 %all_to_all.43.parts_ref = f32[16,4,128]{2,1,0:T(4,128)S(1)} all-to-all(f32[16,4,128]{2,1,0:T(4,128)S(1)} %shard_map.63), channel_id=1, replica_groups=mesh['z'=8,'core'=2,'y'=4,'x'=4] {'y','x'}, dimensions={0} | all-to-all | bytes 65536 | tf_op jit(solution)/shard_map/all_to_all | solution.py:310
  83.6 2.3 %copy-done.1 = bf16[512,4096]{1,0:T(8,128)(2,1)S(1)} copy-done((bf16[512,4096]{1,0:T(8,128)(2,1)S(1)}, bf16[512,4096]{1,0:T(8,128)(2,1)}, u32[]{:S(2)}) %copy-start.1) | copy-done | bytes 4194328
  85.9 1.1 shard_map.64
  87.0 0.0 copy-done.9
  87.0 16.8 %all_to_all.44.parts_ref = f32[16,32,128]{2,1,0:T(8,128)S(1)} all-to-all(f32[16,32,128]{2,1,0:T(8,128)S(1)} %shard_map.64), channel_id=1, replica_groups=mesh['z'=8,'core'=2,'y'=4,'x'=4] {'z','core'}, dimensions={0} | all-to-all | bytes 524288 | tf_op jit(solution)/shard_map/all_to_all | solution.py:309
  103.8 0.0 copy-done.2
  103.8 1.5 shard_map.65
  105.3 16.8 %all_to_all.45.parts_ref = f32[16,40,256]{2,1,0:T(8,128)S(1)} all-to-all(f32[16,40,256]{2,1,0:T(8,128)S(1)} %get-tuple-element.46), channel_id=1, replica_groups=mesh['z'=8,'core'=2,'y'=4,'x'=4] {'y','x'}, dimensions={0} | all-to-all | bytes 1310720 | tf_op jit(solution)/shard_map/all_to_all | solution.py:310
  122.1 0.0 copy-done.7
  122.1 1.0 shard_map.66
  123.1 3.8 %all-to-all-start.6 = ((bf16[16,32,256]{2,1,0:T(8,128)(2,1)}), bf16[16,32,256]{2,1,0:T(8,128)(2,1)S(1)}, u32[]{:S(2)}, u32[]{:S(2)}) async-start(bf16[16,32,256]{2,1,0:T(8,128)(2,1)} %get-tuple-element.53), calls=%async_computation.6 | async-start | bytes 524288 | tf_op jit(solution)/shard_map/all_to_all | solution.py:310
  126.9 0.0 all-gather.5.cloned.1.call-done
  126.9 8.3 %shard_map.67.g_ref = f32[256,256]{1,0:T(8,128)} custom-call(bf16[256,256]{1,0:T(8,128)(2,1)} %copy-done.10, bf16[16,512,256]{2,1,0:T(8,128)(2,1)} %bitcast.4, bf16[16,48,128]{2,1,0:T(8,128)(2,1)} %copy-done.9), custom_call_target="tpu_custom_call" | custom-call | flops 2147483648 | bytes 4521984 | tf_op jit(solution)/shard_map/pallas_call | solution.py:48
  135.2 0.0 all-to-all-done.6.piece_ref
  135.2 5.3 %all-to-all-start.7 = ((f32[16,8,128]{2,1,0:T(8,128)}), f32[16,8,128]{2,1,0:T(8,128)S(1)}, u32[]{:S(2)}, u32[]{:S(2)}) async-start(f32[16,8,128]{2,1,0:T(8,128)} %get-tuple-element.54), calls=%async_computation.7 | async-start | bytes 131072 | tf_op jit(solution)/shard_map/all_to_all | solution.py:309
  140.5 0.0 copy-done.11
  140.5 0.0 copy-start.4
  140.5 2.2 %copy-done.4 = bf16[8192,256]{1,0:T(8,128)(2,1)S(1)} copy-done((bf16[8192,256]{1,0:T(8,128)(2,1)S(1)}, bf16[8192,256]{1,0:T(8,128)(2,1)}, u32[]{:S(2)}) %copy-start.4) | copy-done | bytes 4194328
  142.7 1.8 %shard_map.68 = (bf16[256,8192]{1,0:T(8,128)(2,1)S(1)}, f32[8,128]{1,0:T(8,128)}) custom-call(bf16[256,256]{1,0:T(8,128)(2,1)S(1)} %copy-done.11, bf16[16,512,256]{2,1,0:T(8,128)(2,1)S(1)} %bitcast.6), custom_call_target="tpu_custom_call" | custom-call | flops 1073741824 | bytes 4325376 | tf_op jit(solution)/shard_map/pallas_call | solution.py:48
  144.5 2.0 %copy-done.5 = bf16[256,8192]{1,0:T(8,128)(2,1)} copy-done((bf16[256,8192]{1,0:T(8,128)(2,1)}, bf16[256,8192]{1,0:T(8,128)(2,1)S(1)}, u32[]{:S(2)}) %copy-start.5) | copy-done | bytes 4194328
  146.5 1.8 %all-to-all-done.7.parts_ref = f32[16,8,128]{2,1,0:T(8,128)S(1)} async-done(((f32[16,8,128]{2,1,0:T(8,128)}), f32[16,8,128]{2,1,0:T(8,128)S(1)}, u32[]{:S(2)}, u32[]{:S(2)}) %all-to-all-start.7) | async-done | bytes 65568 | tf_op jit(solution)/shard_map/all_to_all | solution.py:309
  148.3 0.0 copy-done.12
  148.3 2.2 %copy-done.3 = bf16[8192,256]{1,0:T(8,128)(2,1)S(1)} copy-done((bf16[8192,256]{1,0:T(8,128)(2,1)S(1)}, bf16[8192,256]{1,0:T(8,128)(2,1)}, u32[]{:S(2)}) %copy-start.3) | copy-done | bytes 4194328
  150.5 2.2 %copy-done.6 = bf16[256,8192]{1,0:T(8,128)(2,1)S(1)} copy-done((bf16[256,8192]{1,0:T(8,128)(2,1)S(1)}, bf16[256,8192]{1,0:T(8,128)(2,1)}, u32[]{:S(2)}) %copy-start.6) | copy-done | bytes 4194328
  152.7 2.2 %shard_map.69 = (f32[256,256]{1,0:T(8,128)}, f32[1,1]{1,0:T(1,128)}, f32[512,256]{1,0:T(8,128)}) custom-call(f32[16,8,128]{2,1,0:T(8,128)S(1)} %all-to-all-done.7.parts_ref, bf16[256,8192]{1,0:T(8,128)(2,1)S(1)} %copy-done.6, bf16[16,512,256]{2,1,0:T(8,128)(2,1)S(1)} %bitcast.5, f32[256,256]{1,0:T(8,128)S(1)} %copy-done.12, ...), custom_call_target="tpu_custom_call" | custom-call | flops 1073741824 | bytes 9125888 | tf_op jit(solution)/shard_map/pallas_call | solution.py:48
  (10 shorter events, 0.0 us)
Async XLA Ops:
  7.2 67.2 %all-gather.7.cloned.1.call-start = ((), (), s32[]{:S(2)}) async-start(), calls=%async_computation.9 | async-start | bytes 4456448 | tf_op jit(solution)/shard_map/all_gather | solution.py:324
  9.2 6.1 %copy-start.8 = (bf16[512,256]{1,0:T(8,128)(2,1)S(1)}, bf16[512,256]{1,0:T(8,128)(2,1)}, u32[]{:S(2)}) copy-start(bf16[512,256]{1,0:T(8,128)(2,1)} %get-tuple-element.33.sh_ref) | copy-start | bytes 786436
  9.2 117.7 %all-gather.5.cloned.1.call-start = ((), (), s32[]{:S(2)}) async-start(), calls=%async_computation.8 | async-start | bytes 4456448 | tf_op jit(solution)/shard_map/all_gather | solution.py:325
  10.0 1.0 copy-start.13
  10.9 1.6 copy-start.14
  14.6 0.7 copy-start.10
  15.3 58.2 %copy-start = (bf16[512,4096]{1,0:T(8,128)(2,1)}, bf16[512,4096]{1,0:T(8,128)(2,1)S(1)}, u32[]{:S(2)}) copy-start(bf16[512,4096]{1,0:T(8,128)(2,1)S(1)} %get-tuple-element.39.e_ref) | copy-start | bytes 12582916
  73.4 13.6 %copy-start.9 = (bf16[16,48,128]{2,1,0:T(8,128)(2,1)}, bf16[16,48,128]{2,1,0:T(8,128)(2,1)S(1)}, u32[]{:S(2)}) copy-start(bf16[16,48,128]{2,1,0:T(8,128)(2,1)S(1)} %all_to_all.42.parts_ref) | copy-start | bytes 589828
  83.6 2.3 %copy-start.1 = (bf16[512,4096]{1,0:T(8,128)(2,1)S(1)}, bf16[512,4096]{1,0:T(8,128)(2,1)}, u32[]{:S(2)}) copy-start(bf16[512,4096]{1,0:T(8,128)(2,1)} %copy-done) | copy-start | bytes 12582916
  85.9 17.9 %copy-start.2 = (bf16[512,4096]{1,0:T(8,128)(2,1)S(1)}, bf16[512,4096]{1,0:T(8,128)(2,1)}, u32[]{:S(2)}) copy-start(bf16[512,4096]{1,0:T(8,128)(2,1)} %copy-done) | copy-start | bytes 12582916
  103.8 18.3 %copy-start.7 = (bf16[512,256]{1,0:T(8,128)(2,1)S(1)}, bf16[512,256]{1,0:T(8,128)(2,1)}, u32[]{:S(2)}) copy-start(bf16[512,256]{1,0:T(8,128)(2,1)} %s_ref.1) | copy-start | bytes 786436
  123.1 17.4 %copy-start.11 = (bf16[256,256]{1,0:T(8,128)(2,1)S(1)}, bf16[256,256]{1,0:T(8,128)(2,1)}, u32[]{:S(2)}) copy-start(bf16[256,256]{1,0:T(8,128)(2,1)} %copy-done.10) | copy-start | bytes 393220
  123.1 12.1 %all-to-all-start.6 = ((bf16[16,32,256]{2,1,0:T(8,128)(2,1)}), bf16[16,32,256]{2,1,0:T(8,128)(2,1)S(1)}, u32[]{:S(2)}, u32[]{:S(2)}) async-start(bf16[16,32,256]{2,1,0:T(8,128)(2,1)} %get-tuple-element.53), calls=%async_computation.6 | async-start | bytes 524288 | tf_op jit(solution)/shard_map/all_to_all | solution.py:310
  135.2 13.1 %all-to-all-start.7 = ((f32[16,8,128]{2,1,0:T(8,128)}), f32[16,8,128]{2,1,0:T(8,128)S(1)}, u32[]{:S(2)}, u32[]{:S(2)}) async-start(f32[16,8,128]{2,1,0:T(8,128)} %get-tuple-element.54), calls=%async_computation.7 | async-start | bytes 131072 | tf_op jit(solution)/shard_map/all_to_all | solution.py:309
  140.5 2.2 %copy-start.4 = (bf16[8192,256]{1,0:T(8,128)(2,1)S(1)}, bf16[8192,256]{1,0:T(8,128)(2,1)}, u32[]{:S(2)}) copy-start(bf16[8192,256]{1,0:T(8,128)(2,1)} %all-gather.7.cloned.1.call-done) | copy-start | bytes 12582916
  142.7 5.6 %copy-start.12 = (f32[256,256]{1,0:T(8,128)S(1)}, f32[256,256]{1,0:T(8,128)}, u32[]{:S(2)}) copy-start(f32[256,256]{1,0:T(8,128)} %shard_map.67.g_ref) | copy-start | bytes 786436
  144.5 2.0 %copy-start.5 = (bf16[256,8192]{1,0:T(8,128)(2,1)}, bf16[256,8192]{1,0:T(8,128)(2,1)S(1)}, u32[]{:S(2)}) copy-start(bf16[256,8192]{1,0:T(8,128)(2,1)S(1)} %get-tuple-element.56.e_ref) | copy-start | bytes 12582916
  148.3 2.2 %copy-start.3 = (bf16[8192,256]{1,0:T(8,128)(2,1)S(1)}, bf16[8192,256]{1,0:T(8,128)(2,1)}, u32[]{:S(2)}) copy-start(bf16[8192,256]{1,0:T(8,128)(2,1)} %all-gather.5.cloned.1.call-done) | copy-start | bytes 12582916
  150.5 2.2 %copy-start.6 = (bf16[256,8192]{1,0:T(8,128)(2,1)S(1)}, bf16[256,8192]{1,0:T(8,128)(2,1)}, u32[]{:S(2)}) copy-start(bf16[256,8192]{1,0:T(8,128)(2,1)} %copy-done.5) | copy-start | bytes 12582916
Sparse Core Ops, SparseCore 0:
  10.4 48.4 all-gather.6
  61.3 45.5 all-gather.4

commit v3 on v2

--- a/solution.py
+++ b/solution.py
@@ -80,15 +80,19 @@
     return lax.axis_index("y") * lax.axis_size("x") + lax.axis_index("x")
 
 
-def halves_kernel(t_hbm, s_hbm, th_ref, sh_ref, t_buf, s_buf, sems):
+def halves_kernel(t_hbm, s_hbm, th_ref, sh_ref, keep_t, keep_s, t_buf, s_buf, sems):
     one, two = begin([(t_hbm, t_buf), (s_hbm, s_buf)], sems)
     one.wait()
-    th_ref[...] = half_unit(t_buf[...])
+    half = half_unit(t_buf[...])
+    th_ref[...] = half
+    keep_t[...] = half
     two.wait()
-    sh_ref[...] = half_unit(s_buf[...])
-
-
-def teacher_kernel(n, th_ref, w_ref, e_ref, wh_ref, own_ref, msg_ref, sums):
+    half = half_unit(s_buf[...])
+    sh_ref[...] = half
+    keep_s[...] = half
+
+
+def teacher_kernel(n, th_ref, w_ref, e_ref, wh_ref, msg_ref, sums):
     for j in range(w_ref.shape[0] // CHUNK):
         w_half = half_unit(w_ref[lanes(j), :])
         wh_ref[lanes(j), :] = w_half
@@ -102,8 +106,6 @@
     total = sums[...].astype(msg_ref.dtype)
     for k in range(n):
         msg_ref[k] = total
-    owned = own_ref.shape[0]
-    own_ref[...] = w_ref[pl.ds(pl.multiple_of(dp_place() * owned, owned), owned), :]
 
 
 def student_kernel(sh_ref, wh_ref, tot_ref, p_ref, acc):
@@ -127,10 +129,16 @@
     size = CHUNK // n
     tails = [jnp.concatenate([row, tot_ref[i : i + 1, :]], axis=1)
              for i, row in enumerate(row_sums(parts_ref, e_ref, c_ref))]
-    tail = jnp.concatenate(tails + [jnp.zeros((4, 256), F32)], axis=0)
-    for k in range(n):
-        msg_ref[k, 0:size, :] = p_ref[lanes(k, size), :]
-        msg_ref[k, size : size + 8, :] = tail
+    tail = split_pair(jnp.concatenate(tails, axis=0))
+    for k in range(n):
+        msg_ref[k, 0:size, :] = p_ref[lanes(k, size), :].astype(BF16)
+        msg_ref[k, size : size + 16, :] = tail
+
+
+def split_pair(rows):
+    high = rows.astype(BF16).astype(F32)
+    zeros = jnp.zeros((8, rows.shape[1]), F32)
+    return jnp.concatenate([high, rows - high, zeros], axis=0).astype(BF16)
 
 
 def row_sums(parts_ref, e_ref, c_ref):
@@ -164,26 +172,21 @@
 
 def first_column_kernel(n, parts_ref, e_ref, msg_ref, tot_ref, p_ref, row_col, out):
     size = p_ref.shape[0]
-    total = jnp.sum(parts_ref[...], axis=0)
+    total = jnp.sum(parts_ref[...].astype(F32), axis=0)
     p_ref[...] = total[0:size]
-    tot = total[size : size + 4, 128:256]
+    sums = total[size : size + 4] + total[size + 4 : size + 8]
+    tot = sums[:, 128:256]
     tot_ref[...] = tot
-    column_sums(1.0 / total[size : size + 4, 0:128], e_ref, row_col, out)
+    column_sums(1.0 / sums[:, 0:128], e_ref, row_col, out)
     whole = out[...].astype(BF16)
-    high = tot.astype(BF16)
-    low = (tot - high.astype(F32)).astype(BF16)
-    tail = jnp.concatenate([high.astype(F32), low.astype(F32), jnp.zeros((8, 128), F32)], 0)
-    tail = tail.astype(BF16)
+    tail = split_pair(tot)
     for k in range(n):
         msg_ref[k, 0:32, :] = whole
         msg_ref[k, 32:48, :] = tail
 
 
-def column_kernel(n, parts_ref, e_ref, msg_ref, row_col, out):
-    column_sums(1.0 / jnp.sum(parts_ref[...], axis=0), e_ref, row_col, out)
-    whole = out[...]
-    for k in range(n):
-        msg_ref[k] = whole
+def column_kernel(parts_ref, e_ref, msg_ref, row_col):
+    column_sums(1.0 / jnp.sum(parts_ref[...], axis=0), e_ref, row_col, msg_ref)
 
 
 def last_kernel(n, parts_ref, e_ref, wh_ref, sh_ref, msg_ref, c_ref, prod, acc):
@@ -223,7 +226,7 @@
 
 
 def crops_kernel(
-    n_dp, n, parts_ref, tot_ref, p_ref, s_ref, rmsg_ref, gmsg_ref, rows_ref, col_ref
+    n_dp, n, parts_ref, tot_ref, p_ref, s_ref, done_ref, rmsg_ref, gmsg_ref, rows_ref, col_ref
 ):
     size = CHUNK // n
     total = jnp.sum(parts_ref[...], axis=0)
@@ -247,49 +250,76 @@
         gmsg_ref[k] = grad
 
 
-def own_teacher_kernel(w_ref, t_ref, e_ref, done_ref):
-    w_half = half_unit(w_ref[...])
-    for d in range(t_ref.shape[0]):
-        scores = lax.dot_general(w_half, t_ref[d], LAST, preferred_element_type=F32)
-        e_ref[:, lanes(d)] = jnp.exp2(scores * T_SCALE).astype(BF16)
+def pairs_of(src, buf, step):
+    return [(src.at[k : k + step], buf.at[k : k + step]) for k in range(0, buf.shape[0], step)]
+
+
+def own_rows(w_hbm, w_buf):
+    owned = w_buf.shape[0]
+    return w_hbm.at[pl.ds(pl.multiple_of(dp_place() * owned, owned), owned), :]
+
+
+def own_kernel(
+    w_hbm, t_hbm, s_hbm, parts_ref, e_hbm, g_ref, done_ref,
+    w_buf, t_buf, s_buf, e_buf, w_sem, t_sems, s_sems, e_sems,
+):
+    step = 4
+    w_copies = begin([(own_rows(w_hbm, w_buf), w_buf)], w_sem)
+    t_copies = begin(pairs_of(t_hbm, t_buf, step), t_sems)
+    s_copies = begin(pairs_of(s_hbm, s_buf, step), s_sems)
+    e_copies = copies(pairs_of(e_buf, e_hbm, step), e_sems)
+    w_copies[0].wait()
+    w_half = half_unit(w_buf[...])
+    for k in range(len(t_copies)):
+        t_copies[k].wait()
+        for d in range(k * step, k * step + step):
+            scores = lax.dot_general(w_half, t_buf[d], LAST, preferred_element_type=F32)
+            e_buf[d] = jnp.exp2(scores * T_SCALE).astype(BF16)
+        e_copies[k].start()
+    total = jnp.zeros((256, 256), F32)
+    for k in range(len(s_copies)):
+        s_copies[k].wait()
+        for d in range(k * step, k * step + step):
+            scores = lax.dot_general(w_half, s_buf[d], LAST, preferred_element_type=F32)
+            tail = parts_ref[d, 32:48, :].astype(F32)
+            inv = 1.0 / (tail[0:4] + tail[4:8])
+            row = jnp.concatenate([inv[i : i + 1] for i in range(4)], axis=1)
+            probs = (jnp.exp2(scores * S_SCALE) * row).astype(BF16)
+            total += jnp.dot(probs, s_buf[d], preferred_element_type=F32)
+    g_ref[...] = total
     done_ref[...] = jnp.zeros((8, 128), F32)
-
-
-def own_student_kernel(w_ref, s_hbm, parts_ref, g_ref, s_buf, sems):
-    blocks = s_buf.shape[0]
-    fetched = begin([(s_hbm.at[d], s_buf.at[d]) for d in range(blocks)], sems)
-    w_half = half_unit(w_ref[...])
-    total = jnp.zeros((256, 256), F32)
-    for d in range(blocks):
-        fetched[d].wait()
-        scores = lax.dot_general(w_half, s_buf[d], LAST, preferred_element_type=F32)
-        tail = parts_ref[d, 32:48, :].astype(F32)
-        inv = 1.0 / (tail[0:4] + tail[4:8])
-        row = jnp.concatenate([inv[i : i + 1] for i in range(4)], axis=1)
-        probs = (jnp.exp2(scores * S_SCALE) * row).astype(BF16)
-        total += jnp.dot(probs, s_buf[d], preferred_element_type=F32)
-    g_ref[...] = total
+    for c in e_copies:
+        c.wait()
 
 
 def protos_kernel(
-    count, parts_ref, e_ref, s_ref, g_ref, c_ref, w_ref, piece_ref, out_ref, loss_ref, crop_ref
+    count, parts_ref, e_hbm, s_hbm, g_ref, c_ref, w_hbm, out_ref, loss_ref,
+    w_buf, e_buf, s_buf, w_sem, e_sems, s_sems,
 ):
-    size = piece_ref.shape[1]
-    for k in range(piece_ref.shape[0]):
-        crop_ref[lanes(k, size), :] = piece_ref[k].astype(F32)
-    total = jnp.zeros((256, 256), F32)
-    loss = jnp.zeros((1, 128), F32)
-    for d in range(s_ref.shape[0]):
-        row = jnp.concatenate([parts_ref[d, i : i + 1, :] for i in range(4)], axis=1)
-        loss += parts_ref[d, 4:5, :]
-        scaled = (e_ref[:, lanes(d)].astype(F32) * row).astype(BF16)
-        total += jnp.dot(scaled, s_ref[d], preferred_element_type=F32)
-    values = w_ref[...].astype(F32)
+    step = 4
+    w_copies = begin([(own_rows(w_hbm, w_buf), w_buf)], w_sem)
+    e_copies = copies(pairs_of(e_hbm, e_buf, step), e_sems)
+    s_copies = copies(pairs_of(s_hbm, s_buf, step), s_sems)
+    for one, two in zip(e_copies, s_copies):
+        one.start()
+        two.start()
+    w_copies[0].wait()
+    values = w_buf[...].astype(F32)
     inverse = inverse_norms(values)
     w_unit = values * inverse
     first = dp_place() * 2
     cols = [column(c_ref[pl.ds(first + k, 1), :]) for k in range(2)]
     cols = twice(jnp.concatenate(cols, axis=0))
+    total = jnp.zeros((256, 256), F32)
+    loss = jnp.zeros((1, 128), F32)
+    for k in range(len(e_copies)):
+        e_copies[k].wait()
+        s_copies[k].wait()
+        for d in range(k * step, k * step + step):
+            row = jnp.concatenate([parts_ref[d, i : i + 1, :] for i in range(4)], axis=1)
+            loss += parts_ref[d, 4:5, :]
+            scaled = (e_buf[d].astype(F32) * row).astype(BF16)
+            total += jnp.dot(scaled, s_buf[d], preferred_element_type=F32)
     grad = (g_ref[...] - total * cols) * 10.0
     out_ref[...] = (grad - w_unit * jnp.sum(w_unit * grad, axis=-1, keepdims=True)) * inverse
     loss_ref[0, 0] = loss[0, 0] * (-1.0 / count)
@@ -313,22 +343,22 @@
     sems = lambda count: pltpu.SemaphoreType.DMA((count,))
     block_flops = 2 * crops * protos * width
 
-    t_half, s_half = call(
+    t_send, s_send, t_half, s_half = call(
         halves_kernel,
-        (shape((crops, width), BF16), shape((crops, width), BF16)),
+        (shape((crops, width), BF16),) * 4,
         (teacher_emb, student_emb),
         specs=[HBM, HBM],
         scratch=[vm((crops, width), BF16), vm((crops, width), BF16), sems(2)],
         limit=57,
     )
-    t_all = lax.all_gather(t_half, CROPS)
-    s_all = lax.all_gather(s_half, CROPS)
-
-    expo, w_half, w_own, msg = call(
+    t_all = lax.all_gather(t_send, CROPS)
+    s_all = lax.all_gather(s_send, CROPS)
+
+    expo, w_half, msg = call(
         functools.partial(teacher_kernel, n_dp),
         (
             shape((crops, protos), BF16), shape((protos, width), BF16),
-            shape((owned, width), BF16), shape((n_dp, 32, 128), BF16),
+            shape((n_dp, 32, 128), BF16),
         ),
         (t_half, prototypes),
         scratch=[vm((32, 128))],
@@ -345,7 +375,7 @@
     parts = to_dp(msg)
     msg = call(
         functools.partial(first_row_kernel, n),
-        shape((n, size + 8, width)),
+        shape((n, size + 16, width), BF16),
         (parts, expo, tot_part, p_part),
         scratch=[vm((32, 128))],
     )
@@ -364,23 +394,15 @@
         (tot_parts, expo),
         scratch=[vm((32, 128))],
     )
-    msg, t_all = tie((msg, t_all))
     parts = to_proto(msg)
-    parts, t_all = tie((parts, t_all))
-    e_own, done = call(
-        own_teacher_kernel,
-        (shape((owned, n_dp * crops), BF16), shape((8, 128))),
-        (w_own, t_all),
-        flops=block_flops,
-    )
     msg = call(
-        functools.partial(column_kernel, n_dp),
-        shape((n_dp, 32, 128)),
+        column_kernel,
+        shape((32, 128)),
         (parts, expo),
-        scratch=column_scratch,
-    )
-    msg, done = tie((msg, done))
-    parts = to_dp(msg)
+        scratch=column_scratch[:1],
+    )
+    msg = msg + lax.ppermute(msg, "core", [(0, 1), (1, 0)])
+    parts = lax.all_to_all(jnp.broadcast_to(msg, (lax.axis_size("z"), 32, 128)), "z", 0, 0)
     msg, col = call(
         functools.partial(last_kernel, n),
         (shape((n, size + 8, width)), shape((32, 128))),
@@ -388,33 +410,46 @@
         scratch=[vm((crops, width)), vm((crops, 128))],
         flops=block_flops,
     )
+    msg, t_all = tie((msg, t_all))
+    blocks = lambda rows, columns: vm((n_dp, rows, columns), BF16)
+    e_own, g_student, done = call(
+        own_kernel,
+        (shape((n_dp, owned, crops), BF16), shape((owned, width)), shape((8, 128))),
+        (prototypes, t_all, s_all, tot_parts),
+        specs=[HBM, HBM, HBM, VMEM],
+        outs=(HBM, VMEM, VMEM),
+        scratch=[
+            vm((owned, width), BF16),
+            blocks(crops, width), blocks(crops, width), blocks(owned, crops),
+            sems(1), sems(4), sems(4), sems(4),
+        ],
+        flops=3 * block_flops,
+        limit=57,
+    )
     parts = to_proto(msg)
     rmsg, gmsg = call(
         functools.partial(crops_kernel, n_dp, n),
         (shape((n_dp, 8, 128)), shape((n, size, width), BF16)),
-        (parts, totals, p_sum, student_emb),
+        (parts, totals, p_sum, student_emb, done),
         scratch=[vm((8, 128)), vm((128, 128))],
     )
-    s_all, rmsg = tie((s_all, rmsg))
-    g_student = call(
-        own_student_kernel,
-        shape((owned, width)),
-        (w_own, s_all, tot_parts),
-        specs=[VMEM, HBM, VMEM],
-        scratch=[vm((n_dp, crops, width), BF16), sems(n_dp)],
-        flops=2 * block_flops,
+    parts = to_dp(rmsg)
+    parts, gmsg = tie((parts, gmsg))
+    pieces = to_proto(gmsg)
+    grad_protos, loss = call(
+        functools.partial(protos_kernel, float(crops * n_dp)),
+        (shape((owned, width)), shape((1, 1))),
+        (parts, e_own, s_all, g_student, col, prototypes),
+        specs=[VMEM, HBM, HBM, VMEM, VMEM, HBM],
+        outs=(VMEM, SMEM),
+        scratch=[
+            vm((owned, width), BF16), blocks(owned, crops), blocks(crops, width),
+            sems(1), sems(4), sems(4),
+        ],
+        flops=block_flops,
         limit=57,
     )
-    pieces = to_proto(gmsg)
-    rmsg, g_student, pieces = tie((rmsg, g_student, pieces))
-    parts = to_dp(rmsg)
-    grad_protos, loss, grad_student = call(
-        functools.partial(protos_kernel, float(crops * n_dp)),
-        (shape((owned, width)), shape((1, 1)), shape((crops, width))),
-        (parts, e_own, s_all, g_student, col, w_own, pieces),
-        outs=(VMEM, SMEM, VMEM),
-        flops=block_flops,
-    )
+    grad_student = pieces.astype(F32).reshape(crops, width)
     return grad_student, grad_protos[None], loss[0, 0]
 
 

time: 162 us -> 152 us (0.938)
  blocking collectives: 96.5 us -> 85.5 us
  local copies, waits for them, and re-layouts: 14.1 us -> 3.84 us
  Pallas kernels: 25.3 us -> 31.9 us
    all_to_all x3 -> x2, blocking collectives: 45.5 us -> 25.4 us  [per_device(): to_proto = lambda msg: lax.all_to_all(msg, PROTOS, 0, 0)]
    all_to_all x0 -> x1, blocking collectives: none -> 12.8 us  [per_device(): lax.all_to_all(jnp.broadcast_to(msg, (lax.axis_size('z'), 32, 128)), 'z',...]
    unnamed x30 -> x14, local copies, waits for them, and re-layouts: 14.1 us -> 3.82 us
    pallas_call x12 -> x11, Pallas kernels: 25.3 us -> 31.9 us  [call(): pl.pallas_call(kernel, out_shape=out, in_specs=specs or [VMEM] * len(oper...]
    all_to_all x1 -> x2, starting transfers between devices: 3.83 us -> 9.46 us  [per_device(): to_proto = lambda msg: lax.all_to_all(msg, PROTOS, 0, 0)]
    all_to_all x1 -> x0, starting transfers between devices: 5.26 us -> none  [per_device(): to_dp = lambda msg: lax.all_to_all(msg, CROPS, 0, 0)]
    all_to_all x3, blocking collectives: 51 us -> 47.2 us  [per_device(): to_dp = lambda msg: lax.all_to_all(msg, CROPS, 0, 0)]
    all_to_all x1 -> x0, waiting for transfers between devices: 1.8 us -> none  [per_device(): to_dp = lambda msg: lax.all_to_all(msg, CROPS, 0, 0)]
  transfers between devices with their start and end apart: 4 -> 5, of which waited for: 1 -> 3; matrix products, arithmetic and copies ran while one was open for 0% -> 0% of each run, Pallas kernels for 13% -> 19%
where the time goes in v3:
time: 152 us; the launch traced here: 151 us
  blocking collectives  85.5 us (56%)
  Pallas kernels  31.9 us (21%)
  between operations  14.2 us (9%)
  starting transfers between devices  10.7 us (7%)
  waiting for transfers between devices  4.13 us (3%)
  local copies, waits for them, and re-layouts  3.84 us (3%)
    all_to_all x3, blocking collectives, per_device(): to_dp = lambda msg: lax.all_to_all(msg, CROPS, 0, 0)  47.2 us
    pallas_call x11, Pallas kernels, call(): pl.pallas_call(kernel, out_shape=out, in_specs=specs or [VMEM] * len(oper...  31.9 us
    all_to_all x2, blocking collectives, per_device(): to_proto = lambda msg: lax.all_to_all(msg, PROTOS, 0, 0)  25.4 us
    all_to_all x1, blocking collectives, per_device(): lax.all_to_all(jnp.broadcast_to(msg, (lax.axis_size('z'), 32, 128)), 'z',...  12.8 us
    all_to_all x2, starting transfers between devices, per_device(): to_proto = lambda msg: lax.all_to_all(msg, PROTOS, 0, 0)  9.46 us
    unnamed x14, local copies, waits for them, and re-layouts  3.82 us
  transfers between devices with their start and end apart: 5, of which 3 were waited for; matrix products, arithmetic and copies ran while one was open for 0% of the time, Pallas kernels for 19%

profile of v3, /device:TPU:1, one launch (start us, length us, event | category | flops | bytes accessed | tf_op | source)
XLA Modules:
  0.0 151.1 jit_solution(3569422067424563185)
XLA Ops:
  7.2 0.0 all-gather.5.cloned.1.call-start
  7.2 2.2 %shard_map.58 = (bf16[512,256]{1,0:T(8,128)(2,1)}, bf16[512,256]{1,0:T(8,128)(2,1)}, bf16[512,256]{1,0:T(8,128)(2,1)}, bf16[512,256]{1,0:T(8,128)(2,1)}) custom-call(bf16[512,256]{1,0:T(8,128)(2,1)} %t_hbm.1, bf16[512,256]{1,0:T(8,128)(2,1)} %s_ref.1), custom_call_target="tpu_custom_call" | custom-call | bytes 524288 | tf_op jit(solution)/shard_map/pallas_call | solution.py:48
  9.4 0.0 copy-start.3
  9.4 0.0 all-gather.5.cloned.1.call-update
  9.4 0.0 all-gather.7.cloned.1.call-start
  9.5 0.7 all-gather.7.cloned.1.call-update
  10.2 0.0 copy-start
  10.2 1.6 %copy-done = bf16[4096,256]{1,0:T(8,128)(2,1)S(1)} copy-done((bf16[4096,256]{1,0:T(8,128)(2,1)S(1)}, bf16[4096,256]{1,0:T(8,128)(2,1)}, u32[]{:S(2)}) %copy-start) | copy-done | bytes 2097176
  11.8 0.0 copy-start.6
  11.8 0.9 copy-done.6
  12.7 2.1 %shard_map.59 = (bf16[512,4096]{1,0:T(8,128)(2,1)S(1)}, bf16[4096,256]{1,0:T(8,128)(2,1)S(1)}, bf16[16,32,128]{2,1,0:T(8,128)(2,1)S(1)}) custom-call(bf16[512,256]{1,0:T(8,128)(2,1)S(1)} %copy-done.6, bf16[4096,256]{1,0:T(8,128)(2,1)S(1)} %copy-done), custom_call_target="tpu_custom_call" | custom-call | flops 1073741824 | bytes 2359296 | tf_op jit(solution)/shard_map/pallas_call | solution.py:48
  14.8 0.0 copy-done.3
  14.8 2.5 %shard_map.60 = (f32[4,128]{1,0:T(4,128)S(1)}, f32[512,256]{1,0:T(8,128)S(1)}) custom-call(bf16[512,256]{1,0:T(8,128)(2,1)S(1)} %copy-done.3, bf16[4096,256]{1,0:T(8,128)(2,1)S(1)} %get-tuple-element.33.wh_ref), custom_call_target="tpu_custom_call" | custom-call | flops 2147483648 | bytes 2359296 | tf_op jit(solution)/shard_map/pallas_call | solution.py:48
  17.3 20.4 %all_to_all.40.parts_ref = bf16[16,32,128]{2,1,0:T(8,128)(2,1)S(1)} all-to-all(bf16[16,32,128]{2,1,0:T(8,128)(2,1)S(1)} %get-tuple-element.35), channel_id=1, replica_groups=mesh['z'=8,'core'=2,'y'=4,'x'=4] {'z','core'}, dimensions={0} | all-to-all | bytes 262144 | tf_op jit(solution)/shard_map/all_to_all | solution.py:339
  37.7 0.9 shard_map.61
  38.6 16.4 %all_to_all.41.parts_ref = bf16[16,48,256]{2,1,0:T(8,128)(2,1)S(1)} all-to-all(bf16[16,48,256]{2,1,0:T(8,128)(2,1)S(1)} %shard_map.61), channel_id=1, replica_groups=mesh['z'=8,'core'=2,'y'=4,'x'=4] {'y','x'}, dimensions={0} | all-to-all | bytes 786432 | tf_op jit(solution)/shard_map/all_to_all | solution.py:340
  55.0 1.2 shard_map.62
  56.2 14.0 %all_to_all.42.parts_ref = bf16[16,48,128]{2,1,0:T(8,128)(2,1)S(1)} all-to-all(bf16[16,48,128]{2,1,0:T(8,128)(2,1)S(1)} %get-tuple-element.39), channel_id=1, replica_groups=mesh['z'=8,'core'=2,'y'=4,'x'=4] {'z','core'}, dimensions={0} | all-to-all | bytes 393216 | tf_op jit(solution)/shard_map/all_to_all | solution.py:339
  70.2 0.0 copy-start.2
  70.2 0.9 shard_map.63
  71.1 9.1 %all_to_all.43.parts_ref = f32[16,4,128]{2,1,0:T(4,128)S(1)} all-to-all(f32[16,4,128]{2,1,0:T(4,128)S(1)} %shard_map.63), channel_id=1, replica_groups=mesh['z'=8,'core'=2,'y'=4,'x'=4] {'y','x'}, dimensions={0} | all-to-all | bytes 65536 | tf_op jit(solution)/shard_map/all_to_all | solution.py:340
  80.2 1.1 shard_map.64
  81.3 0.0 copy-done.2
  81.3 1.2 collective-permute-start
  82.5 0.8 collective-permute-done
  83.3 12.8 %all_to_all.44.parts_ref = f32[8,32,128]{2,1,0:T(8,128)S(1)} all-to-all(f32[8,32,128]{2,1,0:T(8,128)S(1)} %broadcast_in_dim.6), channel_id=1, replica_groups=mesh['z'=8,'core'=2,'y'=4,'x'=4] {'z'}, dimensions={0} | all-to-all | bytes 262144 | tf_op jit(solution)/shard_map/all_to_all | solution.py:405
  96.1 2.3 %shard_map.65 = (f32[16,40,256]{2,1,0:T(8,128)}, f32[32,128]{1,0:T(8,128)S(1)}) custom-call(f32[8,32,128]{2,1,0:T(8,128)S(1)} %all_to_all.44.parts_ref, bf16[512,4096]{1,0:T(8,128)(2,1)S(1)} %get-tuple-element.36.e_ref, bf16[4096,256]{1,0:T(8,128)(2,1)S(1)} %get-tuple-element.33.wh_ref, bf16[512,256]{1,0:T(8,128)(2,1)S(1)} %copy-done.3), custom_call_target="tpu_custom_call" | custom-call | flops 1073741824 | bytes 6684672 | tf_op jit(solution)/shard_map/pallas_call | solution.py:48
  98.5 0.0 copy-start.4
  98.5 0.6 copy-done.4
  99.1 0.0 all-gather.5.cloned.1.call-done
  99.1 3.6 %all-to-all-start.5 = ((f32[16,40,256]{2,1,0:T(8,128)}), f32[16,40,256]{2,1,0:T(8,128)S(1)}, u32[]{:S(2)}, u32[]{:S(2)}) async-start(f32[16,40,256]{2,1,0:T(8,128)} %get-tuple-element.42), calls=%async_computation.5 | async-start | bytes 1310720 | tf_op jit(solution)/shard_map/all_to_all | solution.py:340
  102.7 1.8 %all-gather.7.cloned.1.call-done = bf16[8192,256]{1,0:T(8,128)(2,1)} async-done(((bf16[512,256]{1,0:T(8,128)(2,1)}), bf16[8192,256]{1,0:T(8,128)(2,1)}) %all-gather.7.cloned.1.call-update) | async-done | bytes 4194320 | tf_op jit(solution)/shard_map/all_gather | solution.py:355
  104.5 0.0 copy-start.1
  104.5 10.2 %shard_map.66 = (bf16[16,256,512]{2,1,0:T(8,128)(2,1)}, f32[256,256]{1,0:T(8,128)}, f32[8,128]{1,0:T(8,128)}) custom-call(bf16[4096,256]{1,0:T(8,128)(2,1)} %w_hbm.3, bf16[16,512,256]{2,1,0:T(8,128)(2,1)} %bitcast.9, bf16[16,512,256]{2,1,0:T(8,128)(2,1)} %bitcast.7, bf16[16,48,128]{2,1,0:T(8,128)(2,1)} %copy-done.2), custom_call_target="tpu_custom_call" | custom-call | flops 3221225472 | bytes 10682368 | tf_op jit(solution)/shard_map/pallas_call | solution.py:48
  114.7 0.0 all-to-all-done.5.parts_ref
  114.7 0.0 copy-done.1
  114.7 0.0 copy-start.5
  114.7 0.7 copy-done.5
  115.4 1.0 shard_map.67
  116.4 12.8 %all_to_all.45.parts_ref = f32[16,8,128]{2,1,0:T(8,128)} all-to-all(f32[16,8,128]{2,1,0:T(8,128)S(1)} %get-tuple-element.48), channel_id=1, replica_groups=mesh['z'=8,'core'=2,'y'=4,'x'=4] {'z','core'}, dimensions={0} | all-to-all | bytes 131072 | tf_op jit(solution)/shard_map/all_to_all | solution.py:339
  129.2 5.9 %all-to-all-start.7 = ((bf16[16,32,256]{2,1,0:T(8,128)(2,1)}), bf16[16,32,256]{2,1,0:T(8,128)(2,1)S(1)}, u32[]{:S(2)}, u32[]{:S(2)}) async-start(bf16[16,32,256]{2,1,0:T(8,128)(2,1)} %get-tuple-element.50), calls=%async_computation.7 | async-start | bytes 524288 | tf_op jit(solution)/shard_map/all_to_all | solution.py:340
  135.0 7.6 %shard_map.68 = (f32[256,256]{1,0:T(8,128)}, f32[1,1]{1,0:T(1,128)}) custom-call(f32[16,8,128]{2,1,0:T(8,128)} %all_to_all.45.parts_ref, bf16[16,256,512]{2,1,0:T(8,128)(2,1)} %get-tuple-element.52.e_hbm, bf16[16,512,256]{2,1,0:T(8,128)(2,1)} %bitcast.8, f32[256,256]{1,0:T(8,128)} %get-tuple-element.53.g_ref, f32[32,128]{1,0:T(8,128)} %copy-done.4, ...), custom_call_target="tpu_custom_call" | custom-call | flops 1073741824 | bytes 10829824 | tf_op jit(solution)/shard_map/pallas_call | solution.py:48
  142.7 0.7 all-to-all-done.7
  143.4 0.8 bitcast_convert_fusion
  (2 shorter events, 0.0 us)
Async XLA Ops:
  7.2 91.9 %all-gather.5.cloned.1.call-start = ((), (), s32[]{:S(2)}) async-start(), calls=%async_computation.8 | async-start | bytes 4456448 | tf_op jit(solution)/shard_map/all_gather | solution.py:354
  9.4 5.4 %copy-start.3 = (bf16[512,256]{1,0:T(8,128)(2,1)S(1)}, bf16[512,256]{1,0:T(8,128)(2,1)}, u32[]{:S(2)}) copy-start(bf16[512,256]{1,0:T(8,128)(2,1)} %get-tuple-element.32.sh_ref) | copy-start | bytes 786436
  9.4 95.1 %all-gather.7.cloned.1.call-start = ((), (), s32[]{:S(2)}) async-start(), calls=%async_computation.9 | async-start | bytes 4456448 | tf_op jit(solution)/shard_map/all_gather | solution.py:355
  10.2 1.6 %copy-start = (bf16[4096,256]{1,0:T(8,128)(2,1)S(1)}, bf16[4096,256]{1,0:T(8,128)(2,1)}, u32[]{:S(2)}) copy-start(bf16[4096,256]{1,0:T(8,128)(2,1)} %w_hbm.3) | copy-start | bytes 6291460
  11.8 0.9 copy-start.6
  70.2 11.1 %copy-start.2 = (bf16[16,48,128]{2,1,0:T(8,128)(2,1)}, bf16[16,48,128]{2,1,0:T(8,128)(2,1)S(1)}, u32[]{:S(2)}) copy-start(bf16[16,48,128]{2,1,0:T(8,128)(2,1)S(1)} %all_to_all.42.parts_ref) | copy-start | bytes 589828
  81.3 2.0 %collective-permute-start = (f32[32,128]{1,0:T(8,128)S(1)}, f32[32,128]{1,0:T(8,128)S(1)}, u32[]{:S(2)}, u32[]{:S(2)}) collective-permute-start(f32[32,128]{1,0:T(8,128)S(1)} %shard_map.64), channel_id=1, source_target_pairs={{0,16},{16,0},{1,17},{17,1},{2,18},{18,2},{3,19},{19,3},{4,20},{20... | collective-permute-start | bytes 49160 | tf_op jit(solution)/shard_map/ppermute | solution.py:404
  98.5 0.6 copy-start.4
  99.1 15.6 %all-to-all-start.5 = ((f32[16,40,256]{2,1,0:T(8,128)}), f32[16,40,256]{2,1,0:T(8,128)S(1)}, u32[]{:S(2)}, u32[]{:S(2)}) async-start(f32[16,40,256]{2,1,0:T(8,128)} %get-tuple-element.42), calls=%async_computation.5 | async-start | bytes 1310720 | tf_op jit(solution)/shard_map/all_to_all | solution.py:340
  104.5 10.2 %copy-start.1 = (bf16[512,256]{1,0:T(8,128)(2,1)S(1)}, bf16[512,256]{1,0:T(8,128)(2,1)}, u32[]{:S(2)}) copy-start(bf16[512,256]{1,0:T(8,128)(2,1)} %s_ref.1) | copy-start | bytes 786436
  114.7 0.7 copy-start.5
  129.2 14.2 %all-to-all-start.7 = ((bf16[16,32,256]{2,1,0:T(8,128)(2,1)}), bf16[16,32,256]{2,1,0:T(8,128)(2,1)S(1)}, u32[]{:S(2)}, u32[]{:S(2)}) async-start(bf16[16,32,256]{2,1,0:T(8,128)(2,1)} %get-tuple-element.50), calls=%async_computation.7 | async-start | bytes 524288 | tf_op jit(solution)/shard_map/all_to_all | solution.py:340
Sparse Core Ops, SparseCore 0:
  10.4 48.6 all-gather.4
  61.5 42.9 all-gather.6

commit v4 on v3

v4 whole, which is shorter than its diff:
```python
import functools

import jax
import jax.numpy as jnp
import numpy as np
from jax import lax
from jax.experimental import pallas as pl
from jax.experimental.pallas import tpu as pltpu
from jax.sharding import Mesh, PartitionSpec as P

CROPS = ("z", "core")
PROTOS = ("y", "x")
LOG2E = 1.4426950408889634
T_SCALE = LOG2E / 0.07
S_SCALE = LOG2E / 0.1
F32 = jnp.float32
BF16 = jnp.bfloat16
VMEM = pl.BlockSpec(memory_space=pltpu.VMEM)
SMEM = pl.BlockSpec(memory_space=pltpu.SMEM)
HBM = pl.BlockSpec(memory_space=pltpu.HBM)
LAST = (((1,), (1,)), ((), ()))
CHUNK = 512


def inverse_norms(values):
    return lax.rsqrt(jnp.sum(values * values, axis=-1, keepdims=True) + 1e-06)


def half_unit(block):
    values = block.astype(F32)
    return (values * inverse_norms(values)).astype(BF16)


def column(row):
    return jnp.broadcast_to(row, (128, 128)).T


def lay_down(block):
    return jnp.sum(block.T, axis=0, keepdims=True)


def twice(block):
    return jnp.concatenate([block, block], axis=1)


def call(kernel, out, operands, specs=None, outs=None, scratch=(), flops=0, limit=12):
    touched = sum(x.size * x.dtype.itemsize for x in operands)
    return pl.pallas_call(
        kernel,
        out_shape=out,
        in_specs=specs or [VMEM] * len(operands),
        out_specs=outs or jax.tree.map(lambda _: VMEM, out),
        scratch_shapes=list(scratch),
        cost_estimate=pl.CostEstimate(flops=flops, bytes_accessed=touched, transcendentals=0),
        compiler_params=pltpu.CompilerParams(vmem_limit_bytes=limit << 20),
    )(*operands)


def copies(pairs, sems):
    out = [pltpu.make_async_copy(a, b, sems.at[k]) for k, (a, b) in enumerate(pairs)]
    return out


def begin(pairs, sems):
    started = copies(pairs, sems)
    for c in started:
        c.start()
    return started


def lanes(k, size=CHUNK):
    return pl.ds(k * size, size)


def dp_place():
    return lax.axis_index("z") * lax.axis_size("core") + lax.axis_index("core")


def proto_place():
    return lax.axis_index("y") * lax.axis_size("x") + lax.axis_index("x")


def teacher_kernel(n, t_ref, s_ref, w_ref, x_ref, sh_ref, e0, e1, wh_ref, msg_ref, sums):
    t_half = half_unit(t_ref[...])
    x_ref[0] = t_half
    for j in range(w_ref.shape[0] // CHUNK):
        w_half = half_unit(w_ref[lanes(j), :])
        wh_ref[lanes(j), :] = w_half
        scores = lax.dot_general(x_ref[0], w_half, LAST, preferred_element_type=F32)
        expo = jnp.exp2(scores * T_SCALE)
        for i, e_ref in enumerate((e0, e1)):
            e_ref[:, lanes(j)] = expo[i * 256 : (i + 1) * 256].astype(BF16)
        part = jnp.sum(expo, axis=0, keepdims=True)
        for b in range(CHUNK // 128):
            at = j * (CHUNK // 128) + b
            sums[at : at + 1, :] = part[:, b * 128 : (b + 1) * 128]
    total = sums[...].astype(msg_ref.dtype)
    for k in range(n):
        msg_ref[k] = total
    s_half = half_unit(s_ref[...])
    x_ref[1] = s_half
    sh_ref[...] = s_half


def student_kernel(sh_ref, wh_ref, tot_ref, p_ref, acc):
    for j in range(wh_ref.shape[0] // CHUNK):
        w_half = wh_ref[lanes(j), :]
        scores = lax.dot_general(sh_ref[...], w_half, LAST, preferred_element_type=F32)
        expo = jnp.exp2(scores * S_SCALE)
        part = sum(expo[:, b * 128 : (b + 1) * 128] for b in range(CHUNK // 128))
        prod = jnp.dot(expo.astype(BF16), w_half, preferred_element_type=F32)
        if j == 0:
            acc[...] = part
            p_ref[...] = prod
        else:
            acc[...] += part
            p_ref[...] += prod
    for i in range(4):
        tot_ref[i : i + 1, :] = lay_down(acc[lanes(i, 128), :])


def first_row_kernel(n, parts_ref, e0, e1, tot_ref, p_ref, msg_ref, c_ref):
    size = CHUNK // n
    tails = [jnp.concatenate([row, tot_ref[i : i + 1, :]], axis=1)
             for i, row in enumerate(row_sums(parts_ref, (e0, e1), c_ref))]
    tail = split_pair(jnp.concatenate(tails, axis=0))
    for k in range(n):
        msg_ref[k, 0:size, :] = p_ref[lanes(k, size), :].astype(BF16)
        msg_ref[k, size : size + 16, :] = tail


def split_pair(rows):
    high = rows.astype(BF16).astype(F32)
    zeros = jnp.zeros((8, rows.shape[1]), F32)
    return jnp.concatenate([high, rows - high, zeros], axis=0).astype(BF16)


def row_sums(parts_ref, e_refs, c_ref):
    c_ref[...] = 1.0 / jnp.sum(parts_ref[:, 0:32, :].astype(F32), axis=0)
    out = []
    for i in range(4):
        rows = lanes(i % 2, 128)
        acc = jnp.zeros((128, 128), F32)
        for b in range(32):
            part = e_refs[i // 2][rows, b * 128 : (b + 1) * 128].astype(F32)
            acc += part * c_ref[b : b + 1, :]
        out.append(lay_down(acc))
    return out


def row_kernel(n, parts_ref, e0, e1, msg_ref, c_ref):
    whole = jnp.concatenate(row_sums(parts_ref, (e0, e1), c_ref), axis=0)
    for k in range(n):
        msg_ref[k] = whole


def column_sums(scale, e_refs, row_col, out):
    for i in range(4):
        row_col[lanes(i, 128), :] = column(scale[i : i + 1])
    for b in range(32):
        acc = jnp.zeros((8, 128), F32)
        for i in range(4):
            rows = lanes(i, 128)
            part = e_refs[i // 2][lanes(i % 2, 128), b * 128 : (b + 1) * 128].astype(F32)
            prod = part * row_col[rows, :]
            acc += jnp.sum(prod.reshape(16, 8, 128), axis=0)
        out[b : b + 1, :] = jnp.sum(acc, axis=0, keepdims=True)


def first_column_kernel(n, parts_ref, e0, e1, msg_ref, tot_ref, p_ref, row_col, out):
    size = p_ref.shape[0]
    total = jnp.sum(parts_ref[...].astype(F32), axis=0)
    p_ref[...] = total[0:size]
    sums = total[size : size + 4] + total[size + 4 : size + 8]
    tot = sums[:, 128:256]
    tot_ref[...] = tot
    column_sums(1.0 / sums[:, 0:128], (e0, e1), row_col, out)
    whole = out[...].astype(BF16)
    tail = split_pair(tot)
    for k in range(n):
        msg_ref[k, 0:32, :] = whole
        msg_ref[k, 32:48, :] = tail


def column_kernel(parts_ref, e0, e1, msg_ref, row_col):
    column_sums(1.0 / jnp.sum(parts_ref[...], axis=0), (e0, e1), row_col, msg_ref)


def last_kernel(n, parts_ref, e0, e1, wh_ref, sh_ref, msg_ref, c_ref, prod, acc):
    c_ref[...] = 1.0 / jnp.sum(parts_ref[...], axis=0)
    size = CHUNK // n
    for j in range(e0.shape[1] // CHUNK):
        pieces = []
        for b in range(CHUNK // 128):
            at = j * (CHUNK // 128) + b
            span = slice(at * 128, (at + 1) * 128)
            piece = jnp.concatenate([e[:, span] for e in (e0, e1)], axis=0)
            pieces.append(piece.astype(F32) * c_ref[at : at + 1, :])
        part = sum(pieces)
        scaled = jnp.concatenate([p.astype(BF16) for p in pieces], axis=1)
        term = jnp.dot(scaled, wh_ref[lanes(j), :], preferred_element_type=F32)
        if j == 0:
            acc[...] = part
            prod[...] = term
        else:
            acc[...] += part
            prod[...] += term
    tails = []
    for i in range(4):
        rows = lanes(i, 128)
        dots = prod[rows, :] * sh_ref[rows, :].astype(F32)
        dots = (dots[:, 0:128] + dots[:, 128:256]) * 10.0
        tails.append(jnp.concatenate([lay_down(acc[rows, :]), lay_down(dots)], axis=1))
    tail = jnp.concatenate(tails + [jnp.zeros((4, 256), F32)], axis=0)
    for k in range(n):
        msg_ref[k, 0:size, :] = prod[lanes(k, size), :]
        msg_ref[k, size : size + 8, :] = tail


def pick_rows(rows_ref, col_ref, me, size):
    per = 128 // size
    col_ref[...] = column(rows_ref[pl.ds(me // per, 1), :])
    return twice(col_ref[pl.ds(pl.multiple_of((me % per) * size, 8), size), :])


def crops_kernel(
    n_z, n, parts_ref, tot_ref, p_ref, s_ref, rmsg_ref, gmsg_ref, rows_ref, col_ref
):
    size = CHUNK // n
    total = jnp.sum(parts_ref[...], axis=0)
    scale = 1.0 / total[size : size + 4, 0:128]
    tot = tot_ref[...]
    loss = jnp.sum(scale * total[size : size + 4, 128:256] - jnp.log(tot))
    whole = jnp.concatenate([scale, jnp.full((4, 128), loss, F32)], axis=0)
    for k in range(n_z):
        rmsg_ref[k] = whole
    me = proto_place()
    rows_ref[...] = jnp.concatenate([scale, 1.0 / tot], axis=0)
    r_col = pick_rows(rows_ref.at[0:4], col_ref, me, size)
    tot_col = pick_rows(rows_ref.at[4:8], col_ref, me, size)
    grad = (p_ref[...] * tot_col - r_col * total[0:size]) * 10.0
    values = s_ref[pl.ds(pl.multiple_of(me * size, 16), size), :].astype(F32)
    inverse = inverse_norms(values)
    s_unit = values * inverse
    grad = (grad - s_unit * jnp.sum(s_unit * grad, axis=-1, keepdims=True)) * inverse
    grad = grad.astype(BF16)
    for k in range(n):
        gmsg_ref[k] = grad


HOPS = (0, -1, 1, -2, 2, -3, 3, -4)


def slot_place(k):
    n_z = lax.axis_size("z")
    return lax.rem(lax.axis_index("z") + HOPS[k] + n_z, n_z)


def chip_rows(w_hbm, w_buf):
    rows = w_buf.shape[0]
    return w_hbm.at[pl.ds(pl.multiple_of(lax.axis_index("z") * rows, rows), rows), :]


def student_term(w_half, s_half, parts_ref, k):
    scores = lax.dot_general(w_half, s_half, LAST, preferred_element_type=F32)
    tail = parts_ref[slot_place(k) * 2 + lax.axis_index("core"), 32:48, :].astype(F32)
    inv = 1.0 / (tail[0:4] + tail[4:8])
    row = jnp.concatenate([inv[i : i + 1] for i in range(4)], axis=1)
    probs = (jnp.exp2(scores * S_SCALE) * row).astype(BF16)
    return jnp.dot(probs, s_half, preferred_element_type=F32)


def own_teacher_kernel(w_hbm, *refs):
    blocks = refs[:8]
    parts_ref, e_hbm, g_ref, w_buf, t_buf, s_buf, e_buf, w_sem, t_sems, s_sem, e_sems = refs[8:]
    w_copies = begin([(chip_rows(w_hbm, w_buf), w_buf)], w_sem)
    t_copies = begin([(x.at[0], t_buf.at[k]) for k, x in enumerate(blocks)], t_sems)
    s_copies = begin([(blocks[7].at[1], s_buf)], s_sem)
    e_copies = copies([(e_buf.at[k], e_hbm.at[k]) for k in range(8)], e_sems)
    w_copies[0].wait()
    w_half = half_unit(w_buf[...])
    for k in range(8):
        t_copies[k].wait()
        scores = lax.dot_general(w_half, t_buf[k], LAST, preferred_element_type=F32)
        e_buf[k] = jnp.exp2(scores * T_SCALE).astype(BF16)
        e_copies[k].start()
    s_copies[0].wait()
    g_ref[...] = student_term(w_half, s_buf[...], parts_ref, 7)
    for c in e_copies:
        c.wait()


def own_student_kernel(w_hbm, *refs):
    blocks = refs[:7]
    parts_ref, g_ref, w_buf, s_buf, total, w_sem, s_sems = refs[7:]
    w_copies = begin([(chip_rows(w_hbm, w_buf), w_buf)], w_sem)
    s_copies = begin([(x.at[1], s_buf.at[k]) for k, x in enumerate(blocks)], s_sems)
    w_copies[0].wait()
    w_half = half_unit(w_buf[...])
    for k in range(7):
        s_copies[k].wait()
        term = student_term(w_half, s_buf[k], parts_ref, k)
        if k == 0:
            total[...] = term
        else:
            total[...] += term
    g_ref[...] = total[...]


def protos_kernel(parts_ref, e_hbm, g_ref, late_ref, c_ref, w_hbm, *refs):
    blocks = refs[:8]
    keep_ref, give_ref, own_ref, e_buf, s_buf, total, w_sem, e_sems, s_sems = refs[8:]
    half = own_ref.shape[0]
    start = pl.multiple_of(dp_place() * half, half)
    w_copies = begin([(w_hbm.at[pl.ds(start, half), :], own_ref)], w_sem)
    e_copies = copies([(e_hbm.at[k], e_buf.at[k]) for k in range(8)], e_sems)
    s_copies = copies([(x.at[1], s_buf.at[k]) for k, x in enumerate(blocks)], s_sems)
    for one, two in zip(e_copies, s_copies):
        one.start()
        two.start()
    first = lax.axis_index("z") * 4
    cols = [column(c_ref[pl.ds(first + i, 1), :]) for i in range(4)]
    loss = jnp.zeros((1, 128), F32)
    for k in range(8):
        z = slot_place(k)
        row = jnp.concatenate([parts_ref[z, i : i + 1, :] for i in range(4)], axis=1)
        loss += parts_ref[z, 4:5, :]
        e_copies[k].wait()
        scaled = (e_buf[k].astype(F32) * row).astype(BF16)
        s_copies[k].wait()
        term = jnp.dot(scaled, s_buf[k], preferred_element_type=F32)
        if k == 0:
            total[...] = term
        else:
            total[...] += term
    for i in range(4):
        rows = lanes(i, 128)
        total[rows, :] = (
            g_ref[rows, :] + late_ref[rows, :] - total[rows, :] * twice(cols[i])
        ) * 10.0
    core = lax.axis_index("core")
    keep_ref[0:half, :] = total[pl.ds(pl.multiple_of(core * half, half), half), :]
    give_ref[0:half, :] = total[pl.ds(pl.multiple_of((1 - core) * half, half), half), :]
    loss = twice(jnp.broadcast_to(loss, (8, 128)))
    give_ref[half : half + 8, :] = loss
    keep_ref[half : half + 8, :] = loss
    w_copies[0].wait()
    keep_ref[half + 8 : 2 * half + 8, :] = own_ref[...].astype(F32)


def finish_kernel(count, keep_ref, got_ref, out_ref, mean_ref):
    half = out_ref.shape[0]
    values = keep_ref[half + 8 : 2 * half + 8, :]
    inverse = inverse_norms(values)
    w_unit = values * inverse
    grad = keep_ref[0:half, :] + got_ref[0:half, :]
    loss = keep_ref[half : half + 1, :] + got_ref[half : half + 1, :]
    out_ref[...] = (grad - w_unit * jnp.sum(w_unit * grad, axis=-1, keepdims=True)) * inverse
    mean_ref[0, 0] = loss[0, 0] * (-1.0 / count)


def shape(dims, dtype=F32):
    return jax.ShapeDtypeStruct(dims, dtype)


def per_device(teacher_emb, student_emb, prototypes):
    n_z = lax.axis_size("z")
    n_dp = n_z * lax.axis_size("core")
    n = lax.axis_size("y") * lax.axis_size("x")
    crops, width = teacher_emb.shape
    protos = prototypes.shape[0]
    owned = protos // n_dp
    size = crops // n
    to_dp = lambda msg: lax.all_to_all(msg, CROPS, 0, 0)
    to_proto = lambda msg: lax.all_to_all(msg, PROTOS, 0, 0)
    tie = lax.optimization_barrier
    vm = lambda dims, dtype=F32: pltpu.VMEM(dims, dtype)
    sems = lambda count: pltpu.SemaphoreType.DMA((count,))
    block_flops = 2 * crops * protos * width

    right = lambda x: lax.ppermute(x, "z", [(i, (i + 1) % n_z) for i in range(n_z)])
    left = lambda x: lax.ppermute(x, "z", [(i, (i - 1) % n_z) for i in range(n_z)])
    swap = lambda x: lax.ppermute(x, "core", [(0, 1), (1, 0)])

    here, s_half, *expo, w_half, msg = call(
        functools.partial(teacher_kernel, n_dp),
        (
            shape((2, crops, width), BF16), shape((crops, width), BF16),
            *[shape((crops // 2, protos), BF16)] * 2, shape((protos, width), BF16),
            shape((n_dp, 32, 128), BF16),
        ),
        (teacher_emb, student_emb, prototypes),
        scratch=[vm((32, 128))],
        flops=block_flops,
    )
    a1, b1 = right(here), left(here)
    tot_part, p_part = call(
        student_kernel,
        (shape((4, 128)), shape((crops, width))),
        (s_half, w_half),
        scratch=[vm((crops, 128))],
        flops=2 * block_flops,
    )
    msg, p_part = tie((msg, p_part))
    parts = to_dp(msg)
    parts, a1, b1 = tie((parts, a1, b1))
    a2, b2 = right(a1), left(b1)
    msg = call(
        functools.partial(first_row_kernel, n),
        shape((n, size + 16, width), BF16),
        (parts, *expo, tot_part, p_part),
        scratch=[vm((32, 128))],
    )
    parts = to_proto(msg)
    column_scratch = [vm((crops, 128)), vm((32, 128))]
    msg, totals, p_sum = call(
        functools.partial(first_column_kernel, n_dp),
        (shape((n_dp, 48, 128), BF16), shape((4, 128)), shape((size, width))),
        (parts, *expo),
        scratch=column_scratch,
    )
    tot_parts = to_dp(msg)
    msg = call(
        functools.partial(row_kernel, n),
        shape((n, 4, 128)),
        (tot_parts, *expo),
        scratch=[vm((32, 128))],
    )
    msg, a2, b2 = tie((msg, a2, b2))
    a3, b3 = right(a2), left(b2)
    parts = to_proto(msg)
    msg = call(
        column_kernel,
        shape((32, 128)),
        (parts, *expo),
        scratch=column_scratch[:1],
    )
    msg = msg + swap(msg)
    to_z = lambda msg: lax.all_to_all(msg, "z", 0, 0)
    parts = to_z(jnp.broadcast_to(msg, (n_z, 32, 128)))
    parts, a3, b3 = tie((parts, a3, b3))
    a4 = right(a3)
    gathered = (here, a1, b1, a2, b2, a3, b3, a4)
    msg, col = call(
        functools.partial(last_kernel, n),
        (shape((n, size + 8, width)), shape((32, 128))),
        (parts, *expo, w_half, s_half),
        scratch=[vm((crops, width)), vm((crops, 128))],
        flops=block_flops,
    )
    msg, *gathered = tie((msg,) + gathered[:-1])
    gathered = tuple(gathered) + (a4,)
    blocks = lambda rows, columns: vm((n_z, rows, columns), BF16)
    chip = 2 * owned
    g_student = call(
        own_student_kernel,
        shape((chip, width)),
        (prototypes,) + gathered[:-1] + (tot_parts,),
        specs=[HBM] * 8 + [VMEM],
        scratch=[
            vm((chip, width), BF16), blocks(crops, width), vm((chip, width)), sems(1), sems(n_z),
        ],
        flops=2 * block_flops,
        limit=57,
    )
    parts = to_proto(msg)
    rmsg, gmsg = call(
        functools.partial(crops_kernel, n_z, n),
        (shape((n_z, 8, 128)), shape((n, size, width), BF16)),
        (parts, totals, p_sum, student_emb),
        scratch=[vm((8, 128)), vm((128, 128))],
    )
    rmsg, g_student, *late = tie((rmsg, g_student) + gathered)
    e_own, g_late = call(
        own_teacher_kernel,
        (shape((n_z, chip, crops), BF16), shape((chip, width))),
        (prototypes,) + tuple(late) + (tot_parts,),
        specs=[HBM] * 9 + [VMEM],
        outs=(HBM, VMEM),
        scratch=[
            vm((chip, width), BF16), blocks(crops, width), vm((crops, width), BF16),
            blocks(chip, crops), sems(1), sems(n_z), sems(1), sems(n_z),
        ],
        flops=block_flops,
        limit=57,
    )
    parts = to_z(rmsg)
    parts, gmsg, e_own = tie((parts, gmsg, e_own))
    pieces = to_proto(gmsg)
    keep, give = call(
        protos_kernel,
        (shape((2 * owned + 8, width)), shape((owned + 8, width))),
        (parts, e_own, g_student, g_late, col, prototypes) + tuple(late),
        specs=[VMEM, HBM, VMEM, VMEM, VMEM, HBM] + [HBM] * 8,
        scratch=[
            vm((owned, width), BF16), blocks(chip, crops), blocks(crops, width), vm((chip, width)),
            sems(1), sems(n_z), sems(n_z),
        ],
        flops=block_flops,
        limit=57,
    )
    grad_protos, loss = call(
        functools.partial(finish_kernel, float(crops * n_dp)),
        (shape((owned, width)), shape((1, 1))),
        (keep, swap(give)),
        outs=(VMEM, SMEM),
    )
    grad_student = pieces.astype(F32).reshape(crops, width)
    return grad_student, grad_protos[None], loss[0, 0]


def solution(mesh):
    fine = Mesh(np.asarray(mesh.devices).reshape(8, 2, 4, 4), ("z", "core", "y", "x"))
    in_specs = (P(CROPS, None), P(CROPS, None), P(PROTOS, None))
    out_specs = (P(CROPS, None), P(PROTOS, CROPS, None), P())
    return jax.shard_map(
        per_device, mesh=fine, in_specs=in_specs, out_specs=out_specs, check_vma=False
    )
```

time: 152 us -> 147 us (0.967)
  blocking collectives: 85.5 us -> 50.6 us
  starting transfers between devices: 10.7 us -> 38.3 us
  between operations: 14.2 us -> 1.07 us
  waiting for transfers between devices: 4.13 us -> 12.1 us
  local copies, waits for them, and re-layouts: 3.84 us -> 7.64 us
  Pallas kernels: 31.9 us -> 35.3 us
    ppermute x1 -> x9, starting transfers between devices: 1.19 us -> 18.4 us  [the longest x3 10.6 us: per_device(): lax.ppermute(x, 'z', [(i, (i - 1) % n_z) for i in range(n_z)])]
    all_to_all x2 -> x1, blocking collectives: 25.4 us -> 9.06 us  [per_device(): to_proto = lambda msg: lax.all_to_all(msg, PROTOS, 0, 0)]
    all_to_all x3 -> x2, blocking collectives: 47.2 us -> 31 us  [per_device(): to_dp = lambda msg: lax.all_to_all(msg, CROPS, 0, 0)]
    all_to_all x2 -> x3, waiting for transfers between devices: 0.74 us -> 10 us  [per_device(): to_proto = lambda msg: lax.all_to_all(msg, PROTOS, 0, 0)]
    all_to_all x2 -> x3, starting transfers between devices: 9.46 us -> 16.7 us  [per_device(): to_proto = lambda msg: lax.all_to_all(msg, PROTOS, 0, 0)]
    unnamed x14 -> x38, local copies, waits for them, and re-layouts: 3.82 us -> 7.63 us
    pallas_call x11 -> x12, Pallas kernels: 31.9 us -> 35.3 us  [call(): pl.pallas_call(kernel, out_shape=out, in_specs=specs or [VMEM] * len(oper...]
    all_to_all x0 -> x1, starting transfers between devices: none -> 3.33 us  [per_device(): to_z = lambda msg: lax.all_to_all(msg, 'z', 0, 0)]
  transfers between devices with their start and end apart: 5 -> 13, of which waited for: 3 -> 5; matrix products, arithmetic and copies ran while one was open for 0% -> 1% of each run, Pallas kernels for 19% -> 19%
where the time goes in v4:
time: 147 us; the launch traced here: 146 us
  blocking collectives  50.6 us (34%)
  starting transfers between devices  38.3 us (26%)
  Pallas kernels  35.3 us (24%)
  waiting for transfers between devices  12.1 us (8%)
  local copies, waits for them, and re-layouts  7.64 us (5%)
    pallas_call x12, Pallas kernels, call(): pl.pallas_call(kernel, out_shape=out, in_specs=specs or [VMEM] * len(oper...  35.3 us
    all_to_all x2, blocking collectives, per_device(): to_dp = lambda msg: lax.all_to_all(msg, CROPS, 0, 0)  31 us
    all_to_all x3, starting transfers between devices, per_device(): to_proto = lambda msg: lax.all_to_all(msg, PROTOS, 0, 0)  16.7 us
    all_to_all x1, blocking collectives, per_device(): to_z = lambda msg: lax.all_to_all(msg, 'z', 0, 0)  10.6 us
    ppermute x3, starting transfers between devices, per_device(): lax.ppermute(x, 'z', [(i, (i - 1) % n_z) for i in range(n_z)])  10.6 us
    all_to_all x3, waiting for transfers between devices, per_device(): to_proto = lambda msg: lax.all_to_all(msg, PROTOS, 0, 0)  10 us
    all_to_all x1, blocking collectives, per_device(): to_proto = lambda msg: lax.all_to_all(msg, PROTOS, 0, 0)  9.06 us
    unnamed x38, local copies, waits for them, and re-layouts  7.63 us
  transfers between devices with their start and end apart: 13, of which 5 were waited for; matrix products, arithmetic and copies ran while one was open for 1% of the time, Pallas kernels for 19%

profile of v4, /device:TPU:1, one launch (start us, length us, event | category | flops | bytes accessed | tf_op | source)
XLA Modules:
  0.0 145.9 jit_solution(9612048781323505878)
XLA Ops:
  0.6 0.0 copy-start.3
  0.6 1.6 %copy-done.3 = bf16[4096,256]{1,0:T(8,128)(2,1)S(1)} copy-done((bf16[4096,256]{1,0:T(8,128)(2,1)S(1)}, bf16[4096,256]{1,0:T(8,128)(2,1)}, u32[]{:S(2)}) %copy-start.3) | copy-done | bytes 2097176
  2.2 0.9 copy-done.9
  3.2 0.9 copy-done.12
  4.1 2.2 %shard_map.58 = (bf16[2,512,256]{2,1,0:T(8,128)(2,1)S(1)}, bf16[512,256]{1,0:T(8,128)(2,1)S(1)}, bf16[256,4096]{1,0:T(8,128)(2,1)S(1)}, bf16[256,4096]{1,0:T(8,1...) custom-call(bf16[512,256]{1,0:T(8,128)(2,1)S(1)} %copy-done.12, ...), custom_call_target="tpu_custom_call" | custom-call | flops 1073741824 | bytes 2621440 | tf_op jit(solution)/shard_map/pallas_call | solution.py:48
  6.3 0.0 copy-start.6
  6.4 6.5 %collective-permute-start.1 = (bf16[2,512,256]{2,1,0:T(8,128)(2,1)S(1)}, bf16[2,512,256]{2,1,0:T(8,128)(2,1)S(1)}, u32[]{:S(2)}, u32[]{:S(2)}) collective-permute-start(bf16[2,512,256]{2,1,0:T(8,128)(2,1)S(1)} %get-tuple-element.90.refs_0_), channel_id=1, source_target_pairs={{0,224},{32,0},{64,32},{96,64},{128,96},{160,128},{192,160},{224,1... | collective-permute-start | bytes 1572872 | tf_op jit(solution)/shard_map/ppermute | solution.py:382
  12.8 2.5 %shard_map.59 = (f32[4,128]{1,0:T(4,128)S(1)}, f32[512,256]{1,0:T(8,128)S(1)}) custom-call(bf16[512,256]{1,0:T(8,128)(2,1)S(1)} %get-tuple-element.57.sh_ref, bf16[4096,256]{1,0:T(8,128)(2,1)S(1)} %get-tuple-element.58.wh_ref), custom_call_target="tpu_custom_call" | custom-call | flops 2147483648 | bytes 2359296 | tf_op jit(solution)/shard_map/pallas_call | solution.py:48
  15.4 14.9 %all_to_all.40.parts_ref = bf16[16,32,128]{2,1,0:T(8,128)(2,1)S(1)} all-to-all(bf16[16,32,128]{2,1,0:T(8,128)(2,1)S(1)} %get-tuple-element.60), channel_id=1, replica_groups=mesh['z'=8,'core'=2,'y'=4,'x'=4] {'z','core'}, dimensions={0} | all-to-all | bytes 262144 | tf_op jit(solution)/shard_map/all_to_all | solution.py:374
  30.2 0.0 collective-permute-done.1.refs_2_
  30.3 0.0 collective-permute-done.refs_1_
  30.3 0.9 copy-done.14
  31.1 1.7 %shard_map.60 = bf16[16,48,256]{2,1,0:T(8,128)(2,1)} custom-call(bf16[16,32,128]{2,1,0:T(8,128)(2,1)S(1)} %all_to_all.40.parts_ref, bf16[256,4096]{1,0:T(8,128)(2,1)S(1)} %get-tuple-element.63.e0, bf16[256,4096]{1,0:T(8,128)(2,1)S(1)} %get-tuple-element.64.e1, f32[4,128]{1,0:T(4,128)S(1)} %get-tuple-element.65.tot_ref, f32[512,256]{1,0:T(8,128)S(1)} %get-tuple-element.66.p_ref), custom_call_target="tpu_custom_call" | custom-call | bytes 4851712 | tf_op jit(solution)/shard_map/pallas_call | solution.py:48
  32.8 6.8 %all-to-all-start.1 = ((bf16[16,48,256]{2,1,0:T(8,128)(2,1)}), bf16[16,48,256]{2,1,0:T(8,128)(2,1)S(1)}, u32[]{:S(2)}, u32[]{:S(2)}) async-start(bf16[16,48,256]{2,1,0:T(8,128)(2,1)} %shard_map.60), calls=%async_computation.1 | async-start | bytes 786432 | tf_op jit(solution)/shard_map/all_to_all | solution.py:375
  39.6 1.3 collective-permute-start.2
  40.9 1.4 collective-permute-start.3
  42.3 6.1 %all-to-all-done.1.parts_ref = bf16[16,48,256]{2,1,0:T(8,128)(2,1)S(1)} async-done(((bf16[16,48,256]{2,1,0:T(8,128)(2,1)}), bf16[16,48,256]{2,1,0:T(8,128)(2,1)S(1)}, u32[]{:S(2)}, u32[]{:S(2)}) %all-to-all-start.1) | async-done | bytes 393248 | tf_op jit(solution)/shard_map/all_to_all | solution.py:375
  48.5 1.6 %copy-done.1 = bf16[256,4096]{1,0:T(8,128)(2,1)S(1)} copy-done((bf16[256,4096]{1,0:T(8,128)(2,1)S(1)}, bf16[256,4096]{1,0:T(8,128)(2,1)}, u32[]{:S(2)}) %copy-start.1) | copy-done | bytes 2097176
  50.1 1.1 shard_map.61
  51.2 16.1 %all_to_all.41.parts_ref.refs_7_.refs_8_ = bf16[16,48,128]{2,1,0:T(8,128)(2,1)S(1)} all-to-all(bf16[16,48,128]{2,1,0:T(8,128)(2,1)S(1)} %get-tuple-element.67), channel_id=1, replica_groups=mesh['z'=8,'core'=2,'y'=4,'x'=4] {'z','core'}, dimensions={0} | all-to-all | bytes 393216 | tf_op jit(solution)/shard_map/all_to_all | solution.py:374
  67.3 0.9 shard_map.62
  68.2 0.0 collective-permute-done.2.refs_3_
  68.3 0.3 collective-permute-start.5
  68.5 2.7 %collective-permute-start.6 = (bf16[2,512,256]{2,1,0:T(8,128)(2,1)}, bf16[2,512,256]{2,1,0:T(8,128)(2,1)S(1)}, u32[]{:S(2)}, u32[]{:S(2)}) collective-permute-start(bf16[2,512,256]{2,1,0:T(8,128)(2,1)} %collective-permute-done.3.refs_4_), channel_id=1, source_target_pairs={{0,224},{32,0},{64,32},{96,64},{128,96},{160,128},{192,160},{224,1... | collective-permute-start | bytes 1572872 | tf_op jit(solution)/shard_map/ppermute | solution.py:382
  71.2 9.1 %all_to_all.42.parts_ref = f32[16,4,128]{2,1,0:T(4,128)S(1)} all-to-all(f32[16,4,128]{2,1,0:T(4,128)S(1)} %shard_map.62), channel_id=1, replica_groups=mesh['z'=8,'core'=2,'y'=4,'x'=4] {'y','x'}, dimensions={0} | all-to-all | bytes 65536 | tf_op jit(solution)/shard_map/all_to_all | solution.py:375
  80.3 1.1 shard_map.63
  81.3 1.8 %collective-permute-start.4 = (f32[32,128]{1,0:T(8,128)S(1)}, f32[32,128]{1,0:T(8,128)S(1)}, u32[]{:S(2)}, u32[]{:S(2)}) collective-permute-start(f32[32,128]{1,0:T(8,128)S(1)} %shard_map.63), channel_id=1, source_target_pairs={{0,16},{16,0},{1,17},{17,1},{2,18},{18,2},{3,19},{19,3},{4,20},{20... | collective-permute-start | bytes 49160 | tf_op jit(solution)/shard_map/ppermute | solution.py:383
  83.1 0.8 collective-permute-done.4
  84.0 10.6 %all_to_all.43.parts_ref = f32[8,32,128]{2,1,0:T(8,128)S(1)} all-to-all(f32[8,32,128]{2,1,0:T(8,128)S(1)} %broadcast_in_dim.6), channel_id=1, replica_groups=mesh['z'=8,'core'=2,'y'=4,'x'=4] {'z'}, dimensions={0} | all-to-all | bytes 262144 | tf_op jit(solution)/shard_map/all_to_all | solution.py:439
  94.6 2.3 %shard_map.64 = (f32[16,40,256]{2,1,0:T(8,128)}, f32[32,128]{1,0:T(8,128)S(1)}) custom-call(f32[8,32,128]{2,1,0:T(8,128)S(1)} %all_to_all.43.parts_ref, bf16[256,4096]{1,0:T(8,128)(2,1)S(1)} %get-tuple-element.63.e0, bf16[256,4096]{1,0:T(8,128)(2,1)S(1)} %copy-done.2, bf16[4096,256]{1,0:T(8,128)(2,1)S(1)} %copy-done.5, ...), custom_call_target="tpu_custom_call" | custom-call | flops 1073741824 | bytes 6684672 | tf_op jit(solution)/shard_map/pallas_call | solution.py:48
  96.9 0.6 copy-done.11
  97.5 3.6 %all-to-all-start.5 = ((f32[16,40,256]{2,1,0:T(8,128)}), f32[16,40,256]{2,1,0:T(8,128)S(1)}, u32[]{:S(2)}, u32[]{:S(2)}) async-start(f32[16,40,256]{2,1,0:T(8,128)} %get-tuple-element.77), calls=%async_computation.5 | async-start | bytes 1310720 | tf_op jit(solution)/shard_map/all_to_all | solution.py:375
  101.1 0.0 copy-start.10
  101.2 0.2 collective-permute-start.7
  101.3 6.9 %shard_map.66.g_ref = f32[512,256]{1,0:T(8,128)} custom-call(bf16[4096,256]{1,0:T(8,128)(2,1)} %w_hbm.5, bf16[2,512,256]{2,1,0:T(8,128)(2,1)} %copy-done.6, bf16[2,512,256]{2,1,0:T(8,128)(2,1)} %copy-done.14, bf16[2,512,256]{2,1,0:T(8,128)(2,1)} %copy-done.13, bf16[2,512,256]{2,1,0:T(8,128)(2,1)} %collective-permute-done.2.refs_3_, ...), custom_call_target="tpu_custom_call" | custom-call | flops 2147483648 | bytes 5963776 | tf_op jit(solution)/shard_map/pallas_call | solution.py:48
  108.2 3.9 %all-to-all-done.5.parts_ref = f32[16,40,256]{2,1,0:T(8,128)S(1)} async-done(((f32[16,40,256]{2,1,0:T(8,128)}), f32[16,40,256]{2,1,0:T(8,128)S(1)}, u32[]{:S(2)}, u32[]{:S(2)}) %all-to-all-start.5) | async-done | bytes 655392 | tf_op jit(solution)/shard_map/all_to_all | solution.py:375
  112.1 1.0 shard_map.65
  113.1 0.7 collective-permute-done.7.refs_7_
  113.8 3.3 %all-to-all-start.6 = ((f32[8,8,128]{2,1,0:T(8,128)}), f32[8,8,128]{2,1,0:T(8,128)S(1)}, u32[]{:S(2)}, u32[]{:S(2)}) async-start(f32[8,8,128]{2,1,0:T(8,128)} %get-tuple-element.88), calls=%async_computation.6 | async-start | bytes 65536 | tf_op jit(solution)/shard_map/all_to_all | solution.py:439
  117.1 7.4 %shard_map.67 = (bf16[8,512,512]{2,1,0:T(8,128)(2,1)}, f32[512,256]{1,0:T(8,128)}) custom-call(bf16[4096,256]{1,0:T(8,128)(2,1)} %w_hbm.5, bf16[2,512,256]{2,1,0:T(8,128)(2,1)} %copy-done.6, bf16[2,512,256]{2,1,0:T(8,128)(2,1)} %copy-done.14, bf16[2,512,256]{2,1,0:T(8,128)(2,1)} %copy-done.13, bf16[2,512,256]{2,1,0:T(8,128)(2,1)} %collective-permute-done.2.refs_3_, ...), custom_call_target="tpu_custom_call" | custom-call | flops 1073741824 | bytes 6488064 | tf_op jit(solution)/shard_map/pallas_call | solution.py:48
  124.5 0.0 all-to-all-done.6.parts_ref
  124.5 6.3 %all-to-all-start.7 = ((bf16[16,32,256]{2,1,0:T(8,128)(2,1)}), bf16[16,32,256]{2,1,0:T(8,128)(2,1)S(1)}, u32[]{:S(2)}, u32[]{:S(2)}) async-start(bf16[16,32,256]{2,1,0:T(8,128)(2,1)} %get-tuple-element.99), calls=%async_computation.7 | async-start | bytes 524288 | tf_op jit(solution)/shard_map/all_to_all | solution.py:375
  130.8 7.3 %shard_map.68 = (f32[520,256]{1,0:T(8,128)}, f32[264,256]{1,0:T(8,128)}) custom-call(f32[8,8,128]{2,1,0:T(8,128)} %copy-done.18, bf16[8,512,512]{2,1,0:T(8,128)(2,1)} %get-tuple-element.101.e_hbm, f32[512,256]{1,0:T(8,128)} %shard_map.66.g_ref, f32[512,256]{1,0:T(8,128)} %get-tuple-element.103.late_ref, f32[32,128]{1,0:T(8,128)} %copy-done.11, ...), custom_call_target="tpu_custom_call" | custom-call | flops 1073741824 | bytes 11583488 | tf_op jit(solution)/shard_map/pallas_call | solution.py:48
  138.1 4.2 %collective-permute-start.8 = (f32[264,256]{1,0:T(8,128)}, f32[264,256]{1,0:T(8,128)S(1)}, u32[]{:S(2)}, u32[]{:S(2)}) collective-permute-start(f32[264,256]{1,0:T(8,128)} %get-tuple-element.106), channel_id=1, source_target_pairs={{0,16},{16,0},{1,17},{17,1},{2,18},{18,2},{3,19},{19,3},{4,20},{20... | collective-permute-start | bytes 811016 | tf_op jit(solution)/shard_map/ppermute | solution.py:383
  142.4 0.8 bitcast_convert_fusion
  143.2 0.5 collective-permute-done.8.got_ref
  143.8 1.0 copy-done.8
  144.8 0.9 shard_map.69
  (35 shorter events, 0.1 us)
Async XLA Ops:
  0.6 1.6 %copy-start.3 = (bf16[4096,256]{1,0:T(8,128)(2,1)S(1)}, bf16[4096,256]{1,0:T(8,128)(2,1)}, u32[]{:S(2)}) copy-start(bf16[4096,256]{1,0:T(8,128)(2,1)} %w_hbm.5) | copy-start | bytes 6291460
  2.2 0.9 copy-start.9
  3.2 0.9 copy-start.12
  6.3 9.0 %copy-start.4 = (bf16[4096,256]{1,0:T(8,128)(2,1)}, bf16[4096,256]{1,0:T(8,128)(2,1)S(1)}, u32[]{:S(2)}) copy-start(bf16[4096,256]{1,0:T(8,128)(2,1)S(1)} %get-tuple-element.58.wh_ref) | copy-start | bytes 6291460
  6.3 9.0 %copy-start.6 = (bf16[2,512,256]{2,1,0:T(8,128)(2,1)}, bf16[2,512,256]{2,1,0:T(8,128)(2,1)S(1)}, u32[]{:S(2)}) copy-start(bf16[2,512,256]{2,1,0:T(8,128)(2,1)S(1)} %get-tuple-element.90.refs_0_) | copy-start | bytes 1572868
  6.3 24.8 %copy-start = (bf16[256,4096]{1,0:T(8,128)(2,1)}, bf16[256,4096]{1,0:T(8,128)(2,1)S(1)}, u32[]{:S(2)}) copy-start(bf16[256,4096]{1,0:T(8,128)(2,1)S(1)} %get-tuple-element.64.e1) | copy-start | bytes 6291460
  6.4 23.9 %collective-permute-start.1 = (bf16[2,512,256]{2,1,0:T(8,128)(2,1)S(1)}, bf16[2,512,256]{2,1,0:T(8,128)(2,1)S(1)}, u32[]{:S(2)}, u32[]{:S(2)}) collective-permute-start(bf16[2,512,256]{2,1,0:T(8,128)(2,1)S(1)} %get-tuple-element.90.refs_0_), channel_id=1, source_target_pairs={{0,224},{32,0},{64,32},{96,64},{128,96},{160,128},{192,160},{224,1... | collective-permute-start | bytes 1572872 | tf_op jit(solution)/shard_map/ppermute | solution.py:382
  12.8 17.4 %collective-permute-start = (bf16[2,512,256]{2,1,0:T(8,128)(2,1)S(1)}, bf16[2,512,256]{2,1,0:T(8,128)(2,1)S(1)}, u32[]{:S(2)}, u32[]{:S(2)}) collective-permute-start(bf16[2,512,256]{2,1,0:T(8,128)(2,1)S(1)} %get-tuple-element.90.refs_0_), channel_id=1, source_target_pairs={{0,32},{32,64},{64,96},{96,128},{128,160},{160,192},{192,224},{224... | collective-permute-start | bytes 1572872 | tf_op jit(solution)/shard_map/ppermute | solution.py:381
  30.2 10.7 %copy-start.13 = (bf16[2,512,256]{2,1,0:T(8,128)(2,1)}, bf16[2,512,256]{2,1,0:T(8,128)(2,1)S(1)}, u32[]{:S(2)}) copy-start(bf16[2,512,256]{2,1,0:T(8,128)(2,1)S(1)} %collective-permute-done.1.refs_2_) | copy-start | bytes 1572868
  30.3 0.9 copy-start.14
  32.8 15.6 %all-to-all-start.1 = ((bf16[16,48,256]{2,1,0:T(8,128)(2,1)}), bf16[16,48,256]{2,1,0:T(8,128)(2,1)S(1)}, u32[]{:S(2)}, u32[]{:S(2)}) async-start(bf16[16,48,256]{2,1,0:T(8,128)(2,1)} %shard_map.60), calls=%async_computation.1 | async-start | bytes 786432 | tf_op jit(solution)/shard_map/all_to_all | solution.py:375
  39.6 28.7 %collective-permute-start.2 = (bf16[2,512,256]{2,1,0:T(8,128)(2,1)}, bf16[2,512,256]{2,1,0:T(8,128)(2,1)}, u32[]{:S(2)}, u32[]{:S(2)}) collective-permute-start(bf16[2,512,256]{2,1,0:T(8,128)(2,1)} %copy-done.14), channel_id=1, source_target_pairs={{0,32},{32,64},{64,96},{96,128},{128,160},{160,192},{192,224},{224... | collective-permute-start | bytes 1572872 | tf_op jit(solution)/shard_map/ppermute | solution.py:381
  40.9 27.3 %collective-permute-start.3 = (bf16[2,512,256]{2,1,0:T(8,128)(2,1)S(1)}, bf16[2,512,256]{2,1,0:T(8,128)(2,1)}, u32[]{:S(2)}, u32[]{:S(2)}) collective-permute-start(bf16[2,512,256]{2,1,0:T(8,128)(2,1)S(1)} %collective-permute-done.1.refs_2_), channel_id=1, source_target_pairs={{0,224},{32,0},{64,32},{96,64},{128,96},{160,128},{192,160},{224,1... | collective-permute-start | bytes 1572872 | tf_op jit(solution)/shard_map/ppermute | solution.py:382
  48.5 1.6 %copy-start.1 = (bf16[256,4096]{1,0:T(8,128)(2,1)S(1)}, bf16[256,4096]{1,0:T(8,128)(2,1)}, u32[]{:S(2)}) copy-start(bf16[256,4096]{1,0:T(8,128)(2,1)} %copy-done) | copy-start | bytes 6291460
  67.3 0.9 copy-start.7
  68.3 26.3 %collective-permute-start.5 = (bf16[2,512,256]{2,1,0:T(8,128)(2,1)}, bf16[2,512,256]{2,1,0:T(8,128)(2,1)S(1)}, u32[]{:S(2)}, u32[]{:S(2)}) collective-permute-start(bf16[2,512,256]{2,1,0:T(8,128)(2,1)} %collective-permute-done.2.refs_3_), channel_id=1, source_target_pairs={{0,32},{32,64},{64,96},{96,128},{128,160},{160,192},{192,224},{224... | collective-permute-start | bytes 1572872 | tf_op jit(solution)/shard_map/ppermute | solution.py:381
  68.5 26.0 %collective-permute-start.6 = (bf16[2,512,256]{2,1,0:T(8,128)(2,1)}, bf16[2,512,256]{2,1,0:T(8,128)(2,1)S(1)}, u32[]{:S(2)}, u32[]{:S(2)}) collective-permute-start(bf16[2,512,256]{2,1,0:T(8,128)(2,1)} %collective-permute-done.3.refs_4_), channel_id=1, source_target_pairs={{0,224},{32,0},{64,32},{96,64},{128,96},{160,128},{192,160},{224,1... | collective-permute-start | bytes 1572872 | tf_op jit(solution)/shard_map/ppermute | solution.py:382
  80.3 14.3 %copy-start.2 = (bf16[256,4096]{1,0:T(8,128)(2,1)S(1)}, bf16[256,4096]{1,0:T(8,128)(2,1)}, u32[]{:S(2)}) copy-start(bf16[256,4096]{1,0:T(8,128)(2,1)} %copy-done) | copy-start | bytes 6291460
  80.3 14.3 %copy-start.5 = (bf16[4096,256]{1,0:T(8,128)(2,1)S(1)}, bf16[4096,256]{1,0:T(8,128)(2,1)}, u32[]{:S(2)}) copy-start(bf16[4096,256]{1,0:T(8,128)(2,1)} %copy-done.4) | copy-start | bytes 6291460
  81.3 2.6 %collective-permute-start.4 = (f32[32,128]{1,0:T(8,128)S(1)}, f32[32,128]{1,0:T(8,128)S(1)}, u32[]{:S(2)}, u32[]{:S(2)}) collective-permute-start(f32[32,128]{1,0:T(8,128)S(1)} %shard_map.63), channel_id=1, source_target_pairs={{0,16},{16,0},{1,17},{17,1},{2,18},{18,2},{3,19},{19,3},{4,20},{20... | collective-permute-start | bytes 49160 | tf_op jit(solution)/shard_map/ppermute | solution.py:383
  94.6 6.6 %copy-start.15 = (bf16[2,512,256]{2,1,0:T(8,128)(2,1)}, bf16[2,512,256]{2,1,0:T(8,128)(2,1)S(1)}, u32[]{:S(2)}) copy-start(bf16[2,512,256]{2,1,0:T(8,128)(2,1)S(1)} %collective-permute-done.5.refs_5_) | copy-start | bytes 1572868
  94.6 2.4 %copy-start.16 = (bf16[2,512,256]{2,1,0:T(8,128)(2,1)}, bf16[2,512,256]{2,1,0:T(8,128)(2,1)S(1)}, u32[]{:S(2)}) copy-start(bf16[2,512,256]{2,1,0:T(8,128)(2,1)S(1)} %collective-permute-done.6.refs_6_) | copy-start | bytes 1572868
  96.9 0.6 copy-start.11
  97.5 14.6 %all-to-all-start.5 = ((f32[16,40,256]{2,1,0:T(8,128)}), f32[16,40,256]{2,1,0:T(8,128)S(1)}, u32[]{:S(2)}, u32[]{:S(2)}) async-start(f32[16,40,256]{2,1,0:T(8,128)} %get-tuple-element.77), calls=%async_computation.5 | async-start | bytes 1310720 | tf_op jit(solution)/shard_map/all_to_all | solution.py:375
  101.1 11.0 %copy-start.10 = (bf16[512,256]{1,0:T(8,128)(2,1)S(1)}, bf16[512,256]{1,0:T(8,128)(2,1)}, u32[]{:S(2)}) copy-start(bf16[512,256]{1,0:T(8,128)(2,1)} %s_ref.3) | copy-start | bytes 786436
  101.2 12.6 %collective-permute-start.7 = (bf16[2,512,256]{2,1,0:T(8,128)(2,1)S(1)}, bf16[2,512,256]{2,1,0:T(8,128)(2,1)S(1)}, u32[]{:S(2)}, u32[]{:S(2)}) collective-permute-start(bf16[2,512,256]{2,1,0:T(8,128)(2,1)S(1)} %collective-permute-done.5.refs_5_), channel_id=1, source_target_pairs={{0,32},{32,64},{64,96},{96,128},{128,160},{160,192},{192,224},{224... | collective-permute-start | bytes 1572872 | tf_op jit(solution)/shard_map/ppermute | solution.py:381
  113.8 3.3 %copy-start.17 = (bf16[2,512,256]{2,1,0:T(8,128)(2,1)}, bf16[2,512,256]{2,1,0:T(8,128)(2,1)S(1)}, u32[]{:S(2)}) copy-start(bf16[2,512,256]{2,1,0:T(8,128)(2,1)S(1)} %collective-permute-done.7.refs_7_) | copy-start | bytes 1572868
  113.8 10.7 %all-to-all-start.6 = ((f32[8,8,128]{2,1,0:T(8,128)}), f32[8,8,128]{2,1,0:T(8,128)S(1)}, u32[]{:S(2)}, u32[]{:S(2)}) async-start(f32[8,8,128]{2,1,0:T(8,128)} %get-tuple-element.88), calls=%async_computation.6 | async-start | bytes 65536 | tf_op jit(solution)/shard_map/all_to_all | solution.py:439
  124.5 6.3 %copy-start.18 = (f32[8,8,128]{2,1,0:T(8,128)}, f32[8,8,128]{2,1,0:T(8,128)S(1)}, u32[]{:S(2)}) copy-start(f32[8,8,128]{2,1,0:T(8,128)S(1)} %all-to-all-done.6.parts_ref) | copy-start | bytes 98308
  124.5 17.9 %all-to-all-start.7 = ((bf16[16,32,256]{2,1,0:T(8,128)(2,1)}), bf16[16,32,256]{2,1,0:T(8,128)(2,1)S(1)}, u32[]{:S(2)}, u32[]{:S(2)}) async-start(bf16[16,32,256]{2,1,0:T(8,128)(2,1)} %get-tuple-element.99), calls=%async_computation.7 | async-start | bytes 524288 | tf_op jit(solution)/shard_map/all_to_all | solution.py:375
  138.1 5.6 %collective-permute-start.8 = (f32[264,256]{1,0:T(8,128)}, f32[264,256]{1,0:T(8,128)S(1)}, u32[]{:S(2)}, u32[]{:S(2)}) collective-permute-start(f32[264,256]{1,0:T(8,128)} %get-tuple-element.106), channel_id=1, source_target_pairs={{0,16},{16,0},{1,17},{17,1},{2,18},{18,2},{3,19},{19,3},{4,20},{20... | collective-permute-start | bytes 811016 | tf_op jit(solution)/shard_map/ppermute | solution.py:383
  143.8 1.0 copy-start.8

commit v5 on v4

--- a/solution.py
+++ b/solution.py
@@ -80,9 +80,12 @@
     return lax.axis_index("y") * lax.axis_size("x") + lax.axis_index("x")
 
 
-def teacher_kernel(n, t_ref, s_ref, w_ref, x_ref, sh_ref, e0, e1, wh_ref, msg_ref, sums):
-    t_half = half_unit(t_ref[...])
-    x_ref[0] = t_half
+def halves_kernel(t_ref, s_ref, x_ref):
+    x_ref[0] = half_unit(t_ref[...])
+    x_ref[1] = half_unit(s_ref[...])
+
+
+def teacher_kernel(n, x_ref, w_ref, sh_ref, e0, e1, wh_ref, msg_ref, sums):
     for j in range(w_ref.shape[0] // CHUNK):
         w_half = half_unit(w_ref[lanes(j), :])
         wh_ref[lanes(j), :] = w_half
@@ -97,9 +100,7 @@
     total = sums[...].astype(msg_ref.dtype)
     for k in range(n):
         msg_ref[k] = total
-    s_half = half_unit(s_ref[...])
-    x_ref[1] = s_half
-    sh_ref[...] = s_half
+    sh_ref[...] = x_ref[1]
 
 
 def student_kernel(sh_ref, wh_ref, tot_ref, p_ref, acc):
@@ -382,18 +383,19 @@
     left = lambda x: lax.ppermute(x, "z", [(i, (i - 1) % n_z) for i in range(n_z)])
     swap = lambda x: lax.ppermute(x, "core", [(0, 1), (1, 0)])
 
-    here, s_half, *expo, w_half, msg = call(
+    here = call(halves_kernel, shape((2, crops, width), BF16), (teacher_emb, student_emb))
+    a1, b1 = right(here), left(here)
+    s_half, *expo, w_half, msg = call(
         functools.partial(teacher_kernel, n_dp),
         (
-            shape((2, crops, width), BF16), shape((crops, width), BF16),
+            shape((crops, width), BF16),
             *[shape((crops // 2, protos), BF16)] * 2, shape((protos, width), BF16),
             shape((n_dp, 32, 128), BF16),
         ),
-        (teacher_emb, student_emb, prototypes),
+        (here, prototypes),
         scratch=[vm((32, 128))],
         flops=block_flops,
     )
-    a1, b1 = right(here), left(here)
     tot_part, p_part = call(
         student_kernel,
         (shape((4, 128)), shape((crops, width))),
@@ -403,14 +405,14 @@
     )
     msg, p_part = tie((msg, p_part))
     parts = to_dp(msg)
-    parts, a1, b1 = tie((parts, a1, b1))
-    a2, b2 = right(a1), left(b1)
     msg = call(
         functools.partial(first_row_kernel, n),
         shape((n, size + 16, width), BF16),
         (parts, *expo, tot_part, p_part),
         scratch=[vm((32, 128))],
     )
+    msg, a1, b1 = tie((msg, a1, b1))
+    a2, b2 = right(a1), left(b1)
     parts = to_proto(msg)
     column_scratch = [vm((crops, 128)), vm((32, 128))]
     msg, totals, p_sum = call(

time: 147 us -> 145 us (0.986)
  blocking collectives: 50.6 us -> 48.2 us
    all_to_all x2, blocking collectives: 31 us -> 28.4 us  [per_device(): to_dp = lambda msg: lax.all_to_all(msg, CROPS, 0, 0)]
    unnamed x38 -> x34, local copies, waits for them, and re-layouts: 7.63 us -> 6.77 us
    pallas_call x12 -> x13, Pallas kernels: 35.3 us -> 35.3 us  [call(): pl.pallas_call(kernel, out_shape=out, in_specs=specs or [VMEM] * len(oper...]
  transfers between devices with their start and end apart: 13 -> 13, of which waited for: 5 -> 5; matrix products, arithmetic and copies ran while one was open for 1% -> 1% of each run, Pallas kernels for 19% -> 22%
where the time goes in v5:
time: 145 us; the launch traced here: 144 us
  blocking collectives  48.2 us (33%)
  starting transfers between devices  38.3 us (26%)
  Pallas kernels  35.3 us (24%)
  waiting for transfers between devices  13.3 us (9%)
  local copies, waits for them, and re-layouts  6.78 us (5%)
    pallas_call x13, Pallas kernels, call(): pl.pallas_call(kernel, out_shape=out, in_specs=specs or [VMEM] * len(oper...  35.3 us
    all_to_all x2, blocking collectives, per_device(): to_dp = lambda msg: lax.all_to_all(msg, CROPS, 0, 0)  28.4 us
    all_to_all x3, starting transfers between devices, per_device(): to_proto = lambda msg: lax.all_to_all(msg, PROTOS, 0, 0)  16.7 us
    ppermute x3, starting transfers between devices, per_device(): lax.ppermute(x, 'z', [(i, (i - 1) % n_z) for i in range(n_z)])  11.7 us
    all_to_all x3, waiting for transfers between devices, per_device(): to_proto = lambda msg: lax.all_to_all(msg, PROTOS, 0, 0)  11.2 us
    all_to_all x1, blocking collectives, per_device(): to_z = lambda msg: lax.all_to_all(msg, 'z', 0, 0)  10.6 us
    all_to_all x1, blocking collectives, per_device(): to_proto = lambda msg: lax.all_to_all(msg, PROTOS, 0, 0)  9.16 us
    unnamed x34, local copies, waits for them, and re-layouts  6.77 us
  transfers between devices with their start and end apart: 13, of which 5 were waited for; matrix products, arithmetic and copies ran while one was open for 1% of the time, Pallas kernels for 22%

profile of v5, /device:TPU:1, one launch (start us, length us, event | category | flops | bytes accessed | tf_op | source)
XLA Modules:
  0.0 143.8 jit_solution(4203274610567353854)
XLA Ops:
  0.6 0.0 copy-start.8
  0.6 0.9 copy-done.8
  1.6 0.9 copy-done.11
  2.5 0.2 shard_map.58.x_ref.refs_0_
  2.8 0.0 copy-start.4
  2.8 6.5 %collective-permute-start.1 = (bf16[2,512,256]{2,1,0:T(8,128)(2,1)S(1)}, bf16[2,512,256]{2,1,0:T(8,128)(2,1)S(1)}, u32[]{:S(2)}, u32[]{:S(2)}) collective-permute-start(bf16[2,512,256]{2,1,0:T(8,128)(2,1)S(1)} %shard_map.58.x_ref.refs_0_), channel_id=1, source_target_pairs={{0,224},{32,0},{64,32},{96,64},{128,96},{160,128},{192,160},{224,1... | collective-permute-start | bytes 1572872 | tf_op jit(solution)/shard_map/ppermute | solution.py:383
  9.3 0.0 collective-permute-start
  9.3 1.6 %copy-done.3 = bf16[4096,256]{1,0:T(8,128)(2,1)S(1)} copy-done((bf16[4096,256]{1,0:T(8,128)(2,1)S(1)}, bf16[4096,256]{1,0:T(8,128)(2,1)}, u32[]{:S(2)}) %copy-start.3) | copy-done | bytes 2097176
  10.8 2.1 %shard_map.59 = (bf16[512,256]{1,0:T(8,128)(2,1)S(1)}, bf16[256,4096]{1,0:T(8,128)(2,1)S(1)}, bf16[256,4096]{1,0:T(8,128)(2,1)S(1)}, bf16[4096,256]{1,0:T(8,128)(2,1)S(1)}, bf16[16,32,128]{2,1,0:T(8,128)(2,1)S(1)}) custom-call(bf16[2,512,256]{2,1,0:T(8,128)(2,1)S(1)} %shard_map.58.x_ref.refs_0_, bf16[4096,256]{1,0:T(8,128)(2,1)S(1)} %copy-done.3), custom_call_target="tpu_custom_call" | custom-call | flops 1073741824 | bytes 2621440 | tf_op jit(solution)/shard_map/pallas_call | solution.py:48
  12.9 2.5 %shard_map.60 = (f32[4,128]{1,0:T(4,128)S(1)}, f32[512,256]{1,0:T(8,128)S(1)}) custom-call(bf16[512,256]{1,0:T(8,128)(2,1)S(1)} %get-tuple-element.56.sh_ref, bf16[4096,256]{1,0:T(8,128)(2,1)S(1)} %get-tuple-element.57.wh_ref), custom_call_target="tpu_custom_call" | custom-call | flops 2147483648 | bytes 2359296 | tf_op jit(solution)/shard_map/pallas_call | solution.py:48
  15.5 14.6 %all_to_all.40.parts_ref = bf16[16,32,128]{2,1,0:T(8,128)(2,1)S(1)} all-to-all(bf16[16,32,128]{2,1,0:T(8,128)(2,1)S(1)} %get-tuple-element.59), channel_id=1, replica_groups=mesh['z'=8,'core'=2,'y'=4,'x'=4] {'z','core'}, dimensions={0} | all-to-all | bytes 262144 | tf_op jit(solution)/shard_map/all_to_all | solution.py:375
  30.0 1.7 %shard_map.61 = bf16[16,48,256]{2,1,0:T(8,128)(2,1)} custom-call(bf16[16,32,128]{2,1,0:T(8,128)(2,1)S(1)} %all_to_all.40.parts_ref, bf16[256,4096]{1,0:T(8,128)(2,1)S(1)} %get-tuple-element.60.e0, bf16[256,4096]{1,0:T(8,128)(2,1)S(1)} %get-tuple-element.61.e1, f32[4,128]{1,0:T(4,128)S(1)} %get-tuple-element.62.tot_ref, f32[512,256]{1,0:T(8,128)S(1)} %get-tuple-element.63.p_ref), custom_call_target="tpu_custom_call" | custom-call | bytes 4851712 | tf_op jit(solution)/shard_map/pallas_call | solution.py:48
  31.7 0.0 collective-permute-done.1.refs_2_
  31.7 0.0 collective-permute-done.refs_1_
  31.7 6.8 %all-to-all-start.1 = ((bf16[16,48,256]{2,1,0:T(8,128)(2,1)}), bf16[16,48,256]{2,1,0:T(8,128)(2,1)S(1)}, u32[]{:S(2)}, u32[]{:S(2)}) async-start(bf16[16,48,256]{2,1,0:T(8,128)(2,1)} %shard_map.61), calls=%async_computation.1 | async-start | bytes 786432 | tf_op jit(solution)/shard_map/all_to_all | solution.py:376
  38.5 0.2 collective-permute-start.2
  38.7 2.6 %collective-permute-start.3 = (bf16[2,512,256]{2,1,0:T(8,128)(2,1)S(1)}, bf16[2,512,256]{2,1,0:T(8,128)(2,1)}, u32[]{:S(2)}, u32[]{:S(2)}) collective-permute-start(bf16[2,512,256]{2,1,0:T(8,128)(2,1)S(1)} %collective-permute-done.1.refs_2_), channel_id=1, source_target_pairs={{0,224},{32,0},{64,32},{96,64},{128,96},{160,128},{192,160},{224,1... | collective-permute-start | bytes 1572872 | tf_op jit(solution)/shard_map/ppermute | solution.py:383
  41.3 7.3 %all-to-all-done.1.parts_ref = bf16[16,48,256]{2,1,0:T(8,128)(2,1)S(1)} async-done(((bf16[16,48,256]{2,1,0:T(8,128)(2,1)}), bf16[16,48,256]{2,1,0:T(8,128)(2,1)S(1)}, u32[]{:S(2)}, u32[]{:S(2)}) %all-to-all-start.1) | async-done | bytes 393248 | tf_op jit(solution)/shard_map/all_to_all | solution.py:376
  48.6 1.6 %copy-done.1 = bf16[256,4096]{1,0:T(8,128)(2,1)S(1)} copy-done((bf16[256,4096]{1,0:T(8,128)(2,1)S(1)}, bf16[256,4096]{1,0:T(8,128)(2,1)}, u32[]{:S(2)}) %copy-start.1) | copy-done | bytes 2097176
  50.2 1.1 shard_map.62
  51.3 13.8 %all_to_all.41.parts_ref.refs_7_.refs_8_ = bf16[16,48,128]{2,1,0:T(8,128)(2,1)S(1)} all-to-all(bf16[16,48,128]{2,1,0:T(8,128)(2,1)S(1)} %get-tuple-element.65), channel_id=1, replica_groups=mesh['z'=8,'core'=2,'y'=4,'x'=4] {'z','core'}, dimensions={0} | all-to-all | bytes 393216 | tf_op jit(solution)/shard_map/all_to_all | solution.py:375
  65.1 0.9 shard_map.63
  66.1 0.0 collective-permute-done.2.refs_3_
  66.1 0.3 collective-permute-start.5
  66.4 2.7 %collective-permute-start.6 = (bf16[2,512,256]{2,1,0:T(8,128)(2,1)}, bf16[2,512,256]{2,1,0:T(8,128)(2,1)}, u32[]{:S(2)}, u32[]{:S(2)}) collective-permute-start(bf16[2,512,256]{2,1,0:T(8,128)(2,1)} %collective-permute-done.3.refs_4_), channel_id=1, source_target_pairs={{0,224},{32,0},{64,32},{96,64},{128,96},{160,128},{192,160},{224,1... | collective-permute-start | bytes 1572872 | tf_op jit(solution)/shard_map/ppermute | solution.py:383
  69.0 9.2 %all_to_all.42.parts_ref = f32[16,4,128]{2,1,0:T(4,128)S(1)} all-to-all(f32[16,4,128]{2,1,0:T(4,128)S(1)} %shard_map.63), channel_id=1, replica_groups=mesh['z'=8,'core'=2,'y'=4,'x'=4] {'y','x'}, dimensions={0} | all-to-all | bytes 65536 | tf_op jit(solution)/shard_map/all_to_all | solution.py:376
  78.2 1.1 shard_map.64
  79.2 1.8 %collective-permute-start.4 = (f32[32,128]{1,0:T(8,128)S(1)}, f32[32,128]{1,0:T(8,128)S(1)}, u32[]{:S(2)}, u32[]{:S(2)}) collective-permute-start(f32[32,128]{1,0:T(8,128)S(1)} %shard_map.64), channel_id=1, source_target_pairs={{0,16},{16,0},{1,17},{17,1},{2,18},{18,2},{3,19},{19,3},{4,20},{20... | collective-permute-start | bytes 49160 | tf_op jit(solution)/shard_map/ppermute | solution.py:384
  81.0 0.8 collective-permute-done.4
  81.8 10.6 %all_to_all.43.parts_ref = f32[8,32,128]{2,1,0:T(8,128)S(1)} all-to-all(f32[8,32,128]{2,1,0:T(8,128)S(1)} %broadcast_in_dim.6), channel_id=1, replica_groups=mesh['z'=8,'core'=2,'y'=4,'x'=4] {'z'}, dimensions={0} | all-to-all | bytes 262144 | tf_op jit(solution)/shard_map/all_to_all | solution.py:441
  92.5 2.4 %shard_map.65 = (f32[16,40,256]{2,1,0:T(8,128)}, f32[32,128]{1,0:T(8,128)S(1)}) custom-call(f32[8,32,128]{2,1,0:T(8,128)S(1)} %all_to_all.43.parts_ref, bf16[256,4096]{1,0:T(8,128)(2,1)S(1)} %get-tuple-element.60.e0, bf16[256,4096]{1,0:T(8,128)(2,1)S(1)} %copy-done.2, bf16[4096,256]{1,0:T(8,128)(2,1)S(1)} %copy-done.6, ...), custom_call_target="tpu_custom_call" | custom-call | flops 1073741824 | bytes 6684672 | tf_op jit(solution)/shard_map/pallas_call | solution.py:48
  94.8 0.6 copy-done.12
  95.4 3.6 %all-to-all-start.5 = ((f32[16,40,256]{2,1,0:T(8,128)}), f32[16,40,256]{2,1,0:T(8,128)S(1)}, u32[]{:S(2)}, u32[]{:S(2)}) async-start(f32[16,40,256]{2,1,0:T(8,128)} %get-tuple-element.75), calls=%async_computation.5 | async-start | bytes 1310720 | tf_op jit(solution)/shard_map/all_to_all | solution.py:376
  99.1 0.0 copy-start.9
  99.1 0.2 collective-permute-start.7
  99.2 6.9 %shard_map.67.g_ref = f32[512,256]{1,0:T(8,128)} custom-call(bf16[4096,256]{1,0:T(8,128)(2,1)} %w_hbm.5, bf16[2,512,256]{2,1,0:T(8,128)(2,1)} %copy-done.4, bf16[2,512,256]{2,1,0:T(8,128)(2,1)} %collective-permute-done.refs_1_, bf16[2,512,256]{2,1,0:T(8,128)(2,1)} %copy-done.13, bf16[2,512,256]{2,1,0:T(8,128)(2,1)} %collective-permute-done.2.refs_3_, ...), custom_call_target="tpu_custom_call" | custom-call | flops 2147483648 | bytes 5963776 | tf_op jit(solution)/shard_map/pallas_call | solution.py:48
  106.1 3.9 %all-to-all-done.5.parts_ref = f32[16,40,256]{2,1,0:T(8,128)S(1)} async-done(((f32[16,40,256]{2,1,0:T(8,128)}), f32[16,40,256]{2,1,0:T(8,128)S(1)}, u32[]{:S(2)}, u32[]{:S(2)}) %all-to-all-start.5) | async-done | bytes 655392 | tf_op jit(solution)/shard_map/all_to_all | solution.py:376
  110.0 1.0 shard_map.66
  111.0 0.7 collective-permute-done.7.refs_7_
  111.7 3.3 %all-to-all-start.6 = ((f32[8,8,128]{2,1,0:T(8,128)}), f32[8,8,128]{2,1,0:T(8,128)S(1)}, u32[]{:S(2)}, u32[]{:S(2)}) async-start(f32[8,8,128]{2,1,0:T(8,128)} %get-tuple-element.86), calls=%async_computation.6 | async-start | bytes 65536 | tf_op jit(solution)/shard_map/all_to_all | solution.py:441
  115.0 7.3 %shard_map.68 = (bf16[8,512,512]{2,1,0:T(8,128)(2,1)}, f32[512,256]{1,0:T(8,128)}) custom-call(bf16[4096,256]{1,0:T(8,128)(2,1)} %w_hbm.5, bf16[2,512,256]{2,1,0:T(8,128)(2,1)} %copy-done.4, bf16[2,512,256]{2,1,0:T(8,128)(2,1)} %collective-permute-done.refs_1_, bf16[2,512,256]{2,1,0:T(8,128)(2,1)} %copy-done.13, ...), custom_call_target="tpu_custom_call" | custom-call | flops 1073741824 | bytes 6488064 | tf_op jit(solution)/shard_map/pallas_call | solution.py:48
  122.4 6.4 %all-to-all-start.7 = ((bf16[16,32,256]{2,1,0:T(8,128)(2,1)}), bf16[16,32,256]{2,1,0:T(8,128)(2,1)S(1)}, u32[]{:S(2)}, u32[]{:S(2)}) async-start(bf16[16,32,256]{2,1,0:T(8,128)(2,1)} %get-tuple-element.97), calls=%async_computation.7 | async-start | bytes 524288 | tf_op jit(solution)/shard_map/all_to_all | solution.py:376
  128.8 7.3 %shard_map.69 = (f32[520,256]{1,0:T(8,128)}, f32[264,256]{1,0:T(8,128)}) custom-call(f32[8,8,128]{2,1,0:T(8,128)} %copy-done.16, bf16[8,512,512]{2,1,0:T(8,128)(2,1)} %get-tuple-element.99.e_hbm, f32[512,256]{1,0:T(8,128)} %shard_map.67.g_ref, f32[512,256]{1,0:T(8,128)} %get-tuple-element.101.late_ref, f32[32,128]{1,0:T(8,128)} %copy-done.12, ...), custom_call_target="tpu_custom_call" | custom-call | flops 1073741824 | bytes 11583488 | tf_op jit(solution)/shard_map/pallas_call | solution.py:48
  136.1 4.2 %collective-permute-start.8 = (f32[264,256]{1,0:T(8,128)}, f32[264,256]{1,0:T(8,128)S(1)}, u32[]{:S(2)}, u32[]{:S(2)}) collective-permute-start(f32[264,256]{1,0:T(8,128)} %get-tuple-element.104), channel_id=1, source_target_pairs={{0,16},{16,0},{1,17},{17,1},{2,18},{18,2},{3,19},{19,3},{4,20},{20... | collective-permute-start | bytes 811016 | tf_op jit(solution)/shard_map/ppermute | solution.py:384
  140.3 0.8 bitcast_convert_fusion
  141.1 0.5 collective-permute-done.8.got_ref
  141.6 1.0 copy-done.10
  142.7 0.9 shard_map.70
  (32 shorter events, 0.1 us)
Async XLA Ops:
  0.6 1.0 copy-start.8
  1.6 0.9 copy-start.11
  2.8 12.7 %copy-start.4 = (bf16[2,512,256]{2,1,0:T(8,128)(2,1)}, bf16[2,512,256]{2,1,0:T(8,128)(2,1)S(1)}, u32[]{:S(2)}) copy-start(bf16[2,512,256]{2,1,0:T(8,128)(2,1)S(1)} %shard_map.58.x_ref.refs_0_) | copy-start | bytes 1572868
  2.8 29.0 %collective-permute-start.1 = (bf16[2,512,256]{2,1,0:T(8,128)(2,1)S(1)}, bf16[2,512,256]{2,1,0:T(8,128)(2,1)S(1)}, u32[]{:S(2)}, u32[]{:S(2)}) collective-permute-start(bf16[2,512,256]{2,1,0:T(8,128)(2,1)S(1)} %shard_map.58.x_ref.refs_0_), channel_id=1, source_target_pairs={{0,224},{32,0},{64,32},{96,64},{128,96},{160,128},{192,160},{224,1... | collective-permute-start | bytes 1572872 | tf_op jit(solution)/shard_map/ppermute | solution.py:383
  9.3 22.5 %collective-permute-start = (bf16[2,512,256]{2,1,0:T(8,128)(2,1)S(1)}, bf16[2,512,256]{2,1,0:T(8,128)(2,1)}, u32[]{:S(2)}, u32[]{:S(2)}) collective-permute-start(bf16[2,512,256]{2,1,0:T(8,128)(2,1)S(1)} %shard_map.58.x_ref.refs_0_), channel_id=1, source_target_pairs={{0,32},{32,64},{64,96},{96,128},{128,160},{160,192},{192,224},{224... | collective-permute-start | bytes 1572872 | tf_op jit(solution)/shard_map/ppermute | solution.py:382
  9.3 1.6 %copy-start.3 = (bf16[4096,256]{1,0:T(8,128)(2,1)S(1)}, bf16[4096,256]{1,0:T(8,128)(2,1)}, u32[]{:S(2)}) copy-start(bf16[4096,256]{1,0:T(8,128)(2,1)} %w_hbm.5) | copy-start | bytes 6291460
  12.9 2.5 %copy-start.5 = (bf16[4096,256]{1,0:T(8,128)(2,1)}, bf16[4096,256]{1,0:T(8,128)(2,1)S(1)}, u32[]{:S(2)}) copy-start(bf16[4096,256]{1,0:T(8,128)(2,1)S(1)} %get-tuple-element.57.wh_ref) | copy-start | bytes 6291460
  12.9 17.1 %copy-start = (bf16[256,4096]{1,0:T(8,128)(2,1)}, bf16[256,4096]{1,0:T(8,128)(2,1)S(1)}, u32[]{:S(2)}) copy-start(bf16[256,4096]{1,0:T(8,128)(2,1)S(1)} %get-tuple-element.61.e1) | copy-start | bytes 6291460
  31.7 19.6 %copy-start.13 = (bf16[2,512,256]{2,1,0:T(8,128)(2,1)}, bf16[2,512,256]{2,1,0:T(8,128)(2,1)S(1)}, u32[]{:S(2)}) copy-start(bf16[2,512,256]{2,1,0:T(8,128)(2,1)S(1)} %collective-permute-done.1.refs_2_) | copy-start | bytes 1572868
  31.7 16.8 %all-to-all-start.1 = ((bf16[16,48,256]{2,1,0:T(8,128)(2,1)}), bf16[16,48,256]{2,1,0:T(8,128)(2,1)S(1)}, u32[]{:S(2)}, u32[]{:S(2)}) async-start(bf16[16,48,256]{2,1,0:T(8,128)(2,1)} %shard_map.61), calls=%async_computation.1 | async-start | bytes 786432 | tf_op jit(solution)/shard_map/all_to_all | solution.py:376
  38.5 27.5 %collective-permute-start.2 = (bf16[2,512,256]{2,1,0:T(8,128)(2,1)}, bf16[2,512,256]{2,1,0:T(8,128)(2,1)}, u32[]{:S(2)}, u32[]{:S(2)}) collective-permute-start(bf16[2,512,256]{2,1,0:T(8,128)(2,1)} %collective-permute-done.refs_1_), channel_id=1, source_target_pairs={{0,32},{32,64},{64,96},{96,128},{128,160},{160,192},{192,224},{224... | collective-permute-start | bytes 1572872 | tf_op jit(solution)/shard_map/ppermute | solution.py:382
  38.7 27.4 %collective-permute-start.3 = (bf16[2,512,256]{2,1,0:T(8,128)(2,1)S(1)}, bf16[2,512,256]{2,1,0:T(8,128)(2,1)}, u32[]{:S(2)}, u32[]{:S(2)}) collective-permute-start(bf16[2,512,256]{2,1,0:T(8,128)(2,1)S(1)} %collective-permute-done.1.refs_2_), channel_id=1, source_target_pairs={{0,224},{32,0},{64,32},{96,64},{128,96},{160,128},{192,160},{224,1... | collective-permute-start | bytes 1572872 | tf_op jit(solution)/shard_map/ppermute | solution.py:383
  48.6 1.6 %copy-start.1 = (bf16[256,4096]{1,0:T(8,128)(2,1)S(1)}, bf16[256,4096]{1,0:T(8,128)(2,1)}, u32[]{:S(2)}) copy-start(bf16[256,4096]{1,0:T(8,128)(2,1)} %copy-done) | copy-start | bytes 6291460
  65.1 0.9 copy-start.7
  66.1 26.4 %collective-permute-start.5 = (bf16[2,512,256]{2,1,0:T(8,128)(2,1)}, bf16[2,512,256]{2,1,0:T(8,128)(2,1)S(1)}, u32[]{:S(2)}, u32[]{:S(2)}) collective-permute-start(bf16[2,512,256]{2,1,0:T(8,128)(2,1)} %collective-permute-done.2.refs_3_), channel_id=1, source_target_pairs={{0,32},{32,64},{64,96},{96,128},{128,160},{160,192},{192,224},{224... | collective-permute-start | bytes 1572872 | tf_op jit(solution)/shard_map/ppermute | solution.py:382
  66.4 26.1 %collective-permute-start.6 = (bf16[2,512,256]{2,1,0:T(8,128)(2,1)}, bf16[2,512,256]{2,1,0:T(8,128)(2,1)}, u32[]{:S(2)}, u32[]{:S(2)}) collective-permute-start(bf16[2,512,256]{2,1,0:T(8,128)(2,1)} %collective-permute-done.3.refs_4_), channel_id=1, source_target_pairs={{0,224},{32,0},{64,32},{96,64},{128,96},{160,128},{192,160},{224,1... | collective-permute-start | bytes 1572872 | tf_op jit(solution)/shard_map/ppermute | solution.py:383
  78.2 14.3 %copy-start.2 = (bf16[256,4096]{1,0:T(8,128)(2,1)S(1)}, bf16[256,4096]{1,0:T(8,128)(2,1)}, u32[]{:S(2)}) copy-start(bf16[256,4096]{1,0:T(8,128)(2,1)} %copy-done) | copy-start | bytes 6291460
  78.2 14.3 %copy-start.6 = (bf16[4096,256]{1,0:T(8,128)(2,1)S(1)}, bf16[4096,256]{1,0:T(8,128)(2,1)}, u32[]{:S(2)}) copy-start(bf16[4096,256]{1,0:T(8,128)(2,1)} %copy-done.5) | copy-start | bytes 6291460
  79.2 2.6 %collective-permute-start.4 = (f32[32,128]{1,0:T(8,128)S(1)}, f32[32,128]{1,0:T(8,128)S(1)}, u32[]{:S(2)}, u32[]{:S(2)}) collective-permute-start(f32[32,128]{1,0:T(8,128)S(1)} %shard_map.64), channel_id=1, source_target_pairs={{0,16},{16,0},{1,17},{17,1},{2,18},{18,2},{3,19},{19,3},{4,20},{20... | collective-permute-start | bytes 49160 | tf_op jit(solution)/shard_map/ppermute | solution.py:384
  92.5 6.6 %copy-start.14 = (bf16[2,512,256]{2,1,0:T(8,128)(2,1)}, bf16[2,512,256]{2,1,0:T(8,128)(2,1)S(1)}, u32[]{:S(2)}) copy-start(bf16[2,512,256]{2,1,0:T(8,128)(2,1)S(1)} %collective-permute-done.5.refs_5_) | copy-start | bytes 1572868
  94.8 0.6 copy-start.12
  95.4 14.6 %all-to-all-start.5 = ((f32[16,40,256]{2,1,0:T(8,128)}), f32[16,40,256]{2,1,0:T(8,128)S(1)}, u32[]{:S(2)}, u32[]{:S(2)}) async-start(f32[16,40,256]{2,1,0:T(8,128)} %get-tuple-element.75), calls=%async_computation.5 | async-start | bytes 1310720 | tf_op jit(solution)/shard_map/all_to_all | solution.py:376
  99.1 11.0 %copy-start.9 = (bf16[512,256]{1,0:T(8,128)(2,1)S(1)}, bf16[512,256]{1,0:T(8,128)(2,1)}, u32[]{:S(2)}) copy-start(bf16[512,256]{1,0:T(8,128)(2,1)} %s_ref.3) | copy-start | bytes 786436
  99.1 12.6 %collective-permute-start.7 = (bf16[2,512,256]{2,1,0:T(8,128)(2,1)S(1)}, bf16[2,512,256]{2,1,0:T(8,128)(2,1)S(1)}, u32[]{:S(2)}, u32[]{:S(2)}) collective-permute-start(bf16[2,512,256]{2,1,0:T(8,128)(2,1)S(1)} %collective-permute-done.5.refs_5_), channel_id=1, source_target_pairs={{0,32},{32,64},{64,96},{96,128},{128,160},{160,192},{192,224},{224... | collective-permute-start | bytes 1572872 | tf_op jit(solution)/shard_map/ppermute | solution.py:382
  111.7 3.3 %copy-start.15 = (bf16[2,512,256]{2,1,0:T(8,128)(2,1)}, bf16[2,512,256]{2,1,0:T(8,128)(2,1)S(1)}, u32[]{:S(2)}) copy-start(bf16[2,512,256]{2,1,0:T(8,128)(2,1)S(1)} %collective-permute-done.7.refs_7_) | copy-start | bytes 1572868
  111.7 10.7 %all-to-all-start.6 = ((f32[8,8,128]{2,1,0:T(8,128)}), f32[8,8,128]{2,1,0:T(8,128)S(1)}, u32[]{:S(2)}, u32[]{:S(2)}) async-start(f32[8,8,128]{2,1,0:T(8,128)} %get-tuple-element.86), calls=%async_computation.6 | async-start | bytes 65536 | tf_op jit(solution)/shard_map/all_to_all | solution.py:441
  122.4 6.4 %copy-start.16 = (f32[8,8,128]{2,1,0:T(8,128)}, f32[8,8,128]{2,1,0:T(8,128)S(1)}, u32[]{:S(2)}) copy-start(f32[8,8,128]{2,1,0:T(8,128)S(1)} %all-to-all-done.6.parts_ref) | copy-start | bytes 98308
  122.4 17.9 %all-to-all-start.7 = ((bf16[16,32,256]{2,1,0:T(8,128)(2,1)}), bf16[16,32,256]{2,1,0:T(8,128)(2,1)S(1)}, u32[]{:S(2)}, u32[]{:S(2)}) async-start(bf16[16,32,256]{2,1,0:T(8,128)(2,1)} %get-tuple-element.97), calls=%async_computation.7 | async-start | bytes 524288 | tf_op jit(solution)/shard_map/all_to_all | solution.py:376
  136.1 5.6 %collective-permute-start.8 = (f32[264,256]{1,0:T(8,128)}, f32[264,256]{1,0:T(8,128)S(1)}, u32[]{:S(2)}, u32[]{:S(2)}) collective-permute-start(f32[264,256]{1,0:T(8,128)} %get-tuple-element.104), channel_id=1, source_target_pairs={{0,16},{16,0},{1,17},{17,1},{2,18},{18,2},{3,19},{19,3},{4,20},{20... | collective-permute-start | bytes 811016 | tf_op jit(solution)/shard_map/ppermute | solution.py:384
  141.6 1.0 copy-start.10

commit v6 on v5

--- a/solution.py
+++ b/solution.py
@@ -249,6 +249,7 @@
         gmsg_ref[k] = grad
 
 
+EARLY = 2
 HOPS = (0, -1, 1, -2, 2, -3, 3, -4)
 
 
@@ -271,19 +272,24 @@
     return jnp.dot(probs, s_half, preferred_element_type=F32)
 
 
+def teacher_term(w_half, t_half):
+    scores = lax.dot_general(w_half, t_half, LAST, preferred_element_type=F32)
+    return jnp.exp2(scores * T_SCALE).astype(BF16)
+
+
 def own_teacher_kernel(w_hbm, *refs):
-    blocks = refs[:8]
-    parts_ref, e_hbm, g_ref, w_buf, t_buf, s_buf, e_buf, w_sem, t_sems, s_sem, e_sems = refs[8:]
+    late = 8 - EARLY
+    blocks = refs[:late]
+    parts_ref, e_hbm, g_ref, w_buf, t_buf, s_buf, e_buf, w_sem, t_sems, s_sem, e_sems = refs[late:]
     w_copies = begin([(chip_rows(w_hbm, w_buf), w_buf)], w_sem)
     t_copies = begin([(x.at[0], t_buf.at[k]) for k, x in enumerate(blocks)], t_sems)
-    s_copies = begin([(blocks[7].at[1], s_buf)], s_sem)
-    e_copies = copies([(e_buf.at[k], e_hbm.at[k]) for k in range(8)], e_sems)
+    s_copies = begin([(blocks[-1].at[1], s_buf)], s_sem)
+    e_copies = copies([(e_buf.at[k], e_hbm.at[k]) for k in range(late)], e_sems)
     w_copies[0].wait()
     w_half = half_unit(w_buf[...])
-    for k in range(8):
+    for k in range(late):
         t_copies[k].wait()
-        scores = lax.dot_general(w_half, t_buf[k], LAST, preferred_element_type=F32)
-        e_buf[k] = jnp.exp2(scores * T_SCALE).astype(BF16)
+        e_buf[k] = teacher_term(w_half, t_buf[k])
         e_copies[k].start()
     s_copies[0].wait()
     g_ref[...] = student_term(w_half, s_buf[...], parts_ref, 7)
@@ -293,11 +299,17 @@
 
 def own_student_kernel(w_hbm, *refs):
     blocks = refs[:7]
-    parts_ref, g_ref, w_buf, s_buf, total, w_sem, s_sems = refs[7:]
+    parts_ref, e_hbm, g_ref, w_buf, s_buf, t_buf, e_buf, total, w_sem, s_sems, t_sems, e_sems = refs[7:]
     w_copies = begin([(chip_rows(w_hbm, w_buf), w_buf)], w_sem)
+    t_copies = begin([(blocks[k].at[0], t_buf.at[k]) for k in range(EARLY)], t_sems)
     s_copies = begin([(x.at[1], s_buf.at[k]) for k, x in enumerate(blocks)], s_sems)
+    e_copies = copies([(e_buf.at[k], e_hbm.at[k]) for k in range(EARLY)], e_sems)
     w_copies[0].wait()
     w_half = half_unit(w_buf[...])
+    for k in range(EARLY):
+        t_copies[k].wait()
+        e_buf[k] = teacher_term(w_half, t_buf[k])
+        e_copies[k].start()
     for k in range(7):
         s_copies[k].wait()
         term = student_term(w_half, s_buf[k], parts_ref, k)
@@ -306,19 +318,24 @@
         else:
             total[...] += term
     g_ref[...] = total[...]
-
-
-def protos_kernel(parts_ref, e_hbm, g_ref, late_ref, c_ref, w_hbm, *refs):
+    for c in e_copies:
+        c.wait()
+
+
+def protos_kernel(parts_ref, early_hbm, e_hbm, g_ref, late_ref, col_parts_ref, w_hbm, *refs):
     blocks = refs[:8]
-    keep_ref, give_ref, own_ref, e_buf, s_buf, total, w_sem, e_sems, s_sems = refs[8:]
+    keep_ref, give_ref, own_ref, c_ref, e_buf, s_buf, total, w_sem, e_sems, s_sems = refs[8:]
     half = own_ref.shape[0]
     start = pl.multiple_of(dp_place() * half, half)
     w_copies = begin([(w_hbm.at[pl.ds(start, half), :], own_ref)], w_sem)
-    e_copies = copies([(e_hbm.at[k], e_buf.at[k]) for k in range(8)], e_sems)
+    e_pairs = [(early_hbm.at[k], e_buf.at[k]) for k in range(EARLY)]
+    e_pairs += [(e_hbm.at[k - EARLY], e_buf.at[k]) for k in range(EARLY, 8)]
+    e_copies = copies(e_pairs, e_sems)
     s_copies = copies([(x.at[1], s_buf.at[k]) for k, x in enumerate(blocks)], s_sems)
     for one, two in zip(e_copies, s_copies):
         one.start()
         two.start()
+    c_ref[...] = 1.0 / jnp.sum(col_parts_ref[...], axis=0)
     first = lax.axis_index("z") * 4
     cols = [column(c_ref[pl.ds(first + i, 1), :]) for i in range(4)]
     loss = jnp.zeros((1, 128), F32)
@@ -441,26 +458,30 @@
     to_z = lambda msg: lax.all_to_all(msg, "z", 0, 0)
     parts = to_z(jnp.broadcast_to(msg, (n_z, 32, 128)))
     parts, a3, b3 = tie((parts, a3, b3))
+    col_parts = parts
     a4 = right(a3)
     gathered = (here, a1, b1, a2, b2, a3, b3, a4)
-    msg, col = call(
+    msg = call(
         functools.partial(last_kernel, n),
-        (shape((n, size + 8, width)), shape((32, 128))),
+        shape((n, size + 8, width)),
         (parts, *expo, w_half, s_half),
-        scratch=[vm((crops, width)), vm((crops, 128))],
+        scratch=[vm((32, 128)), vm((crops, width)), vm((crops, 128))],
         flops=block_flops,
     )
     msg, *gathered = tie((msg,) + gathered[:-1])
     gathered = tuple(gathered) + (a4,)
     blocks = lambda rows, columns: vm((n_z, rows, columns), BF16)
     chip = 2 * owned
-    g_student = call(
+    e_early, g_student = call(
         own_student_kernel,
-        shape((chip, width)),
+        (shape((EARLY, chip, crops), BF16), shape((chip, width))),
         (prototypes,) + gathered[:-1] + (tot_parts,),
         specs=[HBM] * 8 + [VMEM],
+        outs=(HBM, VMEM),
         scratch=[
-            vm((chip, width), BF16), blocks(crops, width), vm((chip, width)), sems(1), sems(n_z),
+            vm((chip, width), BF16), blocks(crops, width), vm((EARLY, crops, width), BF16),
+            vm((EARLY, chip, crops), BF16), vm((chip, width)),
+            sems(1), sems(n_z), sems(EARLY), sems(EARLY),
         ],
         flops=2 * block_flops,
         limit=57,
@@ -475,13 +496,14 @@
     rmsg, g_student, *late = tie((rmsg, g_student) + gathered)
     e_own, g_late = call(
         own_teacher_kernel,
-        (shape((n_z, chip, crops), BF16), shape((chip, width))),
-        (prototypes,) + tuple(late) + (tot_parts,),
-        specs=[HBM] * 9 + [VMEM],
+        (shape((n_z - EARLY, chip, crops), BF16), shape((chip, width))),
+        (prototypes,) + tuple(late)[EARLY:] + (tot_parts,),
+        specs=[HBM] * (9 - EARLY) + [VMEM],
         outs=(HBM, VMEM),
         scratch=[
-            vm((chip, width), BF16), blocks(crops, width), vm((crops, width), BF16),
-            blocks(chip, crops), sems(1), sems(n_z), sems(1), sems(n_z),
+            vm((chip, width), BF16), vm((n_z - EARLY, crops, width), BF16),
+            vm((crops, width), BF16), vm((n_z - EARLY, chip, crops), BF16),
+            sems(1), sems(n_z - EARLY), sems(1), sems(n_z - EARLY),
         ],
         flops=block_flops,
         limit=57,
@@ -492,10 +514,10 @@
     keep, give = call(
         protos_kernel,
         (shape((2 * owned + 8, width)), shape((owned + 8, width))),
-        (parts, e_own, g_student, g_late, col, prototypes) + tuple(late),
-        specs=[VMEM, HBM, VMEM, VMEM, VMEM, HBM] + [HBM] * 8,
+        (parts, e_early, e_own, g_student, g_late, col_parts, prototypes) + tuple(late),
+        specs=[VMEM, HBM, HBM, VMEM, VMEM, VMEM, HBM] + [HBM] * 8,
         scratch=[
-            vm((owned, width), BF16), blocks(chip, crops), blocks(crops, width), vm((chip, width)),
+            vm((owned, width), BF16), vm((32, 128)), blocks(chip, crops), blocks(crops, width), vm((chip, width)),
             sems(1), sems(n_z), sems(n_z),
         ],
         flops=block_flops,

time: 145 us -> 144 us (level)
  transfers between devices with their start and end apart: 13 -> 13, of which waited for: 5 -> 6; matrix products, arithmetic and copies ran while one was open for 1% -> 1% of each run, Pallas kernels for 22% -> 22%
where the time goes in v6:
time: 144 us; the launch traced here: 143 us
  blocking collectives  48.2 us (33%)
  starting transfers between devices  38.9 us (27%)
  Pallas kernels  35.6 us (25%)
  waiting for transfers between devices  12.6 us (9%)
  local copies, waits for them, and re-layouts  6.18 us (4%)
    pallas_call x13, Pallas kernels, call(): pl.pallas_call(kernel, out_shape=out, in_specs=specs or [VMEM] * len(oper...  35.6 us
    all_to_all x2, blocking collectives, per_device(): to_dp = lambda msg: lax.all_to_all(msg, CROPS, 0, 0)  28.4 us
    all_to_all x3, starting transfers between devices, per_device(): to_proto = lambda msg: lax.all_to_all(msg, PROTOS, 0, 0)  16.7 us
    ppermute x3, starting transfers between devices, per_device(): lax.ppermute(x, 'z', [(i, (i - 1) % n_z) for i in range(n_z)])  11.7 us
    all_to_all x1, blocking collectives, per_device(): to_z = lambda msg: lax.all_to_all(msg, 'z', 0, 0)  10.6 us
    all_to_all x3, waiting for transfers between devices, per_device(): to_proto = lambda msg: lax.all_to_all(msg, PROTOS, 0, 0)  10.2 us
    all_to_all x1, blocking collectives, per_device(): to_proto = lambda msg: lax.all_to_all(msg, PROTOS, 0, 0)  9.16 us
    ppermute x2, starting transfers between devices, per_device(): swap = lambda x: lax.ppermute(x, 'core', [(0, 1), (1, 0)])  6.57 us
  transfers between devices with their start and end apart: 13, of which 6 were waited for; matrix products, arithmetic and copies ran while one was open for 1% of the time, Pallas kernels for 22%

profile of v6, /device:TPU:1, one launch (start us, length us, event | category | flops | bytes accessed | tf_op | source)
XLA Modules:
  0.0 143.3 jit_solution(1459104599053357200)
XLA Ops:
  0.6 0.0 copy-start.9
  0.6 0.9 copy-done.9
  1.6 0.9 copy-done.12
  2.5 0.2 shard_map.58.x_ref.refs_0_
  2.8 0.0 copy-start.6
  2.8 6.5 %collective-permute-start.1 = (bf16[2,512,256]{2,1,0:T(8,128)(2,1)S(1)}, bf16[2,512,256]{2,1,0:T(8,128)(2,1)S(1)}, u32[]{:S(2)}, u32[]{:S(2)}) collective-permute-start(bf16[2,512,256]{2,1,0:T(8,128)(2,1)S(1)} %shard_map.58.x_ref.refs_0_), channel_id=1, source_target_pairs={{0,224},{32,0},{64,32},{96,64},{128,96},{160,128},{192,160},{224,1... | collective-permute-start | bytes 1572872 | tf_op jit(solution)/shard_map/ppermute | solution.py:400
  9.3 0.0 collective-permute-start
  9.3 1.6 %copy-done.3 = bf16[4096,256]{1,0:T(8,128)(2,1)S(1)} copy-done((bf16[4096,256]{1,0:T(8,128)(2,1)S(1)}, bf16[4096,256]{1,0:T(8,128)(2,1)}, u32[]{:S(2)}) %copy-start.3) | copy-done | bytes 2097176
  10.8 2.1 %shard_map.59 = (bf16[512,256]{1,0:T(8,128)(2,1)S(1)}, bf16[256,4096]{1,0:T(8,128)(2,1)S(1)}, bf16[256,4096]{1,0:T(8,128)(2,1)S(1)}, bf16[4096,256]{1,0:T(8,128)(2,1)S(1)}, bf16[16,32,128]{2,1,0:T(8,128)(2,1)S(1)}) custom-call(bf16[2,512,256]{2,1,0:T(8,128)(2,1)S(1)} %shard_map.58.x_ref.refs_0_, bf16[4096,256]{1,0:T(8,128)(2,1)S(1)} %copy-done.3), custom_call_target="tpu_custom_call" | custom-call | flops 1073741824 | bytes 2621440 | tf_op jit(solution)/shard_map/pallas_call | solution.py:48
  12.9 2.5 %shard_map.60 = (f32[4,128]{1,0:T(4,128)S(1)}, f32[512,256]{1,0:T(8,128)S(1)}) custom-call(bf16[512,256]{1,0:T(8,128)(2,1)S(1)} %get-tuple-element.56.sh_ref, bf16[4096,256]{1,0:T(8,128)(2,1)S(1)} %get-tuple-element.57.wh_ref), custom_call_target="tpu_custom_call" | custom-call | flops 2147483648 | bytes 2359296 | tf_op jit(solution)/shard_map/pallas_call | solution.py:48
  15.5 14.6 %all_to_all.40.parts_ref = bf16[16,32,128]{2,1,0:T(8,128)(2,1)S(1)} all-to-all(bf16[16,32,128]{2,1,0:T(8,128)(2,1)S(1)} %get-tuple-element.59), channel_id=1, replica_groups=mesh['z'=8,'core'=2,'y'=4,'x'=4] {'z','core'}, dimensions={0} | all-to-all | bytes 262144 | tf_op jit(solution)/shard_map/all_to_all | solution.py:392
  30.0 1.7 %shard_map.61 = bf16[16,48,256]{2,1,0:T(8,128)(2,1)} custom-call(bf16[16,32,128]{2,1,0:T(8,128)(2,1)S(1)} %all_to_all.40.parts_ref, bf16[256,4096]{1,0:T(8,128)(2,1)S(1)} %get-tuple-element.60.e0, bf16[256,4096]{1,0:T(8,128)(2,1)S(1)} %get-tuple-element.61.e1, f32[4,128]{1,0:T(4,128)S(1)} %get-tuple-element.62.tot_ref, f32[512,256]{1,0:T(8,128)S(1)} %get-tuple-element.63.p_ref), custom_call_target="tpu_custom_call" | custom-call | bytes 4851712 | tf_op jit(solution)/shard_map/pallas_call | solution.py:48
  31.7 0.0 collective-permute-done.1.refs_2_.refs_0_
  31.7 0.0 collective-permute-done.refs_1_
  31.7 6.8 %all-to-all-start.1 = ((bf16[16,48,256]{2,1,0:T(8,128)(2,1)}), bf16[16,48,256]{2,1,0:T(8,128)(2,1)S(1)}, u32[]{:S(2)}, u32[]{:S(2)}) async-start(bf16[16,48,256]{2,1,0:T(8,128)(2,1)} %shard_map.61), calls=%async_computation.1 | async-start | bytes 786432 | tf_op jit(solution)/shard_map/all_to_all | solution.py:393
  38.5 0.2 collective-permute-start.2
  38.7 2.6 %collective-permute-start.3 = (bf16[2,512,256]{2,1,0:T(8,128)(2,1)S(1)}, bf16[2,512,256]{2,1,0:T(8,128)(2,1)}, u32[]{:S(2)}, u32[]{:S(2)}) collective-permute-start(bf16[2,512,256]{2,1,0:T(8,128)(2,1)S(1)} %collective-permute-done.1.refs_2_.refs_0_), channel_id=1, source_target_pairs={{0,224},{32,0},{64,32},{96,64},{128,96},{160,128},{192,160},{224,1... | collective-permute-start | bytes 1572872 | tf_op jit(solution)/shard_map/ppermute | solution.py:400
  41.3 7.3 %all-to-all-done.1.parts_ref = bf16[16,48,256]{2,1,0:T(8,128)(2,1)S(1)} async-done(((bf16[16,48,256]{2,1,0:T(8,128)(2,1)}), bf16[16,48,256]{2,1,0:T(8,128)(2,1)S(1)}, u32[]{:S(2)}, u32[]{:S(2)}) %all-to-all-start.1) | async-done | bytes 393248 | tf_op jit(solution)/shard_map/all_to_all | solution.py:393
  48.6 1.6 %copy-done.1 = bf16[256,4096]{1,0:T(8,128)(2,1)S(1)} copy-done((bf16[256,4096]{1,0:T(8,128)(2,1)S(1)}, bf16[256,4096]{1,0:T(8,128)(2,1)}, u32[]{:S(2)}) %copy-start.1) | copy-done | bytes 2097176
  50.2 1.1 shard_map.62
  51.3 13.8 %all_to_all.41.parts_ref.refs_7_.refs_6_ = bf16[16,48,128]{2,1,0:T(8,128)(2,1)S(1)} all-to-all(bf16[16,48,128]{2,1,0:T(8,128)(2,1)S(1)} %get-tuple-element.65), channel_id=1, replica_groups=mesh['z'=8,'core'=2,'y'=4,'x'=4] {'z','core'}, dimensions={0} | all-to-all | bytes 393216 | tf_op jit(solution)/shard_map/all_to_all | solution.py:392
  65.1 0.9 shard_map.63
  66.1 0.0 collective-permute-done.2.refs_3_.refs_1_
  66.1 0.3 collective-permute-start.5
  66.4 2.7 %collective-permute-start.6 = (bf16[2,512,256]{2,1,0:T(8,128)(2,1)}, bf16[2,512,256]{2,1,0:T(8,128)(2,1)}, u32[]{:S(2)}, u32[]{:S(2)}) collective-permute-start(bf16[2,512,256]{2,1,0:T(8,128)(2,1)} %collective-permute-done.3.refs_4_.refs_2_), channel_id=1, source_target_pairs={{0,224},{32,0},{64,32},{96,64},{128,96},{160,128},{192,160},{224,1... | collective-permute-start | bytes 1572872 | tf_op jit(solution)/shard_map/ppermute | solution.py:400
  69.0 9.2 %all_to_all.42.parts_ref = f32[16,4,128]{2,1,0:T(4,128)S(1)} all-to-all(f32[16,4,128]{2,1,0:T(4,128)S(1)} %shard_map.63), channel_id=1, replica_groups=mesh['z'=8,'core'=2,'y'=4,'x'=4] {'y','x'}, dimensions={0} | all-to-all | bytes 65536 | tf_op jit(solution)/shard_map/all_to_all | solution.py:393
  78.2 1.1 shard_map.64
  79.2 1.8 %collective-permute-start.4 = (f32[32,128]{1,0:T(8,128)S(1)}, f32[32,128]{1,0:T(8,128)S(1)}, u32[]{:S(2)}, u32[]{:S(2)}) collective-permute-start(f32[32,128]{1,0:T(8,128)S(1)} %shard_map.64), channel_id=1, source_target_pairs={{0,16},{16,0},{1,17},{17,1},{2,18},{18,2},{3,19},{19,3},{4,20},{20... | collective-permute-start | bytes 49160 | tf_op jit(solution)/shard_map/ppermute | solution.py:401
  81.0 0.8 collective-permute-done.4
  81.8 10.6 %all_to_all.43.parts_ref.col_parts_ref = f32[8,32,128]{2,1,0:T(8,128)S(1)} all-to-all(f32[8,32,128]{2,1,0:T(8,128)S(1)} %broadcast_in_dim.6), channel_id=1, replica_groups=mesh['z'=8,'core'=2,'y'=4,'x'=4] {'z'}, dimensions={0} | all-to-all | bytes 262144 | tf_op jit(solution)/shard_map/all_to_all | solution.py:458
  92.5 2.5 %shard_map.65 = f32[16,40,256]{2,1,0:T(8,128)} custom-call(f32[8,32,128]{2,1,0:T(8,128)S(1)} %all_to_all.43.parts_ref.col_parts_ref, bf16[256,4096]{1,0:T(8,128)(2,1)S(1)} %get-tuple-element.60.e0, bf16[256,4096]{1,0:T(8,128)(2,1)S(1)} %copy-done.2, bf16[4096,256]{1,0:T(8,128)(2,1)S(1)} %copy-done.5, bf16[512,256]{1,0:T(8,128)(2,1)S(1)} %get-tuple-element.56.sh_ref), custom_call_target="tpu_custom_call" | custom-call | flops 1073741824 | bytes 6684672 | tf_op jit(solution)/shard_map/pallas_call | solution.py:48
  94.9 3.6 %all-to-all-start.5 = ((f32[16,40,256]{2,1,0:T(8,128)}), f32[16,40,256]{2,1,0:T(8,128)S(1)}, u32[]{:S(2)}, u32[]{:S(2)}) async-start(f32[16,40,256]{2,1,0:T(8,128)} %shard_map.65), calls=%async_computation.5 | async-start | bytes 1310720 | tf_op jit(solution)/shard_map/all_to_all | solution.py:393
  98.6 0.0 copy-start.10
  98.6 0.2 collective-permute-start.7
  98.7 7.9 %shard_map.67 = (bf16[2,512,512]{2,1,0:T(8,128)(2,1)}, f32[512,256]{1,0:T(8,128)}) custom-call(bf16[4096,256]{1,0:T(8,128)(2,1)} %w_hbm.5, bf16[2,512,256]{2,1,0:T(8,128)(2,1)} %copy-done.6, bf16[2,512,256]{2,1,0:T(8,128)(2,1)} %collective-permute-done.refs_1_, bf16[2,512,256]{2,1,0:T(8,128)(2,1)} %copy-done.13, ...), custom_call_target="tpu_custom_call" | custom-call | flops 2147483648 | bytes 5963776 | tf_op jit(solution)/shard_map/pallas_call | solution.py:48
  106.6 2.9 %all-to-all-done.5.parts_ref = f32[16,40,256]{2,1,0:T(8,128)S(1)} async-done(((f32[16,40,256]{2,1,0:T(8,128)}), f32[16,40,256]{2,1,0:T(8,128)S(1)}, u32[]{:S(2)}, u32[]{:S(2)}) %all-to-all-start.5) | async-done | bytes 655392 | tf_op jit(solution)/shard_map/all_to_all | solution.py:393
  109.5 1.0 shard_map.66
  110.5 0.7 collective-permute-done.7.refs_5_.refs_7_
  111.2 3.3 %all-to-all-start.6 = ((f32[8,8,128]{2,1,0:T(8,128)}), f32[8,8,128]{2,1,0:T(8,128)S(1)}, u32[]{:S(2)}, u32[]{:S(2)}) async-start(f32[8,8,128]{2,1,0:T(8,128)} %get-tuple-element.86), calls=%async_computation.6 | async-start | bytes 65536 | tf_op jit(solution)/shard_map/all_to_all | solution.py:458
  114.5 6.5 %shard_map.68 = (bf16[6,512,512]{2,1,0:T(8,128)(2,1)}, f32[512,256]{1,0:T(8,128)}) custom-call(bf16[4096,256]{1,0:T(8,128)(2,1)} %w_hbm.5, bf16[2,512,256]{2,1,0:T(8,128)(2,1)} %copy-done.13, bf16[2,512,256]{2,1,0:T(8,128)(2,1)} %collective-permute-done.2.refs_3_.refs_1_, bf16[2,512,256]{2,1,0:T(8,128)(2,1)} %collective-permute-done.3.refs_4_.refs_2_, ...), custom_call_target="tpu_custom_call" | custom-call | flops 1073741824 | bytes 5439488 | tf_op jit(solution)/shard_map/pallas_call | solution.py:48
  121.0 0.3 all-to-all-done.6.parts_ref
  121.3 6.3 %all-to-all-start.7 = ((bf16[16,32,256]{2,1,0:T(8,128)(2,1)}), bf16[16,32,256]{2,1,0:T(8,128)(2,1)S(1)}, u32[]{:S(2)}, u32[]{:S(2)}) async-start(bf16[16,32,256]{2,1,0:T(8,128)(2,1)} %get-tuple-element.95), calls=%async_computation.7 | async-start | bytes 524288 | tf_op jit(solution)/shard_map/all_to_all | solution.py:393
  127.7 7.3 %shard_map.69 = (f32[520,256]{1,0:T(8,128)}, f32[264,256]{1,0:T(8,128)}) custom-call(f32[8,8,128]{2,1,0:T(8,128)} %copy-done.16, bf16[2,512,512]{2,1,0:T(8,128)(2,1)} %get-tuple-element.97.early_hbm, bf16[6,512,512]{2,1,0:T(8,128)(2,1)} %get-tuple-element.98.e_hbm, f32[512,256]{1,0:T(8,128)} %get-tuple-element.99.g_ref, ...), custom_call_target="tpu_custom_call" | custom-call | flops 1073741824 | bytes 11698176 | tf_op jit(solution)/shard_map/pallas_call | solution.py:48
  135.0 4.8 %collective-permute-start.8 = (f32[264,256]{1,0:T(8,128)}, f32[264,256]{1,0:T(8,128)S(1)}, u32[]{:S(2)}, u32[]{:S(2)}) collective-permute-start(f32[264,256]{1,0:T(8,128)} %get-tuple-element.104), channel_id=1, source_target_pairs={{0,16},{16,0},{1,17},{17,1},{2,18},{18,2},{3,19},{19,3},{4,20},{20... | collective-permute-start | bytes 811016 | tf_op jit(solution)/shard_map/ppermute | solution.py:401
  139.8 0.8 bitcast_convert_fusion
  140.6 0.5 collective-permute-done.8.got_ref
  141.2 1.0 copy-done.11
  142.2 0.9 shard_map.70
  (32 shorter events, 0.1 us)
Async XLA Ops:
  0.6 1.0 copy-start.9
  1.6 0.9 copy-start.12
  2.8 12.7 %copy-start.6 = (bf16[2,512,256]{2,1,0:T(8,128)(2,1)}, bf16[2,512,256]{2,1,0:T(8,128)(2,1)S(1)}, u32[]{:S(2)}) copy-start(bf16[2,512,256]{2,1,0:T(8,128)(2,1)S(1)} %shard_map.58.x_ref.refs_0_) | copy-start | bytes 1572868
  2.8 29.0 %collective-permute-start.1 = (bf16[2,512,256]{2,1,0:T(8,128)(2,1)S(1)}, bf16[2,512,256]{2,1,0:T(8,128)(2,1)S(1)}, u32[]{:S(2)}, u32[]{:S(2)}) collective-permute-start(bf16[2,512,256]{2,1,0:T(8,128)(2,1)S(1)} %shard_map.58.x_ref.refs_0_), channel_id=1, source_target_pairs={{0,224},{32,0},{64,32},{96,64},{128,96},{160,128},{192,160},{224,1... | collective-permute-start | bytes 1572872 | tf_op jit(solution)/shard_map/ppermute | solution.py:400
  9.3 22.5 %collective-permute-start = (bf16[2,512,256]{2,1,0:T(8,128)(2,1)S(1)}, bf16[2,512,256]{2,1,0:T(8,128)(2,1)}, u32[]{:S(2)}, u32[]{:S(2)}) collective-permute-start(bf16[2,512,256]{2,1,0:T(8,128)(2,1)S(1)} %shard_map.58.x_ref.refs_0_), channel_id=1, source_target_pairs={{0,32},{32,64},{64,96},{96,128},{128,160},{160,192},{192,224},{224... | collective-permute-start | bytes 1572872 | tf_op jit(solution)/shard_map/ppermute | solution.py:399
  9.3 1.6 %copy-start.3 = (bf16[4096,256]{1,0:T(8,128)(2,1)S(1)}, bf16[4096,256]{1,0:T(8,128)(2,1)}, u32[]{:S(2)}) copy-start(bf16[4096,256]{1,0:T(8,128)(2,1)} %w_hbm.5) | copy-start | bytes 6291460
  12.9 2.5 %copy-start.4 = (bf16[4096,256]{1,0:T(8,128)(2,1)}, bf16[4096,256]{1,0:T(8,128)(2,1)S(1)}, u32[]{:S(2)}) copy-start(bf16[4096,256]{1,0:T(8,128)(2,1)S(1)} %get-tuple-element.57.wh_ref) | copy-start | bytes 6291460
  12.9 17.1 %copy-start = (bf16[256,4096]{1,0:T(8,128)(2,1)}, bf16[256,4096]{1,0:T(8,128)(2,1)S(1)}, u32[]{:S(2)}) copy-start(bf16[256,4096]{1,0:T(8,128)(2,1)S(1)} %get-tuple-element.61.e1) | copy-start | bytes 6291460
  31.7 19.6 %copy-start.13 = (bf16[2,512,256]{2,1,0:T(8,128)(2,1)}, bf16[2,512,256]{2,1,0:T(8,128)(2,1)S(1)}, u32[]{:S(2)}) copy-start(bf16[2,512,256]{2,1,0:T(8,128)(2,1)S(1)} %collective-permute-done.1.refs_2_.refs_0_) | copy-start | bytes 1572868
  31.7 16.8 %all-to-all-start.1 = ((bf16[16,48,256]{2,1,0:T(8,128)(2,1)}), bf16[16,48,256]{2,1,0:T(8,128)(2,1)S(1)}, u32[]{:S(2)}, u32[]{:S(2)}) async-start(bf16[16,48,256]{2,1,0:T(8,128)(2,1)} %shard_map.61), calls=%async_computation.1 | async-start | bytes 786432 | tf_op jit(solution)/shard_map/all_to_all | solution.py:393
  38.5 27.5 %collective-permute-start.2 = (bf16[2,512,256]{2,1,0:T(8,128)(2,1)}, bf16[2,512,256]{2,1,0:T(8,128)(2,1)}, u32[]{:S(2)}, u32[]{:S(2)}) collective-permute-start(bf16[2,512,256]{2,1,0:T(8,128)(2,1)} %collective-permute-done.refs_1_), channel_id=1, source_target_pairs={{0,32},{32,64},{64,96},{96,128},{128,160},{160,192},{192,224},{224... | collective-permute-start | bytes 1572872 | tf_op jit(solution)/shard_map/ppermute | solution.py:399
  38.7 27.4 %collective-permute-start.3 = (bf16[2,512,256]{2,1,0:T(8,128)(2,1)S(1)}, bf16[2,512,256]{2,1,0:T(8,128)(2,1)}, u32[]{:S(2)}, u32[]{:S(2)}) collective-permute-start(bf16[2,512,256]{2,1,0:T(8,128)(2,1)S(1)} %collective-permute-done.1.refs_2_.refs_0_), channel_id=1, source_target_pairs={{0,224},{32,0},{64,32},{96,64},{128,96},{160,128},{192,160},{224,1... | collective-permute-start | bytes 1572872 | tf_op jit(solution)/shard_map/ppermute | solution.py:400
  48.6 1.6 %copy-start.1 = (bf16[256,4096]{1,0:T(8,128)(2,1)S(1)}, bf16[256,4096]{1,0:T(8,128)(2,1)}, u32[]{:S(2)}) copy-start(bf16[256,4096]{1,0:T(8,128)(2,1)} %copy-done) | copy-start | bytes 6291460
  65.1 0.9 copy-start.7
  66.1 26.4 %collective-permute-start.5 = (bf16[2,512,256]{2,1,0:T(8,128)(2,1)}, bf16[2,512,256]{2,1,0:T(8,128)(2,1)S(1)}, u32[]{:S(2)}, u32[]{:S(2)}) collective-permute-start(bf16[2,512,256]{2,1,0:T(8,128)(2,1)} %collective-permute-done.2.refs_3_.refs_1_), channel_id=1, source_target_pairs={{0,32},{32,64},{64,96},{96,128},{128,160},{160,192},{192,224},{224... | collective-permute-start | bytes 1572872 | tf_op jit(solution)/shard_map/ppermute | solution.py:399
  66.4 26.1 %collective-permute-start.6 = (bf16[2,512,256]{2,1,0:T(8,128)(2,1)}, bf16[2,512,256]{2,1,0:T(8,128)(2,1)}, u32[]{:S(2)}, u32[]{:S(2)}) collective-permute-start(bf16[2,512,256]{2,1,0:T(8,128)(2,1)} %collective-permute-done.3.refs_4_.refs_2_), channel_id=1, source_target_pairs={{0,224},{32,0},{64,32},{96,64},{128,96},{160,128},{192,160},{224,1... | collective-permute-start | bytes 1572872 | tf_op jit(solution)/shard_map/ppermute | solution.py:400
  78.2 14.3 %copy-start.2 = (bf16[256,4096]{1,0:T(8,128)(2,1)S(1)}, bf16[256,4096]{1,0:T(8,128)(2,1)}, u32[]{:S(2)}) copy-start(bf16[256,4096]{1,0:T(8,128)(2,1)} %copy-done) | copy-start | bytes 6291460
  78.2 14.3 %copy-start.5 = (bf16[4096,256]{1,0:T(8,128)(2,1)S(1)}, bf16[4096,256]{1,0:T(8,128)(2,1)}, u32[]{:S(2)}) copy-start(bf16[4096,256]{1,0:T(8,128)(2,1)} %copy-done.4) | copy-start | bytes 6291460
  79.2 2.6 %collective-permute-start.4 = (f32[32,128]{1,0:T(8,128)S(1)}, f32[32,128]{1,0:T(8,128)S(1)}, u32[]{:S(2)}, u32[]{:S(2)}) collective-permute-start(f32[32,128]{1,0:T(8,128)S(1)} %shard_map.64), channel_id=1, source_target_pairs={{0,16},{16,0},{1,17},{17,1},{2,18},{18,2},{3,19},{19,3},{4,20},{20... | collective-permute-start | bytes 49160 | tf_op jit(solution)/shard_map/ppermute | solution.py:401
  92.5 2.5 %copy-start.8 = (f32[8,32,128]{2,1,0:T(8,128)}, f32[8,32,128]{2,1,0:T(8,128)S(1)}, u32[]{:S(2)}) copy-start(f32[8,32,128]{2,1,0:T(8,128)S(1)} %all_to_all.43.parts_ref.col_parts_ref) | copy-start | bytes 393220
  92.5 6.1 %copy-start.14 = (bf16[2,512,256]{2,1,0:T(8,128)(2,1)}, bf16[2,512,256]{2,1,0:T(8,128)(2,1)S(1)}, u32[]{:S(2)}) copy-start(bf16[2,512,256]{2,1,0:T(8,128)(2,1)S(1)} %collective-permute-done.5.refs_5_.refs_3_) | copy-start | bytes 1572868
  94.9 14.6 %all-to-all-start.5 = ((f32[16,40,256]{2,1,0:T(8,128)}), f32[16,40,256]{2,1,0:T(8,128)S(1)}, u32[]{:S(2)}, u32[]{:S(2)}) async-start(f32[16,40,256]{2,1,0:T(8,128)} %shard_map.65), calls=%async_computation.5 | async-start | bytes 1310720 | tf_op jit(solution)/shard_map/all_to_all | solution.py:393
  98.6 11.0 %copy-start.10 = (bf16[512,256]{1,0:T(8,128)(2,1)S(1)}, bf16[512,256]{1,0:T(8,128)(2,1)}, u32[]{:S(2)}) copy-start(bf16[512,256]{1,0:T(8,128)(2,1)} %s_ref.3) | copy-start | bytes 786436
  98.6 12.6 %collective-permute-start.7 = (bf16[2,512,256]{2,1,0:T(8,128)(2,1)S(1)}, bf16[2,512,256]{2,1,0:T(8,128)(2,1)S(1)}, u32[]{:S(2)}, u32[]{:S(2)}) collective-permute-start(bf16[2,512,256]{2,1,0:T(8,128)(2,1)S(1)} %collective-permute-done.5.refs_5_.refs_3_), channel_id=1, source_target_pairs={{0,32},{32,64},{64,96},{96,128},{128,160},{160,192},{192,224},{224... | collective-permute-start | bytes 1572872 | tf_op jit(solution)/shard_map/ppermute | solution.py:399
  111.2 3.3 %copy-start.15 = (bf16[2,512,256]{2,1,0:T(8,128)(2,1)}, bf16[2,512,256]{2,1,0:T(8,128)(2,1)S(1)}, u32[]{:S(2)}) copy-start(bf16[2,512,256]{2,1,0:T(8,128)(2,1)S(1)} %collective-permute-done.7.refs_5_.refs_7_) | copy-start | bytes 1572868
  111.2 10.1 %all-to-all-start.6 = ((f32[8,8,128]{2,1,0:T(8,128)}), f32[8,8,128]{2,1,0:T(8,128)S(1)}, u32[]{:S(2)}, u32[]{:S(2)}) async-start(f32[8,8,128]{2,1,0:T(8,128)} %get-tuple-element.86), calls=%async_computation.6 | async-start | bytes 65536 | tf_op jit(solution)/shard_map/all_to_all | solution.py:458
  121.3 6.3 %copy-start.16 = (f32[8,8,128]{2,1,0:T(8,128)}, f32[8,8,128]{2,1,0:T(8,128)S(1)}, u32[]{:S(2)}) copy-start(f32[8,8,128]{2,1,0:T(8,128)S(1)} %all-to-all-done.6.parts_ref) | copy-start | bytes 98308
  121.3 18.5 %all-to-all-start.7 = ((bf16[16,32,256]{2,1,0:T(8,128)(2,1)}), bf16[16,32,256]{2,1,0:T(8,128)(2,1)S(1)}, u32[]{:S(2)}, u32[]{:S(2)}) async-start(bf16[16,32,256]{2,1,0:T(8,128)(2,1)} %get-tuple-element.95), calls=%async_computation.7 | async-start | bytes 524288 | tf_op jit(solution)/shard_map/all_to_all | solution.py:393
  135.0 6.2 %collective-permute-start.8 = (f32[264,256]{1,0:T(8,128)}, f32[264,256]{1,0:T(8,128)S(1)}, u32[]{:S(2)}, u32[]{:S(2)}) collective-permute-start(f32[264,256]{1,0:T(8,128)} %get-tuple-element.104), channel_id=1, source_target_pairs={{0,16},{16,0},{1,17},{17,1},{2,18},{18,2},{3,19},{19,3},{4,20},{20... | collective-permute-start | bytes 811016 | tf_op jit(solution)/shard_map/ppermute | solution.py:401
  141.2 1.0 copy-start.11

commit v7 on v6

--- a/solution.py
+++ b/solution.py
@@ -325,9 +325,8 @@
 def protos_kernel(parts_ref, early_hbm, e_hbm, g_ref, late_ref, col_parts_ref, w_hbm, *refs):
     blocks = refs[:8]
     keep_ref, give_ref, own_ref, c_ref, e_buf, s_buf, total, w_sem, e_sems, s_sems = refs[8:]
-    half = own_ref.shape[0]
-    start = pl.multiple_of(dp_place() * half, half)
-    w_copies = begin([(w_hbm.at[pl.ds(start, half), :], own_ref)], w_sem)
+    half = own_ref.shape[0] // 2
+    w_copies = begin([(chip_rows(w_hbm, own_ref), own_ref)], w_sem)
     e_pairs = [(early_hbm.at[k], e_buf.at[k]) for k in range(EARLY)]
     e_pairs += [(e_hbm.at[k - EARLY], e_buf.at[k]) for k in range(EARLY, 8)]
     e_copies = copies(e_pairs, e_sems)
@@ -353,28 +352,20 @@
             total[...] += term
     for i in range(4):
         rows = lanes(i, 128)
-        total[rows, :] = (
-            g_ref[rows, :] + late_ref[rows, :] - total[rows, :] * twice(cols[i])
-        ) * 10.0
+        grad = (g_ref[rows, :] + late_ref[rows, :] - total[rows, :] * twice(cols[i])) * 10.0
+        if i == 0:
+            w_copies[0].wait()
+        values = own_ref[rows, :].astype(F32)
+        inverse = inverse_norms(values)
+        w_unit = values * inverse
+        grad = (grad - w_unit * jnp.sum(w_unit * grad, axis=-1, keepdims=True)) * inverse
+        total[rows, :] = grad
     core = lax.axis_index("core")
     keep_ref[0:half, :] = total[pl.ds(pl.multiple_of(core * half, half), half), :]
     give_ref[0:half, :] = total[pl.ds(pl.multiple_of((1 - core) * half, half), half), :]
     loss = twice(jnp.broadcast_to(loss, (8, 128)))
     give_ref[half : half + 8, :] = loss
     keep_ref[half : half + 8, :] = loss
-    w_copies[0].wait()
-    keep_ref[half + 8 : 2 * half + 8, :] = own_ref[...].astype(F32)
-
-
-def finish_kernel(count, keep_ref, got_ref, out_ref, mean_ref):
-    half = out_ref.shape[0]
-    values = keep_ref[half + 8 : 2 * half + 8, :]
-    inverse = inverse_norms(values)
-    w_unit = values * inverse
-    grad = keep_ref[0:half, :] + got_ref[0:half, :]
-    loss = keep_ref[half : half + 1, :] + got_ref[half : half + 1, :]
-    out_ref[...] = (grad - w_unit * jnp.sum(w_unit * grad, axis=-1, keepdims=True)) * inverse
-    mean_ref[0, 0] = loss[0, 0] * (-1.0 / count)
 
 
 def shape(dims, dtype=F32):
@@ -513,22 +504,19 @@
     pieces = to_proto(gmsg)
     keep, give = call(
         protos_kernel,
-        (shape((2 * owned + 8, width)), shape((owned + 8, width))),
+        (shape((owned + 8, width)),) * 2,
         (parts, e_early, e_own, g_student, g_late, col_parts, prototypes) + tuple(late),
         specs=[VMEM, HBM, HBM, VMEM, VMEM, VMEM, HBM] + [HBM] * 8,
         scratch=[
-            vm((owned, width), BF16), vm((32, 128)), blocks(chip, crops), blocks(crops, width), vm((chip, width)),
+            vm((chip, width), BF16), vm((32, 128)), blocks(chip, crops), blocks(crops, width), vm((chip, width)),
             sems(1), sems(n_z), sems(n_z),
         ],
         flops=block_flops,
         limit=57,
     )
-    grad_protos, loss = call(
-        functools.partial(finish_kernel, float(crops * n_dp)),
-        (shape((owned, width)), shape((1, 1))),
-        (keep, swap(give)),
-        outs=(VMEM, SMEM),
-    )
+    got = swap(give)
+    grad_protos = keep[:owned] + got[:owned]
+    loss = (keep[owned:, :1] + got[owned:, :1]) * (-1.0 / (crops * n_dp))
     grad_student = pieces.astype(F32).reshape(crops, width)
     return grad_student, grad_protos[None], loss[0, 0]
 

time: 144 us -> 145 us (level)
  other arithmetic: 0.85 us -> 3.22 us
    broadcast_in_dim x0 -> x1, other arithmetic: none -> 1.68 us  [per_device(): return (grad_student, grad_protos[None], loss[0, 0])]
    unnamed x34 -> x32, local copies, waits for them, and re-layouts: 6.17 us -> 5.13 us
    pallas_call x13 -> x12, Pallas kernels: 35.6 us -> 34.8 us  [call(): pl.pallas_call(kernel, out_shape=out, in_specs=specs or [VMEM] * len(oper...]
where the time goes in v7:
time: 145 us; the launch traced here: 144 us
  blocking collectives  48.2 us (33%)
  starting transfers between devices  38.9 us (27%)
  Pallas kernels  34.8 us (24%)
  waiting for transfers between devices  12.6 us (9%)
  local copies, waits for them, and re-layouts  5.65 us (4%)
  other arithmetic  3.22 us (2%)
    pallas_call x12, Pallas kernels, call(): pl.pallas_call(kernel, out_shape=out, in_specs=specs or [VMEM] * len(oper...  34.8 us
    all_to_all x2, blocking collectives, per_device(): to_dp = lambda msg: lax.all_to_all(msg, CROPS, 0, 0)  28.4 us
    all_to_all x3, starting transfers between devices, per_device(): to_proto = lambda msg: lax.all_to_all(msg, PROTOS, 0, 0)  16.7 us
    ppermute x3, starting transfers between devices, per_device(): lax.ppermute(x, 'z', [(i, (i - 1) % n_z) for i in range(n_z)])  11.7 us
    all_to_all x1, blocking collectives, per_device(): to_z = lambda msg: lax.all_to_all(msg, 'z', 0, 0)  10.6 us
    all_to_all x3, waiting for transfers between devices, per_device(): to_proto = lambda msg: lax.all_to_all(msg, PROTOS, 0, 0)  10.2 us
    all_to_all x1, blocking collectives, per_device(): to_proto = lambda msg: lax.all_to_all(msg, PROTOS, 0, 0)  9.16 us
    ppermute x2, starting transfers between devices, per_device(): swap = lambda x: lax.ppermute(x, 'core', [(0, 1), (1, 0)])  6.57 us
  transfers between devices with their start and end apart: 13, of which 6 were waited for; matrix products, arithmetic and copies ran while one was open for 1% of the time, Pallas kernels for 22%

profile of v7, /device:TPU:1, one launch (start us, length us, event | category | flops | bytes accessed | tf_op | source)
XLA Modules:
  0.0 144.1 jit_solution(13287122480023544174)
XLA Ops:
  0.6 0.0 copy-start.9
  0.6 0.9 copy-done.9
  1.6 0.9 copy-done.11
  2.5 0.2 shard_map.58.x_ref.refs_0_
  2.8 0.0 copy-start.6
  2.8 6.5 %collective-permute-start.1 = (bf16[2,512,256]{2,1,0:T(8,128)(2,1)S(1)}, bf16[2,512,256]{2,1,0:T(8,128)(2,1)S(1)}, u32[]{:S(2)}, u32[]{:S(2)}) collective-permute-start(bf16[2,512,256]{2,1,0:T(8,128)(2,1)S(1)} %shard_map.58.x_ref.refs_0_), channel_id=1, source_target_pairs={{0,224},{32,0},{64,32},{96,64},{128,96},{160,128},{192,160},{224,1... | collective-permute-start | bytes 1572872 | tf_op jit(solution)/shard_map/ppermute | solution.py:391
  9.3 0.0 collective-permute-start
  9.3 1.6 %copy-done.3 = bf16[4096,256]{1,0:T(8,128)(2,1)S(1)} copy-done((bf16[4096,256]{1,0:T(8,128)(2,1)S(1)}, bf16[4096,256]{1,0:T(8,128)(2,1)}, u32[]{:S(2)}) %copy-start.3) | copy-done | bytes 2097176
  10.8 2.1 %shard_map.59 = (bf16[512,256]{1,0:T(8,128)(2,1)S(1)}, bf16[256,4096]{1,0:T(8,128)(2,1)S(1)}, bf16[256,4096]{1,0:T(8,128)(2,1)S(1)}, bf16[4096,256]{1,0:T(8,128)(2,1)S(1)}, bf16[16,32,128]{2,1,0:T(8,128)(2,1)S(1)}) custom-call(bf16[2,512,256]{2,1,0:T(8,128)(2,1)S(1)} %shard_map.58.x_ref.refs_0_, bf16[4096,256]{1,0:T(8,128)(2,1)S(1)} %copy-done.3), custom_call_target="tpu_custom_call" | custom-call | flops 1073741824 | bytes 2621440 | tf_op jit(solution)/shard_map/pallas_call | solution.py:48
  12.9 2.5 %shard_map.60 = (f32[4,128]{1,0:T(4,128)S(1)}, f32[512,256]{1,0:T(8,128)S(1)}) custom-call(bf16[512,256]{1,0:T(8,128)(2,1)S(1)} %get-tuple-element.54.sh_ref, bf16[4096,256]{1,0:T(8,128)(2,1)S(1)} %get-tuple-element.55.wh_ref), custom_call_target="tpu_custom_call" | custom-call | flops 2147483648 | bytes 2359296 | tf_op jit(solution)/shard_map/pallas_call | solution.py:48
  15.5 14.6 %all_to_all.40.parts_ref = bf16[16,32,128]{2,1,0:T(8,128)(2,1)S(1)} all-to-all(bf16[16,32,128]{2,1,0:T(8,128)(2,1)S(1)} %get-tuple-element.57), channel_id=1, replica_groups=mesh['z'=8,'core'=2,'y'=4,'x'=4] {'z','core'}, dimensions={0} | all-to-all | bytes 262144 | tf_op jit(solution)/shard_map/all_to_all | solution.py:383
  30.0 1.7 %shard_map.61 = bf16[16,48,256]{2,1,0:T(8,128)(2,1)} custom-call(bf16[16,32,128]{2,1,0:T(8,128)(2,1)S(1)} %all_to_all.40.parts_ref, bf16[256,4096]{1,0:T(8,128)(2,1)S(1)} %get-tuple-element.58.e0, bf16[256,4096]{1,0:T(8,128)(2,1)S(1)} %get-tuple-element.59.e1, f32[4,128]{1,0:T(4,128)S(1)} %get-tuple-element.60.tot_ref, f32[512,256]{1,0:T(8,128)S(1)} %get-tuple-element.61.p_ref), custom_call_target="tpu_custom_call" | custom-call | bytes 4851712 | tf_op jit(solution)/shard_map/pallas_call | solution.py:48
  31.7 0.0 collective-permute-done.1.refs_2_.refs_0_
  31.7 0.0 collective-permute-done.refs_1_
  31.7 6.8 %all-to-all-start.1 = ((bf16[16,48,256]{2,1,0:T(8,128)(2,1)}), bf16[16,48,256]{2,1,0:T(8,128)(2,1)S(1)}, u32[]{:S(2)}, u32[]{:S(2)}) async-start(bf16[16,48,256]{2,1,0:T(8,128)(2,1)} %shard_map.61), calls=%async_computation.1 | async-start | bytes 786432 | tf_op jit(solution)/shard_map/all_to_all | solution.py:384
  38.5 0.2 collective-permute-start.2
  38.7 2.6 %collective-permute-start.3 = (bf16[2,512,256]{2,1,0:T(8,128)(2,1)S(1)}, bf16[2,512,256]{2,1,0:T(8,128)(2,1)}, u32[]{:S(2)}, u32[]{:S(2)}) collective-permute-start(bf16[2,512,256]{2,1,0:T(8,128)(2,1)S(1)} %collective-permute-done.1.refs_2_.refs_0_), channel_id=1, source_target_pairs={{0,224},{32,0},{64,32},{96,64},{128,96},{160,128},{192,160},{224,1... | collective-permute-start | bytes 1572872 | tf_op jit(solution)/shard_map/ppermute | solution.py:391
  41.3 7.3 %all-to-all-done.1.parts_ref = bf16[16,48,256]{2,1,0:T(8,128)(2,1)S(1)} async-done(((bf16[16,48,256]{2,1,0:T(8,128)(2,1)}), bf16[16,48,256]{2,1,0:T(8,128)(2,1)S(1)}, u32[]{:S(2)}, u32[]{:S(2)}) %all-to-all-start.1) | async-done | bytes 393248 | tf_op jit(solution)/shard_map/all_to_all | solution.py:384
  48.6 1.6 %copy-done.1 = bf16[256,4096]{1,0:T(8,128)(2,1)S(1)} copy-done((bf16[256,4096]{1,0:T(8,128)(2,1)S(1)}, bf16[256,4096]{1,0:T(8,128)(2,1)}, u32[]{:S(2)}) %copy-start.1) | copy-done | bytes 2097176
  50.2 1.1 shard_map.62
  51.3 13.8 %all_to_all.41.parts_ref.refs_7_.refs_6_ = bf16[16,48,128]{2,1,0:T(8,128)(2,1)S(1)} all-to-all(bf16[16,48,128]{2,1,0:T(8,128)(2,1)S(1)} %get-tuple-element.63), channel_id=1, replica_groups=mesh['z'=8,'core'=2,'y'=4,'x'=4] {'z','core'}, dimensions={0} | all-to-all | bytes 393216 | tf_op jit(solution)/shard_map/all_to_all | solution.py:383
  65.1 0.9 shard_map.63
  66.1 0.3 collective-permute-start.5
  66.3 2.7 %collective-permute-start.6 = (bf16[2,512,256]{2,1,0:T(8,128)(2,1)}, bf16[2,512,256]{2,1,0:T(8,128)(2,1)}, u32[]{:S(2)}, u32[]{:S(2)}) collective-permute-start(bf16[2,512,256]{2,1,0:T(8,128)(2,1)} %collective-permute-done.3.refs_4_.refs_2_), channel_id=1, source_target_pairs={{0,224},{32,0},{64,32},{96,64},{128,96},{160,128},{192,160},{224,1... | collective-permute-start | bytes 1572872 | tf_op jit(solution)/shard_map/ppermute | solution.py:391
  69.0 9.2 %all_to_all.42.parts_ref = f32[16,4,128]{2,1,0:T(4,128)S(1)} all-to-all(f32[16,4,128]{2,1,0:T(4,128)S(1)} %shard_map.63), channel_id=1, replica_groups=mesh['z'=8,'core'=2,'y'=4,'x'=4] {'y','x'}, dimensions={0} | all-to-all | bytes 65536 | tf_op jit(solution)/shard_map/all_to_all | solution.py:384
  78.2 1.1 shard_map.64
  79.2 1.8 %collective-permute-start.4 = (f32[32,128]{1,0:T(8,128)S(1)}, f32[32,128]{1,0:T(8,128)S(1)}, u32[]{:S(2)}, u32[]{:S(2)}) collective-permute-start(f32[32,128]{1,0:T(8,128)S(1)} %shard_map.64), channel_id=1, source_target_pairs={{0,16},{16,0},{1,17},{17,1},{2,18},{18,2},{3,19},{19,3},{4,20},{20... | collective-permute-start | bytes 49160 | tf_op jit(solution)/shard_map/ppermute | solution.py:392
  81.0 0.8 collective-permute-done.4
  81.8 10.6 %all_to_all.43.parts_ref.col_parts_ref = f32[8,32,128]{2,1,0:T(8,128)S(1)} all-to-all(f32[8,32,128]{2,1,0:T(8,128)S(1)} %broadcast_in_dim.6), channel_id=1, replica_groups=mesh['z'=8,'core'=2,'y'=4,'x'=4] {'z'}, dimensions={0} | all-to-all | bytes 262144 | tf_op jit(solution)/shard_map/all_to_all | solution.py:449
  92.5 2.5 %shard_map.65 = f32[16,40,256]{2,1,0:T(8,128)} custom-call(f32[8,32,128]{2,1,0:T(8,128)S(1)} %all_to_all.43.parts_ref.col_parts_ref, bf16[256,4096]{1,0:T(8,128)(2,1)S(1)} %get-tuple-element.58.e0, bf16[256,4096]{1,0:T(8,128)(2,1)S(1)} %copy-done.2, bf16[4096,256]{1,0:T(8,128)(2,1)S(1)} %copy-done.5, bf16[512,256]{1,0:T(8,128)(2,1)S(1)} %get-tuple-element.54.sh_ref), custom_call_target="tpu_custom_call" | custom-call | flops 1073741824 | bytes 6684672 | tf_op jit(solution)/shard_map/pallas_call | solution.py:48
  94.9 3.6 %all-to-all-start.5 = ((f32[16,40,256]{2,1,0:T(8,128)}), f32[16,40,256]{2,1,0:T(8,128)S(1)}, u32[]{:S(2)}, u32[]{:S(2)}) async-start(f32[16,40,256]{2,1,0:T(8,128)} %shard_map.65), calls=%async_computation.5 | async-start | bytes 1310720 | tf_op jit(solution)/shard_map/all_to_all | solution.py:384
  98.6 0.0 copy-start.10
  98.6 0.2 collective-permute-start.7
  98.7 7.9 %shard_map.67 = (bf16[2,512,512]{2,1,0:T(8,128)(2,1)}, f32[512,256]{1,0:T(8,128)}) custom-call(bf16[4096,256]{1,0:T(8,128)(2,1)} %w_hbm.5, bf16[2,512,256]{2,1,0:T(8,128)(2,1)} %copy-done.6, bf16[2,512,256]{2,1,0:T(8,128)(2,1)} %collective-permute-done.refs_1_, bf16[2,512,256]{2,1,0:T(8,128)(2,1)} %copy-done.12, ...), custom_call_target="tpu_custom_call" | custom-call | flops 2147483648 | bytes 5963776 | tf_op jit(solution)/shard_map/pallas_call | solution.py:48
  106.6 2.9 %all-to-all-done.5.parts_ref = f32[16,40,256]{2,1,0:T(8,128)S(1)} async-done(((f32[16,40,256]{2,1,0:T(8,128)}), f32[16,40,256]{2,1,0:T(8,128)S(1)}, u32[]{:S(2)}, u32[]{:S(2)}) %all-to-all-start.5) | async-done | bytes 655392 | tf_op jit(solution)/shard_map/all_to_all | solution.py:384
  109.5 1.0 shard_map.66
  110.5 0.7 collective-permute-done.7.refs_5_.refs_7_
  111.2 3.3 %all-to-all-start.6 = ((f32[8,8,128]{2,1,0:T(8,128)}), f32[8,8,128]{2,1,0:T(8,128)S(1)}, u32[]{:S(2)}, u32[]{:S(2)}) async-start(f32[8,8,128]{2,1,0:T(8,128)} %get-tuple-element.84), calls=%async_computation.6 | async-start | bytes 65536 | tf_op jit(solution)/shard_map/all_to_all | solution.py:449
  114.5 6.5 %shard_map.68 = (bf16[6,512,512]{2,1,0:T(8,128)(2,1)}, f32[512,256]{1,0:T(8,128)}) custom-call(bf16[4096,256]{1,0:T(8,128)(2,1)} %w_hbm.5, bf16[2,512,256]{2,1,0:T(8,128)(2,1)} %copy-done.12, bf16[2,512,256]{2,1,0:T(8,128)(2,1)} %collective-permute-done.2.refs_3_.refs_1_, bf16[2,512,256]{2,1,0:T(8,128)(2,1)} %collective-permute-done.3.refs_4_.refs_2_, ...), custom_call_target="tpu_custom_call" | custom-call | flops 1073741824 | bytes 5439488 | tf_op jit(solution)/shard_map/pallas_call | solution.py:48
  121.0 0.3 all-to-all-done.6.parts_ref
  121.3 6.3 %all-to-all-start.7 = ((bf16[16,32,256]{2,1,0:T(8,128)(2,1)}), bf16[16,32,256]{2,1,0:T(8,128)(2,1)S(1)}, u32[]{:S(2)}, u32[]{:S(2)}) async-start(bf16[16,32,256]{2,1,0:T(8,128)(2,1)} %get-tuple-element.93), calls=%async_computation.7 | async-start | bytes 524288 | tf_op jit(solution)/shard_map/all_to_all | solution.py:384
  127.7 7.4 %shard_map.69 = (f32[264,256]{1,0:T(8,128)}, f32[264,256]{1,0:T(8,128)}) custom-call(f32[8,8,128]{2,1,0:T(8,128)} %copy-done.15, bf16[2,512,512]{2,1,0:T(8,128)(2,1)} %get-tuple-element.95.early_hbm, bf16[6,512,512]{2,1,0:T(8,128)(2,1)} %get-tuple-element.96.e_hbm, f32[512,256]{1,0:T(8,128)} %get-tuple-element.97.g_ref, ...), custom_call_target="tpu_custom_call" | custom-call | flops 1073741824 | bytes 11698176 | tf_op jit(solution)/shard_map/pallas_call | solution.py:48
  135.1 4.8 %collective-permute-start.8 = (f32[264,256]{1,0:T(8,128)}, f32[264,256]{1,0:T(8,128)S(1)}, u32[]{:S(2)}, u32[]{:S(2)}) collective-permute-start(f32[264,256]{1,0:T(8,128)} %get-tuple-element.102), channel_id=1, source_target_pairs={{0,16},{16,0},{1,17},{17,1},{2,18},{18,2},{3,19},{19,3},{4,20},{20... | collective-permute-start | bytes 811016 | tf_op jit(solution)/shard_map/ppermute | solution.py:392
  139.9 0.8 bitcast_convert_fusion
  140.7 0.5 collective-permute-done.8
  141.3 0.7 fusion.1
  141.9 0.5 slice.19
  142.5 1.7 %fusion = f32[1,256,256]{2,1,0:T(8,128)} fusion(f32[264,256]{1,0:T(8,128)S(1)} %collective-permute-done.8, f32[264,256]{1,0:T(8,128)} %get-tuple-element.101), kind=kLoop, calls=%fused_computation.1 | loop fusion | flops 65536 | bytes 786432 | tf_op jit(solution)/shard_map/broadcast_in_dim | solution.py:521
  (32 shorter events, 0.1 us)
Async XLA Ops:
  0.6 1.0 copy-start.9
  1.6 0.9 copy-start.11
  2.8 12.7 %copy-start.6 = (bf16[2,512,256]{2,1,0:T(8,128)(2,1)}, bf16[2,512,256]{2,1,0:T(8,128)(2,1)S(1)}, u32[]{:S(2)}) copy-start(bf16[2,512,256]{2,1,0:T(8,128)(2,1)S(1)} %shard_map.58.x_ref.refs_0_) | copy-start | bytes 1572868
  2.8 28.9 %collective-permute-start.1 = (bf16[2,512,256]{2,1,0:T(8,128)(2,1)S(1)}, bf16[2,512,256]{2,1,0:T(8,128)(2,1)S(1)}, u32[]{:S(2)}, u32[]{:S(2)}) collective-permute-start(bf16[2,512,256]{2,1,0:T(8,128)(2,1)S(1)} %shard_map.58.x_ref.refs_0_), channel_id=1, source_target_pairs={{0,224},{32,0},{64,32},{96,64},{128,96},{160,128},{192,160},{224,1... | collective-permute-start | bytes 1572872 | tf_op jit(solution)/shard_map/ppermute | solution.py:391
  9.3 22.5 %collective-permute-start = (bf16[2,512,256]{2,1,0:T(8,128)(2,1)S(1)}, bf16[2,512,256]{2,1,0:T(8,128)(2,1)}, u32[]{:S(2)}, u32[]{:S(2)}) collective-permute-start(bf16[2,512,256]{2,1,0:T(8,128)(2,1)S(1)} %shard_map.58.x_ref.refs_0_), channel_id=1, source_target_pairs={{0,32},{32,64},{64,96},{96,128},{128,160},{160,192},{192,224},{224... | collective-permute-start | bytes 1572872 | tf_op jit(solution)/shard_map/ppermute | solution.py:390
  9.3 1.6 %copy-start.3 = (bf16[4096,256]{1,0:T(8,128)(2,1)S(1)}, bf16[4096,256]{1,0:T(8,128)(2,1)}, u32[]{:S(2)}) copy-start(bf16[4096,256]{1,0:T(8,128)(2,1)} %w_hbm.5) | copy-start | bytes 6291460
  12.9 2.5 %copy-start.4 = (bf16[4096,256]{1,0:T(8,128)(2,1)}, bf16[4096,256]{1,0:T(8,128)(2,1)S(1)}, u32[]{:S(2)}) copy-start(bf16[4096,256]{1,0:T(8,128)(2,1)S(1)} %get-tuple-element.55.wh_ref) | copy-start | bytes 6291460
  12.9 17.1 %copy-start = (bf16[256,4096]{1,0:T(8,128)(2,1)}, bf16[256,4096]{1,0:T(8,128)(2,1)S(1)}, u32[]{:S(2)}) copy-start(bf16[256,4096]{1,0:T(8,128)(2,1)S(1)} %get-tuple-element.59.e1) | copy-start | bytes 6291460
  31.7 19.6 %copy-start.12 = (bf16[2,512,256]{2,1,0:T(8,128)(2,1)}, bf16[2,512,256]{2,1,0:T(8,128)(2,1)S(1)}, u32[]{:S(2)}) copy-start(bf16[2,512,256]{2,1,0:T(8,128)(2,1)S(1)} %collective-permute-done.1.refs_2_.refs_0_) | copy-start | bytes 1572868
  31.7 16.8 %all-to-all-start.1 = ((bf16[16,48,256]{2,1,0:T(8,128)(2,1)}), bf16[16,48,256]{2,1,0:T(8,128)(2,1)S(1)}, u32[]{:S(2)}, u32[]{:S(2)}) async-start(bf16[16,48,256]{2,1,0:T(8,128)(2,1)} %shard_map.61), calls=%async_computation.1 | async-start | bytes 786432 | tf_op jit(solution)/shard_map/all_to_all | solution.py:384
  38.5 27.5 %collective-permute-start.2 = (bf16[2,512,256]{2,1,0:T(8,128)(2,1)}, bf16[2,512,256]{2,1,0:T(8,128)(2,1)}, u32[]{:S(2)}, u32[]{:S(2)}) collective-permute-start(bf16[2,512,256]{2,1,0:T(8,128)(2,1)} %collective-permute-done.refs_1_), channel_id=1, source_target_pairs={{0,32},{32,64},{64,96},{96,128},{128,160},{160,192},{192,224},{224... | collective-permute-start | bytes 1572872 | tf_op jit(solution)/shard_map/ppermute | solution.py:390
  38.7 27.4 %collective-permute-start.3 = (bf16[2,512,256]{2,1,0:T(8,128)(2,1)S(1)}, bf16[2,512,256]{2,1,0:T(8,128)(2,1)}, u32[]{:S(2)}, u32[]{:S(2)}) collective-permute-start(bf16[2,512,256]{2,1,0:T(8,128)(2,1)S(1)} %collective-permute-done.1.refs_2_.refs_0_), channel_id=1, source_target_pairs={{0,224},{32,0},{64,32},{96,64},{128,96},{160,128},{192,160},{224,1... | collective-permute-start | bytes 1572872 | tf_op jit(solution)/shard_map/ppermute | solution.py:391
  48.6 1.6 %copy-start.1 = (bf16[256,4096]{1,0:T(8,128)(2,1)S(1)}, bf16[256,4096]{1,0:T(8,128)(2,1)}, u32[]{:S(2)}) copy-start(bf16[256,4096]{1,0:T(8,128)(2,1)} %copy-done) | copy-start | bytes 6291460
  65.1 0.9 copy-start.7
  66.1 26.4 %collective-permute-start.5 = (bf16[2,512,256]{2,1,0:T(8,128)(2,1)}, bf16[2,512,256]{2,1,0:T(8,128)(2,1)S(1)}, u32[]{:S(2)}, u32[]{:S(2)}) collective-permute-start(bf16[2,512,256]{2,1,0:T(8,128)(2,1)} %collective-permute-done.2.refs_3_.refs_1_), channel_id=1, source_target_pairs={{0,32},{32,64},{64,96},{96,128},{128,160},{160,192},{192,224},{224... | collective-permute-start | bytes 1572872 | tf_op jit(solution)/shard_map/ppermute | solution.py:390
  66.3 26.1 %collective-permute-start.6 = (bf16[2,512,256]{2,1,0:T(8,128)(2,1)}, bf16[2,512,256]{2,1,0:T(8,128)(2,1)}, u32[]{:S(2)}, u32[]{:S(2)}) collective-permute-start(bf16[2,512,256]{2,1,0:T(8,128)(2,1)} %collective-permute-done.3.refs_4_.refs_2_), channel_id=1, source_target_pairs={{0,224},{32,0},{64,32},{96,64},{128,96},{160,128},{192,160},{224,1... | collective-permute-start | bytes 1572872 | tf_op jit(solution)/shard_map/ppermute | solution.py:391
  78.2 14.3 %copy-start.2 = (bf16[256,4096]{1,0:T(8,128)(2,1)S(1)}, bf16[256,4096]{1,0:T(8,128)(2,1)}, u32[]{:S(2)}) copy-start(bf16[256,4096]{1,0:T(8,128)(2,1)} %copy-done) | copy-start | bytes 6291460
  78.2 14.3 %copy-start.5 = (bf16[4096,256]{1,0:T(8,128)(2,1)S(1)}, bf16[4096,256]{1,0:T(8,128)(2,1)}, u32[]{:S(2)}) copy-start(bf16[4096,256]{1,0:T(8,128)(2,1)} %copy-done.4) | copy-start | bytes 6291460
  79.2 2.6 %collective-permute-start.4 = (f32[32,128]{1,0:T(8,128)S(1)}, f32[32,128]{1,0:T(8,128)S(1)}, u32[]{:S(2)}, u32[]{:S(2)}) collective-permute-start(f32[32,128]{1,0:T(8,128)S(1)} %shard_map.64), channel_id=1, source_target_pairs={{0,16},{16,0},{1,17},{17,1},{2,18},{18,2},{3,19},{19,3},{4,20},{20... | collective-permute-start | bytes 49160 | tf_op jit(solution)/shard_map/ppermute | solution.py:392
  92.5 2.5 %copy-start.8 = (f32[8,32,128]{2,1,0:T(8,128)}, f32[8,32,128]{2,1,0:T(8,128)S(1)}, u32[]{:S(2)}) copy-start(f32[8,32,128]{2,1,0:T(8,128)S(1)} %all_to_all.43.parts_ref.col_parts_ref) | copy-start | bytes 393220
  92.5 6.1 %copy-start.13 = (bf16[2,512,256]{2,1,0:T(8,128)(2,1)}, bf16[2,512,256]{2,1,0:T(8,128)(2,1)S(1)}, u32[]{:S(2)}) copy-start(bf16[2,512,256]{2,1,0:T(8,128)(2,1)S(1)} %collective-permute-done.5.refs_5_.refs_3_) | copy-start | bytes 1572868
  94.9 14.6 %all-to-all-start.5 = ((f32[16,40,256]{2,1,0:T(8,128)}), f32[16,40,256]{2,1,0:T(8,128)S(1)}, u32[]{:S(2)}, u32[]{:S(2)}) async-start(f32[16,40,256]{2,1,0:T(8,128)} %shard_map.65), calls=%async_computation.5 | async-start | bytes 1310720 | tf_op jit(solution)/shard_map/all_to_all | solution.py:384
  98.6 11.0 %copy-start.10 = (bf16[512,256]{1,0:T(8,128)(2,1)S(1)}, bf16[512,256]{1,0:T(8,128)(2,1)}, u32[]{:S(2)}) copy-start(bf16[512,256]{1,0:T(8,128)(2,1)} %s_ref.3) | copy-start | bytes 786436
  98.6 12.6 %collective-permute-start.7 = (bf16[2,512,256]{2,1,0:T(8,128)(2,1)S(1)}, bf16[2,512,256]{2,1,0:T(8,128)(2,1)S(1)}, u32[]{:S(2)}, u32[]{:S(2)}) collective-permute-start(bf16[2,512,256]{2,1,0:T(8,128)(2,1)S(1)} %collective-permute-done.5.refs_5_.refs_3_), channel_id=1, source_target_pairs={{0,32},{32,64},{64,96},{96,128},{128,160},{160,192},{192,224},{224... | collective-permute-start | bytes 1572872 | tf_op jit(solution)/shard_map/ppermute | solution.py:390
  111.2 3.3 %copy-start.14 = (bf16[2,512,256]{2,1,0:T(8,128)(2,1)}, bf16[2,512,256]{2,1,0:T(8,128)(2,1)S(1)}, u32[]{:S(2)}) copy-start(bf16[2,512,256]{2,1,0:T(8,128)(2,1)S(1)} %collective-permute-done.7.refs_5_.refs_7_) | copy-start | bytes 1572868
  111.2 10.1 %all-to-all-start.6 = ((f32[8,8,128]{2,1,0:T(8,128)}), f32[8,8,128]{2,1,0:T(8,128)S(1)}, u32[]{:S(2)}, u32[]{:S(2)}) async-start(f32[8,8,128]{2,1,0:T(8,128)} %get-tuple-element.84), calls=%async_computation.6 | async-start | bytes 65536 | tf_op jit(solution)/shard_map/all_to_all | solution.py:449
  121.3 6.3 %copy-start.15 = (f32[8,8,128]{2,1,0:T(8,128)}, f32[8,8,128]{2,1,0:T(8,128)S(1)}, u32[]{:S(2)}) copy-start(f32[8,8,128]{2,1,0:T(8,128)S(1)} %all-to-all-done.6.parts_ref) | copy-start | bytes 98308
  121.3 18.6 %all-to-all-start.7 = ((bf16[16,32,256]{2,1,0:T(8,128)(2,1)}), bf16[16,32,256]{2,1,0:T(8,128)(2,1)S(1)}, u32[]{:S(2)}, u32[]{:S(2)}) async-start(bf16[16,32,256]{2,1,0:T(8,128)(2,1)} %get-tuple-element.93), calls=%async_computation.7 | async-start | bytes 524288 | tf_op jit(solution)/shard_map/all_to_all | solution.py:384
  135.1 6.2 %collective-permute-start.8 = (f32[264,256]{1,0:T(8,128)}, f32[264,256]{1,0:T(8,128)S(1)}, u32[]{:S(2)}, u32[]{:S(2)}) collective-permute-start(f32[264,256]{1,0:T(8,128)} %get-tuple-element.102), channel_id=1, source_target_pairs={{0,16},{16,0},{1,17},{17,1},{2,18},{18,2},{3,19},{19,3},{4,20},{20... | collective-permute-start | bytes 811016 | tf_op jit(solution)/shard_map/ppermute | solution.py:392
